TPU v7x, 768 devices: a whole 4x8x12 slice. The times are simulated.
768 devices in a mesh: gx: 16 (over x, y_lo), gy: 48 (over z, y_hi, core).
Axes of the slice: x: 4, y: 8 (y_hi: 2, y_lo: 4; y = y_hi * 4 + y_lo), z: 12, core: 2. Of those that a mesh axis runs over, the one named last changes fastest.
Arguments:
- feats: bfloat16 [16, 48, 256, 128], P('gx', 'gy'), may hold values from -6 to 6
- positions: bfloat16 [16, 48, 3, 256], P('gx', 'gy'), may hold values from 0 to 1
- atom_count: int32 [16, 48], replicated, may hold values from 64 to 256, as said below
- edge_center: int32 [16, 48, 256], P('gx', 'gy'), may hold values from 0 to 255, as said below
- edge_neighbor: int32 [16, 48, 256], P('gx', 'gy'), may hold values from 0 to 2303, as said below
- edge_valid: int32 [16, 48, 256], P('gx', 'gy'), may hold values 0 or 1
- w_center: bfloat16 [128, 128], replicated, may hold values from -0.5 to 0.5
- w_neighbor: bfloat16 [128, 128], replicated, may hold values from -0.5 to 0.5
- w_radial: float32 [8, 128], replicated, may hold values from -2 to 2
- w_second: bfloat16 [128, 128], replicated, may hold values from -0.5 to 0.5
- w_env: bfloat16 [128, 384], replicated, may hold values from -0.5 to 0.5
- readout: float32 [3, 128], replicated, may hold values from -0.5 to 0.5
Outputs:
- atom_energy: float32 [16, 48, 256], P('gx', 'gy')
- forces: float32 [16, 48, 3, 256], P('gx', 'gy')
Inputs may be any that keep to these rules, and one draw needn't show every extreme that they name: `atom_count`: in each row of cells that share a gx index, exactly 12 cells hold 256 atoms and every other cell holds at most 128. `edge_center`: a real atom of the edge's own cell, below its atom_count. `edge_neighbor`: s * 256 + k with k below the atom_count of the cell that s names.
All inputs are finite; a program needn't handle non-finite values. No bound on the sum of `edge_valid` on one device may be relied on, other than what follows from the above.
Results may differ from a plain program's by a relative error of at most 0.022.
Values may be sent and summed in bfloat16 or wider, within the bound.
No kernel may reach another device: no remote copies, remote signals or barrier semaphores. Data moves between devices by JAX's collectives and lax.ppermute only.
A program may use at most 32 MiB of HBM per device.

v0:
```python
import math

import jax
import jax.numpy as jnp
from jax import lax
from jax.sharding import PartitionSpec as P

NBASIS = 8
EBLK = 64


ROOT_THREE = math.sqrt(3.0)
ROOT_FIFTEEN = math.sqrt(15.0)
ROOT_FIVE = math.sqrt(5.0)
LEVELS = (0, 1, 1, 1, 2, 2, 2, 2, 2)


def passed_along(block, axis, distance):
    devices = range(lax.axis_size(axis))
    route = [((i - distance) % len(devices), i) for i in devices]
    return lax.ppermute(block, axis, route)


def extended(block, sides, width):
    for axis, dim in sides:
        count = lax.axis_size(axis)
        forward = [(i, i + 1) for i in range(count - 1)]
        forward.append((count - 1, 0))
        backward = [(target, source) for source, target in forward]
        low = lax.ppermute(
            lax.slice_in_dim(block, block.shape[dim] - width, None, axis=dim), axis, forward
        )
        high = lax.ppermute(lax.slice_in_dim(block, 0, width, axis=dim), axis, backward)
        block = jnp.concatenate([low, block, high], axis=dim)
    return block


def geometry(displace):
    dist_sq = jnp.sum(displace * displace, axis=0) + 0.25
    distance = jnp.sqrt(dist_sq)
    direction = displace / distance[None, :]
    comp_x, comp_y, comp_z = (direction[0], direction[1], direction[2])
    gammas = 0.25 * 1.5 ** jnp.arange(NBASIS, dtype=jnp.float32)
    radial_basis = jnp.exp(-gammas[:, None] * dist_sq[None, :])
    harmonics = jnp.stack(
        [
            jnp.ones_like(comp_x),
            ROOT_THREE * comp_x,
            ROOT_THREE * comp_y,
            ROOT_THREE * comp_z,
            ROOT_FIFTEEN * comp_x * comp_y,
            ROOT_FIFTEEN * comp_y * comp_z,
            0.5 * ROOT_FIVE * (3.0 * comp_z * comp_z - 1.0),
            ROOT_FIFTEEN * comp_x * comp_z,
            0.5 * ROOT_FIFTEEN * (comp_x * comp_x - comp_y * comp_y),
        ]
    )
    return (radial_basis, harmonics)


def local_latent(preact, w_second):
    hidden = jax.nn.silu(preact.astype(jnp.float32)).astype(jnp.bfloat16)
    return jnp.tanh(jnp.dot(hidden, w_second, preferred_element_type=jnp.float32)).astype(
        jnp.bfloat16
    )


def edge_layer(
    near_side,
    far_ghost,
    pos_ghost,
    center,
    neighbor,
    valid_int,
    w_radial,
    w_second,
    w_env,
    readout,
    latent_fn,
):
    atom_rows = near_side.shape[0]
    channels = near_side.shape[1]
    slot_id = neighbor // atom_rows
    offset = jnp.stack([slot_id // 3 - 1, slot_id % 3 - 1, jnp.zeros_like(slot_id)]).astype(
        jnp.float32
    )
    displace = pos_ghost[:, neighbor] + offset - pos_ghost[:, 4 * atom_rows + center]
    radial_basis, harmonics = geometry(displace)
    radial = lax.dot_general(
        radial_basis, w_radial, (((0,), (0,)), ((), ())), precision=lax.Precision.HIGHEST
    )
    preact = (
        near_side[center].astype(jnp.float32) + far_ghost[neighbor].astype(jnp.float32) + radial
    ).astype(jnp.bfloat16)
    latent = latent_fn(preact)
    valid_mask = valid_int.astype(jnp.float32)
    env = jnp.dot(latent, w_env, preferred_element_type=jnp.float32) * valid_mask[:, None]
    env_parts = [env[:, level * channels : (level + 1) * channels] for level in range(3)]
    energy = jnp.zeros((atom_rows,), jnp.float32)
    edge_grads = []
    for comp, level in enumerate(LEVELS):
        gathered = jax.ops.segment_sum(
            env_parts[level] * harmonics[comp][:, None], center, num_segments=atom_rows
        )
        if comp == 0:
            energy = jnp.sum(gathered * readout[0][None, :], axis=1)
            agg_grad = jnp.broadcast_to(readout[0][None, :], gathered.shape)
        else:
            energy = energy + jnp.sum(readout[level][None, :] * gathered * gathered, axis=1)
            agg_grad = 2.0 * readout[level][None, :] * gathered
        edge_grads.append(agg_grad[center])
    env_grad = []
    for level in range(3):
        summed = jnp.zeros_like(env_parts[0])
        for comp, owner in enumerate(LEVELS):
            if owner == level:
                summed = summed + edge_grads[comp] * harmonics[comp][:, None]
        env_grad.append(summed * valid_mask[:, None])
    env_grad = jnp.concatenate(env_grad, axis=1).astype(jnp.bfloat16)
    harm_grad = jnp.stack(
        [jnp.sum(edge_grads[comp] * env_parts[LEVELS[comp]], axis=1) for comp in range(9)]
    )
    latent_grad = lax.dot_general(
        env_grad, w_env, (((1,), (1,)), ((), ())), preferred_element_type=jnp.float32
    )
    latent32 = latent.astype(jnp.float32)
    act_grad = (latent_grad * (1.0 - latent32 * latent32)).astype(jnp.bfloat16)
    hidden_grad = lax.dot_general(
        act_grad, w_second, (((1,), (1,)), ((), ())), preferred_element_type=jnp.float32
    )
    preact32 = preact.astype(jnp.float32)
    sigmoid_pre = jax.nn.sigmoid(preact32)
    preact_grad = hidden_grad * sigmoid_pre * (1.0 + preact32 * (1.0 - sigmoid_pre))
    basis_grad = lax.dot_general(
        w_radial, preact_grad, (((1,), (1,)), ((), ())), precision=lax.Precision.HIGHEST
    )
    _, pullback = jax.vjp(geometry, displace)
    (displace_grad,) = pullback((basis_grad, harm_grad))
    ghost_force = jnp.zeros((3, 9 * atom_rows), jnp.float32)
    ghost_force = ghost_force.at[:, neighbor].add(-displace_grad)
    ghost_force = ghost_force.at[:, 4 * atom_rows + center].add(displace_grad)
    return (energy, ghost_force)


def return_rows(field, which_dim):
    summed = jnp.take(field, 1, axis=which_dim)
    for step_by, which_side in ((-1, 0), (1, 2)):
        summed = summed + passed_along(jnp.take(field, which_side, axis=which_dim), "gy", step_by)
    return summed


def return_slabs(field, which_dim):
    summed = jnp.take(field, 1, axis=which_dim)
    for step_by, which_side in ((-1, 0), (1, 2)):
        summed = summed + passed_along(jnp.take(field, which_side, axis=which_dim), "gx", step_by)
    return summed


def body(
    feats,
    positions,
    atom_count,
    edge_center,
    edge_neighbor,
    edge_valid,
    w_center,
    w_neighbor,
    w_radial,
    w_second,
    w_env,
    readout,
):
    atom_rows = feats.shape[2]
    own_feats = feats[0, 0]
    near_side = jnp.dot(own_feats, w_center, preferred_element_type=jnp.float32).astype(
        jnp.bfloat16
    )
    far_side = jnp.dot(own_feats, w_neighbor, preferred_element_type=jnp.float32).astype(
        jnp.bfloat16
    )
    ghost_far, ghost_pos = (
        extended(far_side[None, None], (("gx", 0), ("gy", 1)), 1),
        extended(positions, (("gx", 0), ("gy", 1)), 1),
    )
    far_ghost = ghost_far.reshape(9 * atom_rows, far_side.shape[1])
    pos_ghost = jnp.moveaxis(ghost_pos, 2, 0).reshape(3, 9 * atom_rows).astype(jnp.float32)
    row_counts = lax.dynamic_index_in_dim(atom_count, lax.axis_index("gx"), 0, keepdims=False)
    own_count = lax.dynamic_index_in_dim(row_counts, lax.axis_index("gy"), 0, keepdims=False)
    edge_slots = edge_valid.shape[2]
    block_total = edge_slots // EBLK
    used_blocks = (own_count * block_total + atom_rows - 1) // atom_rows
    block_id = jnp.arange(edge_slots, dtype=jnp.int32) // EBLK
    valid_int = edge_valid[0, 0] * (block_id < used_blocks).astype(jnp.int32)
    latent_fn = lambda preact: local_latent(preact, w_second)
    energy, ghost_force = edge_layer(
        near_side,
        far_ghost,
        pos_ghost,
        edge_center[0, 0],
        edge_neighbor[0, 0],
        valid_int,
        w_radial,
        w_second,
        w_env,
        readout,
        latent_fn,
    )
    folded = ghost_force.reshape(3, 3, 3, atom_rows)
    row_sum = return_rows(folded, 2)
    owned = return_slabs(row_sum, 1)
    return (energy[None, None], owned[None, None])


def solution(mesh):
    return jax.shard_map(
        body,
        mesh=mesh,
        in_specs=(
            P("gx", "gy", None, None),
            P("gx", "gy", None, None),
            P(),
            P("gx", "gy", None),
            P("gx", "gy", None),
            P("gx", "gy", None),
            P(),
            P(),
            P(),
            P(),
            P(),
            P(),
        ),
        out_specs=(P("gx", "gy", None), P("gx", "gy", None, None)),
        check_vma=False,
    )
```

profile of v0, /device:TPU:1, one launch (start us, length us, event | category | flops | bytes accessed | tf_op | source)
XLA Modules:
  0.0 125.7 jit_solution(4814522464941435412)
XLA Ops:
  0.7 4.2 %collective-permute-start.4 = (bf16[1,1,3,256]{3,2,1,0:T(4,128)(2,1)}, bf16[1,1,3,256]{3,2,1,0:T(4,128)(2,1)S(1)}, u32[]{:S(2)}, u32[]{:S(2)}) collective-permute-start(bf16[1,1,3,256]{3,2,1,0:T(4,128)(2,1)} %param.25), channel_id=1, source_target_pairs={{0,48},{48,96},{96,144},{144,192},{192,240},{240,288},{288,336},{3... | collective-permute-start | bytes 4616 | tf_op jit(solution)/shard_map/ppermute | solution.py:30
  4.8 6.1 %collective-permute-start.5 = (bf16[1,1,3,256]{3,2,1,0:T(4,128)(2,1)}, bf16[1,1,3,256]{3,2,1,0:T(4,128)(2,1)S(1)}, u32[]{:S(2)}, u32[]{:S(2)}) collective-permute-start(bf16[1,1,3,256]{3,2,1,0:T(4,128)(2,1)} %param.25), channel_id=1, source_target_pairs={{48,0},{96,48},{144,96},{192,144},{240,192},{288,240},{336,288},{3... | collective-permute-start | bytes 4616 | tf_op jit(solution)/shard_map/ppermute | solution.py:33
  12.0 3.4 %collective-permute-start.1 = (bf16[1,1,256,128]{3,2,1,0:T(8,128)(2,1)S(1)}, bf16[1,1,256,128]{3,2,1,0:T(8,128)(2,1)S(1)}, u32[]{:S(2)}, u32[]{:S(2)}) collective-permute-start(bf16[1,1,256,128]{3,2,1,0:T(8,128)(2,1)S(1)} %fusion.5), channel_id=1, source_target_pairs={{48,0},{96,48},{144,96},{192,144},{240,192},{288,240},{336,288},{3... | collective-permute-start | bytes 196616 | tf_op jit(solution)/shard_map/ppermute | solution.py:33
  15.3 1.9 %collective-permute-start = (bf16[1,1,256,128]{3,2,1,0:T(8,128)(2,1)S(1)}, bf16[1,1,256,128]{3,2,1,0:T(8,128)(2,1)S(1)}, u32[]{:S(2)}, u32[]{:S(2)}) collective-permute-start(bf16[1,1,256,128]{3,2,1,0:T(8,128)(2,1)S(1)} %fusion.5), channel_id=1, source_target_pairs={{0,48},{48,96},{96,144},{144,192},{192,240},{240,288},{288,336},{3... | collective-permute-start | bytes 196616 | tf_op jit(solution)/shard_map/ppermute | solution.py:30
  24.8 12.6 %collective-permute-start.7 = (bf16[3,1,3,256]{3,2,1,0:T(4,128)(2,1)S(1)}, bf16[3,1,3,256]{3,2,1,0:T(4,128)(2,1)S(1)}, u32[]{:S(2)}, u32[]{:S(2)}) collective-permute-start(bf16[3,1,3,256]{3,2,1,0:T(4,128)(2,1)S(1)} %constant_dynamic-update-slice_fusion), channel_id=1, source_target_pairs={{1,0},{2,1},{3,2},{4,3},{5,4},{6,5},{7,6},{8,7},{9,8},{10,9},{11,1... | collective-permute-start | bytes 13832 | tf_op jit(solution)/shard_map/ppermute | solution.py:33
  37.3 1.9 %collective-permute-start.6 = (bf16[3,1,3,256]{3,2,1,0:T(4,128)(2,1)S(1)}, bf16[3,1,3,256]{3,2,1,0:T(4,128)(2,1)S(1)}, u32[]{:S(2)}, u32[]{:S(2)}) collective-permute-start(bf16[3,1,3,256]{3,2,1,0:T(4,128)(2,1)S(1)} %constant_dynamic-update-slice_fusion), channel_id=1, source_target_pairs={{0,1},{1,2},{2,3},{3,4},{4,5},{5,6},{6,7},{7,8},{8,9},{9,10},{10,1... | collective-permute-start | bytes 13832 | tf_op jit(solution)/shard_map/ppermute | solution.py:30
  40.1 7.0 %collective-permute-done.6 = bf16[3,1,3,256]{3,2,1,0:T(4,128)(2,1)S(1)} collective-permute-done((bf16[3,1,3,256]{3,2,1,0:T(4,128)(2,1)S(1)}, bf16[3,1,3,256]{3,2,1,0:T(4,128)(2,1)S(1)}, u32[]{:S(2)}, u32[]{:S(2)}) %collective-permute-start.6) | collective-permute-done | bytes 4640 | tf_op jit(solution)/shard_map/ppermute | solution.py:30
  49.3 10.4 %collective-permute-start.3 = (bf16[3,1,256,128]{3,2,1,0:T(8,128)(2,1)S(1)}, bf16[3,1,256,128]{3,2,1,0:T(8,128)(2,1)S(1)}, u32[]{:S(2)}, u32[]{:S(2)}) collective-permute-start(bf16[3,1,256,128]{3,2,1,0:T(8,128)(2,1)S(1)} %pad_maximum_fusion.1), channel_id=1, source_target_pairs={{1,0},{2,1},{3,2},{4,3},{5,4},{6,5},{7,6},{8,7},{9,8},{10,9},{11,1... | collective-permute-start | bytes 589832 | tf_op jit(solution)/shard_map/ppermute | solution.py:33
  59.7 1.9 %collective-permute-start.2 = (bf16[3,1,256,128]{3,2,1,0:T(8,128)(2,1)S(1)}, bf16[3,1,256,128]{3,2,1,0:T(8,128)(2,1)S(1)}, u32[]{:S(2)}, u32[]{:S(2)}) collective-permute-start(bf16[3,1,256,128]{3,2,1,0:T(8,128)(2,1)S(1)} %pad_maximum_fusion.1), channel_id=1, source_target_pairs={{0,1},{1,2},{2,3},{3,4},{4,5},{5,6},{6,7},{7,8},{8,9},{9,10},{10,1... | collective-permute-start | bytes 589832 | tf_op jit(solution)/shard_map/ppermute | solution.py:30
  61.7 2.6 %collective-permute-done.2 = bf16[3,1,256,128]{3,2,1,0:T(8,128)(2,1)S(1)} collective-permute-done((bf16[3,1,256,128]{3,2,1,0:T(8,128)(2,1)S(1)}, bf16[3,1,256,128]{3,2,1,0:T(8,128)(2,1)S(1)}, u32[]{:S(2)}, u32[]{:S(2)}) %collective-permute-start.2) | collective-permute-done | bytes 196640 | tf_op jit(solution)/shard_map/ppermute | solution.py:30
  67.7 1.7 %scatter_custom_fusion.7 = f32[256,128]{1,0:T(8,128)S(1)} fusion(s32[256]{0:T(256)} %bitcast.131, f32[256]{0:T(256)S(1)} %get-tuple-element.129, f32[]{:T(128)} %constant.191.clone.1, f32[256,384]{1,0:T(8,128)S(1)} %convolution_multiply_fusion), kind=kCustom, calls=%fused_computation.84 | custom fusion | flops 65536 | bytes 263680 | tf_op jit(solution)/shard_map/scatter-add | solution.py:102
  69.4 1.7 %scatter_custom_fusion.8 = f32[256,128]{1,0:T(8,128)S(1)} fusion(s32[256]{0:T(256)} %bitcast.132, f32[256]{0:T(256)S(1)} %get-tuple-element.133, f32[]{:T(128)} %constant.191.clone.1, f32[256,384]{1,0:T(8,128)S(1)} %convolution_multiply_fusion), kind=kCustom, calls=%fused_computation.82 | custom fusion | flops 65536 | bytes 263680 | tf_op jit(solution)/shard_map/scatter-add | solution.py:102
  72.8 1.7 %scatter_custom_fusion.3 = f32[256,128]{1,0:T(8,128)S(1)} fusion(s32[256]{0:T(256)} %bitcast.134, f32[256,384]{1,0:T(8,128)S(1)} %convolution_multiply_fusion, f32[256]{0:T(256)S(1)} %get-tuple-element.127, f32[]{:T(128)} %constant.191.clone.1), kind=kCustom, calls=%fused_computation.92 | custom fusion | flops 65536 | bytes 263680 | tf_op jit(solution)/shard_map/scatter-add | solution.py:102
  74.5 1.7 %scatter_custom_fusion.5 = f32[256,128]{1,0:T(8,128)S(1)} fusion(s32[256]{0:T(256)} %bitcast.135, f32[256]{0:T(256)S(1)} %get-tuple-element.131, f32[]{:T(128)} %constant.191.clone.1, f32[256,384]{1,0:T(8,128)S(1)} %convolution_multiply_fusion), kind=kCustom, calls=%fused_computation.88 | custom fusion | flops 65536 | bytes 263680 | tf_op jit(solution)/shard_map/scatter-add | solution.py:102
  76.2 1.7 %scatter_custom_fusion.6 = f32[256,128]{1,0:T(8,128)S(1)} fusion(s32[256]{0:T(256)} %bitcast.136, f32[256]{0:T(256)S(1)} %get-tuple-element.128, f32[]{:T(128)} %constant.191.clone.1, f32[256,384]{1,0:T(8,128)S(1)} %convolution_multiply_fusion), kind=kCustom, calls=%fused_computation.86 | custom fusion | flops 65536 | bytes 263680 | tf_op jit(solution)/shard_map/scatter-add | solution.py:102
  77.9 1.9 %scatter_custom_fusion.4 = f32[256,128]{1,0:T(8,128)S(1)} fusion(s32[256]{0:T(256)} %bitcast.137, f32[256]{0:T(256)S(1)} %get-tuple-element.130, f32[]{:T(128)} %constant.191.clone.1, f32[256,384]{1,0:T(8,128)S(1)} %convolution_multiply_fusion), kind=kCustom, calls=%fused_computation.90 | custom fusion | flops 65536 | bytes 263680 | tf_op jit(solution)/shard_map/scatter-add | solution.py:102
  89.4 1.7 %scatter_custom_fusion.9 = f32[3,2304]{0,1:T(8,128)S(1)} fusion(s32[256]{0:T(256)S(1)} %bitcast.125, f32[256,3]{1,0:T(8,128)S(1)} %copy.60, f32[]{:T(128)} %constant.191.clone.1), kind=kCustom, calls=%fused_computation.42 | custom fusion | flops 768 | bytes 27652 | tf_op jit(solution)/shard_map/scatter-add | solution.py:140
  91.2 2.4 %scatter_fusion = f32[3,2304]{0,1:T(8,128)S(1)} fusion(f32[3,2304]{0,1:T(8,128)S(1)} %scatter_custom_fusion.9, s32[256]{0:T(256)S(1)} %bitcast.114, f32[256,3]{1,0:T(8,128)S(1)} %copy.61), kind=kCustom, calls=%fused_computation.23 | custom fusion | flops 768 | bytes 10240 | tf_op jit(solution)/shard_map/scatter-add | solution.py:141
  93.9 8.3 %collective-permute-start.9 = (f32[3,3,256]{2,0,1:T(4,128)S(1)}, f32[3,3,256]{2,0,1:T(4,128)S(1)}, u32[]{:S(2)}, u32[]{:S(2)}) collective-permute-start(f32[3,3,256]{2,0,1:T(4,128)S(1)} %bitcast.110), channel_id=1, source_target_pairs={{47,0},{0,1},{1,2},{2,3},{3,4},{4,5},{5,6},{6,7},{7,8},{8,9},{9,10... | collective-permute-start | bytes 27656 | tf_op jit(solution)/shard_map/ppermute | solution.py:21
  102.2 4.0 %collective-permute-start.8 = (f32[3,3,256]{2,0,1:T(4,128)S(1)}, f32[3,3,256]{2,0,1:T(4,128)S(1)}, u32[]{:S(2)}, u32[]{:S(2)}) collective-permute-start(f32[3,3,256]{2,0,1:T(4,128)S(1)} %bitcast.109), channel_id=1, source_target_pairs={{1,0},{2,1},{3,2},{4,3},{5,4},{6,5},{7,6},{8,7},{9,8},{10,9},{11,1... | collective-permute-start | bytes 27656 | tf_op jit(solution)/shard_map/ppermute | solution.py:21
  106.6 4.6 %collective-permute-done.8 = f32[3,3,256]{2,0,1:T(4,128)S(1)} collective-permute-done((f32[3,3,256]{2,0,1:T(4,128)S(1)}, f32[3,3,256]{2,0,1:T(4,128)S(1)}, u32[]{:S(2)}, u32[]{:S(2)}) %collective-permute-start.8) | collective-permute-done | bytes 9248 | tf_op jit(solution)/shard_map/ppermute | solution.py:21
  111.2 5.7 %collective-permute-start.10 = (f32[3,256]{1,0:T(4,128)S(1)}, f32[3,256]{1,0:T(4,128)S(1)}, u32[]{:S(2)}, u32[]{:S(2)}) collective-permute-start(f32[3,256]{1,0:T(4,128)S(1)} %get-tuple-element.109), channel_id=1, source_target_pairs={{48,0},{96,48},{144,96},{192,144},{240,192},{288,240},{336,288},{3... | collective-permute-start | bytes 9224 | tf_op jit(solution)/shard_map/ppermute | solution.py:21
  116.9 1.9 %collective-permute-start.11 = (f32[3,256]{1,0:T(4,128)S(1)}, f32[3,256]{1,0:T(4,128)S(1)}, u32[]{:S(2)}, u32[]{:S(2)}) collective-permute-start(f32[3,256]{1,0:T(4,128)S(1)} %get-tuple-element.110), channel_id=1, source_target_pairs={{720,0},{0,48},{48,96},{96,144},{144,192},{192,240},{240,288},{288... | collective-permute-start | bytes 9224 | tf_op jit(solution)/shard_map/ppermute | solution.py:21
  119.4 5.8 %collective-permute-done.11 = f32[3,256]{1,0:T(4,128)S(1)} collective-permute-done((f32[3,256]{1,0:T(4,128)S(1)}, f32[3,256]{1,0:T(4,128)S(1)}, u32[]{:S(2)}, u32[]{:S(2)}) %collective-permute-start.11) | collective-permute-done | bytes 3104 | tf_op jit(solution)/shard_map/ppermute | solution.py:21
  (90 shorter events, 27.2 us)
Async XLA Ops:
  0.6 65.2 %copy-start = (bf16[128,384]{1,0:T(8,128)(2,1)S(1)}, bf16[128,384]{1,0:T(8,128)(2,1)}, u32[]{:S(2)}) copy-start(bf16[128,384]{1,0:T(8,128)(2,1)} %param.34) | copy-start | bytes 294916
  0.6 24.1 %copy-start.2 = (bf16[1,1,3,256]{3,2,1,0:T(4,128)(2,1)S(1)}, bf16[1,1,3,256]{3,2,1,0:T(4,128)(2,1)}, u32[]{:S(2)}) copy-start(bf16[1,1,3,256]{3,2,1,0:T(4,128)(2,1)} %param.25) | copy-start | bytes 4612
  0.7 24.0 %collective-permute-start.4 = (bf16[1,1,3,256]{3,2,1,0:T(4,128)(2,1)}, bf16[1,1,3,256]{3,2,1,0:T(4,128)(2,1)S(1)}, u32[]{:S(2)}, u32[]{:S(2)}) collective-permute-start(bf16[1,1,3,256]{3,2,1,0:T(4,128)(2,1)} %param.25), channel_id=1, source_target_pairs={{0,48},{48,96},{96,144},{144,192},{192,240},{240,288},{288,336},{3... | collective-permute-start | bytes 4616 | tf_op jit(solution)/shard_map/ppermute | solution.py:30
  4.8 19.9 %collective-permute-start.5 = (bf16[1,1,3,256]{3,2,1,0:T(4,128)(2,1)}, bf16[1,1,3,256]{3,2,1,0:T(4,128)(2,1)S(1)}, u32[]{:S(2)}, u32[]{:S(2)}) collective-permute-start(bf16[1,1,3,256]{3,2,1,0:T(4,128)(2,1)} %param.25), channel_id=1, source_target_pairs={{48,0},{96,48},{144,96},{192,144},{240,192},{288,240},{336,288},{3... | collective-permute-start | bytes 4616 | tf_op jit(solution)/shard_map/ppermute | solution.py:33
  12.0 37.3 %collective-permute-start.1 = (bf16[1,1,256,128]{3,2,1,0:T(8,128)(2,1)S(1)}, bf16[1,1,256,128]{3,2,1,0:T(8,128)(2,1)S(1)}, u32[]{:S(2)}, u32[]{:S(2)}) collective-permute-start(bf16[1,1,256,128]{3,2,1,0:T(8,128)(2,1)S(1)} %fusion.5), channel_id=1, source_target_pairs={{48,0},{96,48},{144,96},{192,144},{240,192},{288,240},{336,288},{3... | collective-permute-start | bytes 196616 | tf_op jit(solution)/shard_map/ppermute | solution.py:33
  15.3 34.0 %collective-permute-start = (bf16[1,1,256,128]{3,2,1,0:T(8,128)(2,1)S(1)}, bf16[1,1,256,128]{3,2,1,0:T(8,128)(2,1)S(1)}, u32[]{:S(2)}, u32[]{:S(2)}) collective-permute-start(bf16[1,1,256,128]{3,2,1,0:T(8,128)(2,1)S(1)} %fusion.5), channel_id=1, source_target_pairs={{0,48},{48,96},{96,144},{144,192},{192,240},{240,288},{288,336},{3... | collective-permute-start | bytes 196616 | tf_op jit(solution)/shard_map/ppermute | solution.py:30
  24.8 15.4 %collective-permute-start.7 = (bf16[3,1,3,256]{3,2,1,0:T(4,128)(2,1)S(1)}, bf16[3,1,3,256]{3,2,1,0:T(4,128)(2,1)S(1)}, u32[]{:S(2)}, u32[]{:S(2)}) collective-permute-start(bf16[3,1,3,256]{3,2,1,0:T(4,128)(2,1)S(1)} %constant_dynamic-update-slice_fusion), channel_id=1, source_target_pairs={{1,0},{2,1},{3,2},{4,3},{5,4},{6,5},{7,6},{8,7},{9,8},{10,9},{11,1... | collective-permute-start | bytes 13832 | tf_op jit(solution)/shard_map/ppermute | solution.py:33
  37.3 9.8 %collective-permute-start.6 = (bf16[3,1,3,256]{3,2,1,0:T(4,128)(2,1)S(1)}, bf16[3,1,3,256]{3,2,1,0:T(4,128)(2,1)S(1)}, u32[]{:S(2)}, u32[]{:S(2)}) collective-permute-start(bf16[3,1,3,256]{3,2,1,0:T(4,128)(2,1)S(1)} %constant_dynamic-update-slice_fusion), channel_id=1, source_target_pairs={{0,1},{1,2},{2,3},{3,4},{4,5},{5,6},{6,7},{7,8},{8,9},{9,10},{10,1... | collective-permute-start | bytes 13832 | tf_op jit(solution)/shard_map/ppermute | solution.py:30
  49.1 16.1 %copy-start.1 = (f32[8,128]{1,0:T(8,128)S(1)}, f32[8,128]{1,0:T(8,128)}, u32[]{:S(2)}) copy-start(f32[8,128]{1,0:T(8,128)} %param.32) | copy-start | bytes 12292
  49.3 16.4 %copy-start.3 = (bf16[128,128]{1,0:T(8,128)(2,1)S(1)}, bf16[128,128]{1,0:T(8,128)(2,1)}, u32[]{:S(2)}) copy-start(bf16[128,128]{1,0:T(8,128)(2,1)} %param.33) | copy-start | bytes 98308
  49.3 12.4 %collective-permute-start.3 = (bf16[3,1,256,128]{3,2,1,0:T(8,128)(2,1)S(1)}, bf16[3,1,256,128]{3,2,1,0:T(8,128)(2,1)S(1)}, u32[]{:S(2)}, u32[]{:S(2)}) collective-permute-start(bf16[3,1,256,128]{3,2,1,0:T(8,128)(2,1)S(1)} %pad_maximum_fusion.1), channel_id=1, source_target_pairs={{1,0},{2,1},{3,2},{4,3},{5,4},{6,5},{7,6},{8,7},{9,8},{10,9},{11,1... | collective-permute-start | bytes 589832 | tf_op jit(solution)/shard_map/ppermute | solution.py:33
  59.7 4.5 %collective-permute-start.2 = (bf16[3,1,256,128]{3,2,1,0:T(8,128)(2,1)S(1)}, bf16[3,1,256,128]{3,2,1,0:T(8,128)(2,1)S(1)}, u32[]{:S(2)}, u32[]{:S(2)}) collective-permute-start(bf16[3,1,256,128]{3,2,1,0:T(8,128)(2,1)S(1)} %pad_maximum_fusion.1), channel_id=1, source_target_pairs={{0,1},{1,2},{2,3},{3,4},{4,5},{5,6},{6,7},{7,8},{8,9},{9,10},{10,1... | collective-permute-start | bytes 589832 | tf_op jit(solution)/shard_map/ppermute | solution.py:30
  93.9 12.6 %collective-permute-start.9 = (f32[3,3,256]{2,0,1:T(4,128)S(1)}, f32[3,3,256]{2,0,1:T(4,128)S(1)}, u32[]{:S(2)}, u32[]{:S(2)}) collective-permute-start(f32[3,3,256]{2,0,1:T(4,128)S(1)} %bitcast.110), channel_id=1, source_target_pairs={{47,0},{0,1},{1,2},{2,3},{3,4},{4,5},{5,6},{6,7},{7,8},{8,9},{9,10... | collective-permute-start | bytes 27656 | tf_op jit(solution)/shard_map/ppermute | solution.py:21
  102.2 8.9 %collective-permute-start.8 = (f32[3,3,256]{2,0,1:T(4,128)S(1)}, f32[3,3,256]{2,0,1:T(4,128)S(1)}, u32[]{:S(2)}, u32[]{:S(2)}) collective-permute-start(f32[3,3,256]{2,0,1:T(4,128)S(1)} %bitcast.109), channel_id=1, source_target_pairs={{1,0},{2,1},{3,2},{4,3},{5,4},{6,5},{7,6},{8,7},{9,8},{10,9},{11,1... | collective-permute-start | bytes 27656 | tf_op jit(solution)/shard_map/ppermute | solution.py:21
  111.2 8.2 %collective-permute-start.10 = (f32[3,256]{1,0:T(4,128)S(1)}, f32[3,256]{1,0:T(4,128)S(1)}, u32[]{:S(2)}, u32[]{:S(2)}) collective-permute-start(f32[3,256]{1,0:T(4,128)S(1)} %get-tuple-element.109), channel_id=1, source_target_pairs={{48,0},{96,48},{144,96},{192,144},{240,192},{288,240},{336,288},{3... | collective-permute-start | bytes 9224 | tf_op jit(solution)/shard_map/ppermute | solution.py:21
  116.9 8.3 %collective-permute-start.11 = (f32[3,256]{1,0:T(4,128)S(1)}, f32[3,256]{1,0:T(4,128)S(1)}, u32[]{:S(2)}, u32[]{:S(2)}) collective-permute-start(f32[3,256]{1,0:T(4,128)S(1)} %get-tuple-element.110), channel_id=1, source_target_pairs={{720,0},{0,48},{48,96},{96,144},{144,192},{192,240},{240,288},{288... | collective-permute-start | bytes 9224 | tf_op jit(solution)/shard_map/ppermute | solution.py:21
where the time goes:
time: 128 us; the launch traced here: 126 us
  starting transfers between devices  62.4 us (49%)
  other arithmetic  25.2 us (20%)
  waiting for transfers between devices  20 us (16%)
  local copies, waits for them, and re-layouts  13 us (10%)
  matrix products  3.39 us (3%)
  between operations  1.85 us (1%)
    ppermute x4, starting transfers between devices, extended(): lax.ppermute(lax.slice_in_dim(block, 0, width, axis=dim), axis, backward)  32.5 us
    ppermute x4, starting transfers between devices, passed_along(): return lax.ppermute(block, axis, route)  20 us
    scatter-add x9, other arithmetic, edge_layer(): jax.ops.segment_sum(env_parts[level] * harmonics[comp][:, None], center,...  15.3 us
    ppermute x4, waiting for transfers between devices, passed_along(): return lax.ppermute(block, axis, route)  10.4 us
    ppermute x4, starting transfers between devices, extended(): lax.ppermute(lax.slice_in_dim(block, block.shape[dim] - width, None, axis...  9.93 us
    ppermute x4, waiting for transfers between devices, extended(): lax.ppermute(lax.slice_in_dim(block, block.shape[dim] - width, None, axis...  9.58 us
    gather x9, local copies, waits for them, and re-layouts, edge_layer(): edge_grads.append(agg_grad[center])  6.57 us
  transfers between devices with their start and end apart: 12, of which 4 were waited for; matrix products, arithmetic and copies ran while one was open for 9% of the time, Pallas kernels for 0%

commit v1 on v0

v1 whole, which is shorter than its diff:
```python
import math

import jax
import jax.numpy as jnp
from jax import lax
from jax.experimental import pallas as pl
from jax.experimental.pallas import tpu as pltpu
from jax.sharding import PartitionSpec as P

NBASIS = 8
EBLK = 64
POS_ROWS = 16

ROOT_THREE = math.sqrt(3.0)
ROOT_FIFTEEN = math.sqrt(15.0)
ROOT_FIVE = math.sqrt(5.0)
GAMMAS = [0.25 * 1.5**k for k in range(NBASIS)]

NN = (((1,), (0,)), ((), ()))
NT = (((1,), (1,)), ((), ()))


def mm(a, b, dims=NN):
    return lax.dot_general(a, b, dims, preferred_element_type=jnp.float32)


def turned(w):
    return w.astype(jnp.float32).T


def halves(x):
    high = x.astype(jnp.bfloat16).astype(jnp.float32)
    return high, x - high


def prepare(
    feats,
    positions,
    atom_count,
    center,
    neighbor,
    valid,
    w_center,
    w_neighbor,
    w_radial,
    w_second,
    w_env,
    readout,
    hot_nb,
    hot_c,
    same,
    near,
    aux,
    wn_t,
    w2_t,
    we_t,
    wr_t,
    wr16,
    read_b,
):
    atoms = feats.shape[2]
    edges = center.shape[2]
    gx, gy = lax.axis_index("gx"), lax.axis_index("gy")
    c_row = center[0]
    n_row = neighbor[0]
    slot = n_row // atoms
    atom = n_row - slot * atoms
    row_a = jnp.where(slot >= 3, 1, 0) + jnp.where(slot >= 6, 1, 0)
    row_b = slot - 3 * row_a
    in_a = 2 - 2 * (gx % 2)
    in_b = 2 - 2 * (gy % 2)
    place_x = jnp.where(row_a == 1, 0, jnp.where(row_a == in_a, 1, 2))
    place_y = jnp.where(row_b == 1, 0, jnp.where(row_b == in_b, 1, 2))
    local = (3 * place_y + place_x) * atoms + atom
    stacked = jnp.concatenate(
        [
            jnp.broadcast_to(local.astype(jnp.float32), (8, edges)),
            jnp.broadcast_to(c_row.astype(jnp.float32), (8, edges)),
        ],
        axis=0,
    ).T
    n_col = stacked[:, 0:1].astype(jnp.int32)
    c_col = stacked[:, 8:9].astype(jnp.int32)
    lane = lax.broadcasted_iota(jnp.int32, (edges, atoms), 1)
    for part in range(9):
        hot_nb[:, part * atoms : (part + 1) * atoms] = jnp.where(
            lane == n_col - part * atoms, 1.0, 0.0
        ).astype(jnp.bfloat16)
    c_hot = jnp.where(lane == c_col, 1.0, 0.0).astype(jnp.bfloat16)
    hot_c[...] = c_hot
    same[...] = jnp.where(c_col == c_row, 1.0, 0.0).astype(jnp.bfloat16)

    near_all = mm(feats[0, 0], w_center[...]).astype(jnp.bfloat16)
    near[...] = mm(c_hot, near_all).T
    pos16 = jnp.concatenate(
        [positions[0, 0].astype(jnp.float32), jnp.zeros((13, atoms), jnp.float32)], axis=0
    ).astype(jnp.bfloat16)
    pos_c = mm(pos16, c_hot, NT)
    used = (atom_count[gx, gy] * (edges // EBLK) + atoms - 1) // atoms
    block = lax.broadcasted_iota(jnp.int32, (1, edges), 1) // EBLK
    mask = jnp.where(block < used, valid[0], 0).astype(jnp.float32)
    aux[...] = jnp.concatenate(
        [
            (row_a - 1).astype(jnp.float32),
            (row_b - 1).astype(jnp.float32),
            jnp.zeros((1, edges), jnp.float32),
            mask,
            jnp.zeros((4, edges), jnp.float32),
            pos_c[0:8],
        ],
        axis=0,
    )

    wn_t[...] = turned(w_neighbor[...]).astype(jnp.bfloat16)
    w2_t[...] = turned(w_second[...]).astype(jnp.bfloat16)
    we_t[...] = turned(w_env[...]).astype(jnp.bfloat16)
    high, low = halves(w_radial[...])
    wr16[...] = jnp.concatenate([high, low], axis=0).astype(jnp.bfloat16)
    wr_t[...] = (
        jnp.concatenate([high, high, low, jnp.zeros_like(high)], axis=0).T.astype(jnp.bfloat16)
    )
    channels = w_center.shape[0]
    read_t = jnp.concatenate(
        [readout[...], jnp.zeros((5, channels), jnp.float32)], axis=0
    ).T
    for level in range(3):
        read_b[level] = jnp.broadcast_to(read_t[:, level : level + 1], (channels, edges))


def layer(
    slab_own,
    slab_in,
    slab_out,
    hot_nb,
    hot_c,
    same,
    near,
    aux,
    wn_t,
    w2_t,
    we_t,
    wr_t,
    wr16,
    read_b,
    w_second,
    w_env,
    energy,
    f_own,
    f_in,
    f_out,
):
    bf16, f32 = jnp.bfloat16, jnp.float32
    channels, edges = near.shape
    atoms = hot_c.shape[1]
    wide = 3 * atoms
    rows_nb = jnp.zeros((edges, channels), f32)
    pos_nb = jnp.zeros((8, edges), f32)
    for part, slab in enumerate((slab_own, slab_in, slab_out)):
        hot = hot_nb[:, part * wide : (part + 1) * wide]
        rows_nb = rows_nb + mm(hot, slab[0:wide])
        packed = slab[wide : wide + 3 * POS_ROWS].astype(f32)
        pos = jnp.concatenate([packed[8 * k : 8 * k + 8] for k in range(6)], axis=1)
        pos = jnp.concatenate([pos, jnp.zeros_like(pos)], axis=0).astype(bf16)
        pos_nb = pos_nb + mm(pos, hot, NT)[0:8]
    far = mm(wn_t[...], rows_nb.astype(bf16), NT).astype(bf16).astype(f32)

    mask = aux[3:4]
    d = pos_nb[0:3] + aux[0:3] - aux[8:11]
    dist_sq = jnp.sum(d * d, axis=0, keepdims=True) + 0.25
    inv = lax.rsqrt(dist_sq)
    dist = jnp.sqrt(dist_sq)
    u = d / dist
    ux, uy, uz = u[0:1], u[1:2], u[2:3]
    sub = lax.broadcasted_iota(jnp.int32, (NBASIS, edges), 0)
    gamma = jnp.full((NBASIS, edges), GAMMAS[0], f32)
    for k in range(1, NBASIS):
        gamma = jnp.where(sub == k, GAMMAS[k], gamma)
    basis = jnp.exp(-gamma * dist_sq)
    b_high, b_low = halves(basis)
    b32 = jnp.concatenate([b_high, b_low, b_high, jnp.zeros_like(b_high)], axis=0).astype(bf16)
    radial = mm(wr_t[...], b32)
    pre = (near[...] + far + radial).astype(bf16).astype(f32)
    sig = jax.nn.sigmoid(pre)
    latent = jnp.tanh(mm(w2_t[...], (pre * sig).astype(bf16))).astype(bf16)
    env = mm(we_t[...], latent) * mask
    harm = [
        None,
        ROOT_THREE * ux,
        ROOT_THREE * uy,
        ROOT_THREE * uz,
        ROOT_FIFTEEN * ux * uy,
        ROOT_FIFTEEN * uy * uz,
        0.5 * ROOT_FIVE * (3.0 * uz * uz - 1.0),
        ROOT_FIFTEEN * ux * uz,
        0.5 * ROOT_FIFTEEN * (ux * ux - uy * uy),
    ]
    term = jnp.sum(read_b[0] * env[0:channels], axis=0, keepdims=True)
    grads = [read_b[0] * mask]
    hg = [None] * 9
    for level, comps in ((1, (1, 2, 3)), (2, (4, 5, 6, 7, 8))):
        part = env[level * channels : (level + 1) * channels]
        twice = 2.0 * read_b[level]
        scaled = twice * part
        total = jnp.zeros((channels, edges), f32)
        for m in comps:
            gathered = mm((part * harm[m]).astype(bf16), same[...])
            hg[m] = jnp.sum(gathered * scaled, axis=0, keepdims=True)
            total = total + gathered * harm[m]
            term = term + 0.5 * harm[m] * hg[m]
        grads.append(twice * total * mask)
    env_grad = jnp.concatenate(grads, axis=0).astype(bf16)
    lat = latent.astype(f32)
    act_grad = (mm(w_env[...], env_grad) * (1.0 - lat * lat)).astype(bf16)
    pre_grad = mm(w_second[...], act_grad) * sig * (1.0 + pre * (1.0 - sig))
    p_high, p_low = halves(pre_grad)
    both = mm(wr16[...], p_high.astype(bf16)) + mm(wr16[...], p_low.astype(bf16))
    basis_grad = both[0:NBASIS] + both[NBASIS : 2 * NBASIS]
    ds = -jnp.sum(gamma * basis * basis_grad, axis=0, keepdims=True)
    gx = ROOT_THREE * hg[1] + ROOT_FIFTEEN * (uy * hg[4] + uz * hg[7] + ux * hg[8])
    gy = ROOT_THREE * hg[2] + ROOT_FIFTEEN * (ux * hg[4] + uz * hg[5] - uy * hg[8])
    gz = ROOT_THREE * hg[3] + ROOT_FIFTEEN * (uy * hg[5] + ux * hg[7]) + 3.0 * ROOT_FIVE * uz * hg[6]
    ds = ds - 0.5 * inv * inv * (gx * ux + gy * uy + gz * uz)
    g = jnp.concatenate([gx, gy, gz], axis=0)
    dg = g * inv + 2.0 * d * ds
    four_high, four_low = halves(jnp.concatenate([dg, term], axis=0))
    lines = jnp.concatenate([four_high, four_low, jnp.zeros((8, edges), f32)], axis=0).astype(bf16)
    to_c = mm(lines, hot_c[...])
    to_c = to_c[0:4] + to_c[4:8]
    energy[0] = to_c[3:4]
    for part, out in enumerate((f_own, f_in, f_out)):
        to_nb = mm(lines, hot_nb[:, part * wide : (part + 1) * wide])
        to_nb = -(to_nb[0:3] + to_nb[4:7])
        if part == 0:
            out[:, 0:atoms] = to_nb[:, 0:atoms] + to_c[0:3]
            out[:, atoms:wide] = to_nb[:, atoms:wide]
        else:
            out[...] = to_nb


def vmem(n):
    return [pl.BlockSpec(memory_space=pltpu.VMEM)] * n


def pair_in(axis):
    return [(i, i ^ 1) for i in range(lax.axis_size(axis))]


def pair_out(axis):
    count = lax.axis_size(axis)
    return [(i, (i + 1) % count if i % 2 else (i - 1) % count) for i in range(count)]


def body(
    feats,
    positions,
    atom_count,
    edge_center,
    edge_neighbor,
    edge_valid,
    w_center,
    w_neighbor,
    w_radial,
    w_second,
    w_env,
    readout,
):
    f32, bf16 = jnp.float32, jnp.bfloat16
    atoms, channels = feats.shape[2:]
    edges = edge_center.shape[2]
    half = atoms // 2
    pos = positions[0, 0]
    gap = jnp.zeros((5, half), bf16)
    pos_rows = jnp.concatenate([pos[:, :half], gap, pos[:, half:], gap], axis=0)
    own = jnp.concatenate([feats[0, 0], pos_rows], axis=0)
    x_out = lax.ppermute(own, "gx", pair_out("gx"))
    x_in = lax.ppermute(own, "gx", pair_in("gx"))

    shape = jax.ShapeDtypeStruct
    prepared = pl.pallas_call(
        prepare,
        out_shape=[
            shape((edges, 9 * atoms), bf16),
            shape((edges, atoms), bf16),
            shape((edges, edges), bf16),
            shape((channels, edges), f32),
            shape((16, edges), f32),
            shape((channels, channels), bf16),
            shape((channels, channels), bf16),
            shape((3 * channels, channels), bf16),
            shape((channels, 4 * NBASIS), bf16),
            shape((2 * NBASIS, channels), bf16),
            shape((3, channels, edges), f32),
        ],
        in_specs=vmem(2) + [pl.BlockSpec(memory_space=pltpu.SMEM)] + vmem(9),
        out_specs=vmem(11),
        name="prepare",
        cost_estimate=pl.CostEstimate(flops=100000000, bytes_accessed=3000000, transcendentals=0),
    )(
        feats,
        positions,
        atom_count,
        edge_center,
        edge_neighbor,
        edge_valid,
        w_center,
        w_neighbor,
        w_radial,
        w_second,
        w_env,
        readout,
    )

    slab = jnp.concatenate(
        [part[:atoms] for part in (own, x_in, x_out)] + [part[atoms:] for part in (own, x_in, x_out)],
        axis=0,
    )
    y_out = lax.ppermute(slab, "gy", pair_out("gy"))
    y_in = lax.ppermute(slab, "gy", pair_in("gy"))

    energy, f_own, f_in, f_out = pl.pallas_call(
        layer,
        out_shape=[shape((1, 1, edges), f32)] + [shape((3, 3 * atoms), f32)] * 3,
        in_specs=vmem(16),
        out_specs=vmem(4),
        name="layer",
    )(slab, y_in, y_out, *prepared, w_second, w_env)

    r_out = lax.ppermute(f_out, "gy", pair_out("gy"))
    r_in = lax.ppermute(f_in, "gy", pair_in("gy"))
    column = f_own + r_out + r_in
    s_out = lax.ppermute(column[:, 2 * atoms :], "gx", pair_out("gx"))
    s_in = lax.ppermute(column[:, atoms : 2 * atoms], "gx", pair_in("gx"))
    forces = column[:, :atoms] + s_out + s_in
    return (energy, forces[None, None])


def solution(mesh):
    return jax.shard_map(
        body,
        mesh=mesh,
        in_specs=(
            P("gx", "gy", None, None),
            P("gx", "gy", None, None),
            P(),
            P("gx", "gy", None),
            P("gx", "gy", None),
            P("gx", "gy", None),
            P(),
            P(),
            P(),
            P(),
            P(),
            P(),
        ),
        out_specs=(P("gx", "gy", None), P("gx", "gy", None, None)),
        check_vma=False,
    )
```

time: 128 us -> 69 us (0.54); the launches traced: 126 us -> 68.4 us
  other arithmetic: 25.2 us -> 0.72 us
  starting transfers between devices: 62.4 us -> 48.8 us
  waiting for transfers between devices: 20 us -> 6.53 us
  local copies, waits for them, and re-layouts: 13 us -> 3.94 us
  Pallas kernels: 0 us -> 7.62 us
  matrix products: 3.39 us -> 0 us
    scatter-add x11 -> x0, other arithmetic: 19.4 us -> none  [the longest x9 15.3 us: edge_layer(): jax.ops.segment_sum(env_parts[level] * harmonics[comp][:, None], center,...]
    ppermute x12 -> x8, starting transfers between devices: 62.4 us -> 48.8 us  [the longest x1 12.7 us: body(): y_in = lax.ppermute(slab, 'gy', pair_in('gy'))]
    ppermute x12 -> x8, waiting for transfers between devices: 20 us -> 6.53 us  [the longest x1 3.09 us: body(): x_in = lax.ppermute(own, 'gx', pair_in('gx'))]
    gather x16 -> x0, local copies, waits for them, and re-layouts: 9.9 us -> none  [the longest x9 6.57 us: edge_layer(): edge_grads.append(agg_grad[center])]
    pallas_call x0 -> x2, Pallas kernels: none -> 7.62 us  [the longest x1 4.7 us: body(): pl.pallas_call(layer, out_shape=[shape((1, 1, edges), f32)] + [shape((3,...]
    dot_general x7 -> x0, matrix products: 3.39 us -> none  [the longest x1 0.99 us: body(): jnp.dot(own_feats, w_neighbor, preferred_element_type=jnp.float32)]
    concatenate x1 -> x2, local copies, waits for them, and re-layouts: 0.01 us -> 1.88 us  [the longest x1 0.97 us: body(): jnp.concatenate([part[:atoms] for part in (own, x_in, x_out)] + [part[ato...]
    select_n x2 -> x0, other arithmetic: 1.37 us -> none  [the longest x1 0.69 us: edge_layer(): near_side[center].astype(jnp.float32)]
  transfers between devices with their start and end apart: 12 -> 8, of which waited for: 4 -> 3; matrix products, arithmetic and copies ran while one was open for 9% -> 0% of each run, Pallas kernels for 0% -> 4%
where the time goes in v1:
time: 69 us; the launch traced here: 68.4 us
  starting transfers between devices  48.8 us (71%)
  Pallas kernels  7.62 us (11%)
  waiting for transfers between devices  6.53 us (9%)
  local copies, waits for them, and re-layouts  3.94 us (6%)
  between operations  0.77 us (1%)
  other arithmetic  0.72 us (1%)
    ppermute x1, starting transfers between devices, body(): y_in = lax.ppermute(slab, 'gy', pair_in('gy'))  12.7 us
    ppermute x1, starting transfers between devices, body(): r_in = lax.ppermute(f_in, 'gy', pair_in('gy'))  9.09 us
    ppermute x1, starting transfers between devices, body(): x_out = lax.ppermute(own, 'gx', pair_out('gx'))  8.24 us
    ppermute x1, starting transfers between devices, body(): y_out = lax.ppermute(slab, 'gy', pair_out('gy'))  6.73 us
    ppermute x1, starting transfers between devices, body(): s_out = lax.ppermute(column[:, 2 * atoms:], 'gx', pair_out('gx'))  6.31 us
    pallas_call x1, Pallas kernels, body(): pl.pallas_call(layer, out_shape=[shape((1, 1, edges), f32)] + [shape((3,...  4.7 us
    ppermute x1, waiting for transfers between devices, body(): x_in = lax.ppermute(own, 'gx', pair_in('gx'))  3.09 us
    pallas_call x1, Pallas kernels, body(): pl.pallas_call(prepare, out_shape=[shape((edges, 9 * atoms), bf16), shape...  2.92 us
  transfers between devices with their start and end apart: 8, of which 3 were waited for; matrix products, arithmetic and copies ran while one was open for 0% of the time, Pallas kernels for 4%

profile of v1, /device:TPU:1, one launch (start us, length us, event | category | flops | bytes accessed | tf_op | source)
XLA Modules:
  0.0 68.4 jit_solution(3296365029705528342)
XLA Ops:
  0.6 0.7 %fusion.3 = (bf16[3,128]{1,0:T(4,128)(2,1)S(1)}, bf16[3,128]{1,0:T(4,128)(2,1)S(1)}) fusion(bf16[3,256]{1,0:T(4,128)(2,1)} %bitcast.6), kind=kLoop, calls=%fused_computation.5 | loop fusion | bytes 3072 | tf_op jit(solution)/shard_map/slice | solution.py:273
  1.3 0.9 %concatenate.9 = bf16[272,128]{1,0:T(8,128)(2,1)S(1)} concatenate(bf16[256,128]{1,0:T(8,128)(2,1)} %bitcast.4, bf16[3,128]{1,0:T(4,128)(2,1)S(1)} %get-tuple-element.37, bf16[5,128]{1,0:T(8,128)(2,1)S(1)} %broadcast_in_dim.6, bf16[3,128]{1,0:T(4,128)(2,1)S(1)} %get-tuple-element.36, bf16[5,128]{1,0:T(8,128)(2,1)S(1)} %broadcast_in_dim.6), dimensions={0} | concatenate | bytes 139264 | tf_op jit(solution)/shard_map/concatenate | solution.py:274
  2.2 8.2 %collective-permute-start.1 = (bf16[272,128]{1,0:T(8,128)(2,1)S(1)}, bf16[272,128]{1,0:T(8,128)(2,1)S(1)}, u32[]{:S(2)}, u32[]{:S(2)}) collective-permute-start(bf16[272,128]{1,0:T(8,128)(2,1)S(1)} %concatenate.9), channel_id=1, source_target_pairs={{0,720},{48,96},{96,48},{144,192},{192,144},{240,288},{288,240},{3... | collective-permute-start | bytes 208904 | tf_op jit(solution)/shard_map/ppermute | solution.py:275
  10.5 1.9 %collective-permute-start = (bf16[272,128]{1,0:T(8,128)(2,1)S(1)}, bf16[272,128]{1,0:T(8,128)(2,1)S(1)}, u32[]{:S(2)}, u32[]{:S(2)}) collective-permute-start(bf16[272,128]{1,0:T(8,128)(2,1)S(1)} %concatenate.9), channel_id=1, source_target_pairs={{0,48},{48,0},{96,144},{144,96},{192,240},{240,192},{288,336},{336... | collective-permute-start | bytes 208904 | tf_op jit(solution)/shard_map/ppermute | solution.py:276
  12.4 0.0 collective-permute-done.1
  12.5 3.1 %collective-permute-done = bf16[272,128]{1,0:T(8,128)(2,1)S(1)} collective-permute-done((bf16[272,128]{1,0:T(8,128)(2,1)S(1)}, bf16[272,128]{1,0:T(8,128)(2,1)S(1)}, u32[]{:S(2)}, u32[]{:S(2)}) %collective-permute-start) | collective-permute-done | bytes 69664 | tf_op jit(solution)/shard_map/ppermute | solution.py:276
  15.6 1.0 %concatenate.10.slab_own = bf16[816,128]{1,0:T(8,128)(2,1)S(1)} concatenate(bf16[256,128]{1,0:T(8,128)(2,1)} %bitcast.5, bf16[256,128]{1,0:T(8,128)(2,1)S(1)} %slice.38, bf16[256,128]{1,0:T(8,128)(2,1)S(1)} %slice.39, bf16[3,128]{1,0:T(4,128)(2,1)S(1)} %get-tuple-element.37, bf16[5,128]{1,0:T(8,128)(2,1)S(1)} %broadcast_in_dim.6, bf16[3,128]{1,0:T(4,128)(2,1)S(1)} %get-tuple-element.36, ...), dimensions={0} | concatenate | bytes 417792 | tf_op jit(solution)/shard_map/concatenate | solution.py:313
  16.5 6.7 %collective-permute-start.3 = (bf16[816,128]{1,0:T(8,128)(2,1)S(1)}, bf16[816,128]{1,0:T(8,128)(2,1)S(1)}, u32[]{:S(2)}, u32[]{:S(2)}) collective-permute-start(bf16[816,128]{1,0:T(8,128)(2,1)S(1)} %concatenate.10.slab_own), channel_id=1, source_target_pairs={{0,47},{1,2},{2,1},{3,4},{4,3},{5,6},{6,5},{7,8},{8,7},{9,10},{10,... | collective-permute-start | bytes 626696 | tf_op jit(solution)/shard_map/ppermute | solution.py:317
  23.3 12.7 %collective-permute-start.2 = (bf16[816,128]{1,0:T(8,128)(2,1)S(1)}, bf16[816,128]{1,0:T(8,128)(2,1)S(1)}, u32[]{:S(2)}, u32[]{:S(2)}) collective-permute-start(bf16[816,128]{1,0:T(8,128)(2,1)S(1)} %concatenate.10.slab_own), channel_id=1, source_target_pairs={{0,1},{1,0},{2,3},{3,2},{4,5},{5,4},{6,7},{7,6},{8,9},{9,8},{10,11... | collective-permute-start | bytes 626696 | tf_op jit(solution)/shard_map/ppermute | solution.py:318
  36.0 2.9 %prepare.1 = (bf16[256,2304]{1,0:T(8,128)(2,1)}, bf16[256,256]{1,0:T(8,128)(2,1)}, bf16[256,256]{1,0:T(8,128)(2,1)}, f32[128,256]{1,0:T(8,128)}, f32[16,256]{1,0...) custom-call(bf16[1,1,256,128]{3,2,1,0:T(8,128)(2,1)} %feats.1, ...), custom_call_target="tpu_custom_call" | custom-call | flops 100000000 | bytes 3000000 | tf_op jit(solution)/shard_map/prepare/pallas_call | solution.py:279
  38.9 0.0 collective-permute-done.3.slab_out
  38.9 0.0 collective-permute-done.2.slab_in
  39.0 0.6 copy-done.1
  39.6 0.1 copy-done.2
  39.7 4.7 %layer.1 = (f32[1,1,256]{2,1,0:T(1,128)}, f32[3,768]{1,0:T(4,128)}, f32[3,768]{1,0:T(4,128)}, f32[3,768]{1,0:T(4,128)}) custom-call(bf16[816,128]{1,0:T(8,128)(2,1)} %copy-done, bf16[816,128]{1,0:T(8,128)(2,1)} %copy-done.2, bf16[816,128]{1,0:T(8,128)(2,1)} %copy-done.1, bf16[256,2304]{1,0:T(8,128)(2,1)} %get-tuple-element.17.hot_nb, ...), custom_call_target="tpu_custom_call" | custom-call | tf_op jit(solution)/shard_map/layer/pallas_call | solution.py:320
  44.4 1.9 %collective-permute-start.4 = (f32[3,768]{1,0:T(4,128)}, f32[3,768]{1,0:T(4,128)S(1)}, u32[]{:S(2)}, u32[]{:S(2)}) collective-permute-start(f32[3,768]{1,0:T(4,128)} %get-tuple-element.30), channel_id=1, source_target_pairs={{0,47},{1,2},{2,1},{3,4},{4,3},{5,6},{6,5},{7,8},{8,7},{9,10},{10,... | collective-permute-start | bytes 27656 | tf_op jit(solution)/shard_map/ppermute | solution.py:328
  46.3 9.1 %collective-permute-start.5 = (f32[3,768]{1,0:T(4,128)}, f32[3,768]{1,0:T(4,128)S(1)}, u32[]{:S(2)}, u32[]{:S(2)}) collective-permute-start(f32[3,768]{1,0:T(4,128)} %get-tuple-element.31), channel_id=1, source_target_pairs={{0,1},{1,0},{2,3},{3,2},{4,5},{5,4},{6,7},{7,6},{8,9},{9,8},{10,11... | collective-permute-start | bytes 27656 | tf_op jit(solution)/shard_map/ppermute | solution.py:329
  55.4 1.0 %collective-permute-done.5 = f32[3,768]{1,0:T(4,128)S(1)} collective-permute-done((f32[3,768]{1,0:T(4,128)}, f32[3,768]{1,0:T(4,128)S(1)}, u32[]{:S(2)}, u32[]{:S(2)}) %collective-permute-start.5) | collective-permute-done | bytes 9248 | tf_op jit(solution)/shard_map/ppermute | solution.py:329
  56.4 0.7 %add_add_fusion = f32[3,768]{1,0:T(4,128)S(1)} fusion(f32[3,768]{1,0:T(4,128)S(1)} %collective-permute-done.5, f32[3,768]{1,0:T(4,128)} %get-tuple-element.29, f32[3,768]{1,0:T(4,128)S(1)} %collective-permute-done.4), kind=kLoop, calls=%fused_computation | loop fusion | flops 4608 | bytes 36864 | tf_op jit(solution)/shard_map/add | solution.py:330
  57.2 6.3 %collective-permute-start.6 = (f32[3,256]{1,0:T(4,128)S(1)}, f32[3,256]{1,0:T(4,128)S(1)}, u32[]{:S(2)}, u32[]{:S(2)}) collective-permute-start(f32[3,256]{1,0:T(4,128)S(1)} %get-tuple-element.34), channel_id=1, source_target_pairs={{0,720},{48,96},{96,48},{144,192},{192,144},{240,288},{288,240},{3... | collective-permute-start | bytes 9224 | tf_op jit(solution)/shard_map/ppermute | solution.py:331
  63.5 1.9 %collective-permute-start.7 = (f32[3,256]{1,0:T(4,128)S(1)}, f32[3,256]{1,0:T(4,128)S(1)}, u32[]{:S(2)}, u32[]{:S(2)}) collective-permute-start(f32[3,256]{1,0:T(4,128)S(1)} %get-tuple-element.35), channel_id=1, source_target_pairs={{0,48},{48,0},{96,144},{144,96},{192,240},{240,192},{288,336},{336... | collective-permute-start | bytes 9224 | tf_op jit(solution)/shard_map/ppermute | solution.py:332
  65.4 0.0 collective-permute-done.6
  65.4 2.4 %collective-permute-done.7 = f32[3,256]{1,0:T(4,128)S(1)} collective-permute-done((f32[3,256]{1,0:T(4,128)S(1)}, f32[3,256]{1,0:T(4,128)S(1)}, u32[]{:S(2)}, u32[]{:S(2)}) %collective-permute-start.7) | collective-permute-done | bytes 3104 | tf_op jit(solution)/shard_map/ppermute | solution.py:332
  67.8 0.6 copy.14
  (12 shorter events, 0.0 us)
Async XLA Ops:
  2.2 10.2 %collective-permute-start.1 = (bf16[272,128]{1,0:T(8,128)(2,1)S(1)}, bf16[272,128]{1,0:T(8,128)(2,1)S(1)}, u32[]{:S(2)}, u32[]{:S(2)}) collective-permute-start(bf16[272,128]{1,0:T(8,128)(2,1)S(1)} %concatenate.9), channel_id=1, source_target_pairs={{0,720},{48,96},{96,48},{144,192},{192,144},{240,288},{288,240},{3... | collective-permute-start | bytes 208904 | tf_op jit(solution)/shard_map/ppermute | solution.py:275
  10.5 5.1 %collective-permute-start = (bf16[272,128]{1,0:T(8,128)(2,1)S(1)}, bf16[272,128]{1,0:T(8,128)(2,1)S(1)}, u32[]{:S(2)}, u32[]{:S(2)}) collective-permute-start(bf16[272,128]{1,0:T(8,128)(2,1)S(1)} %concatenate.9), channel_id=1, source_target_pairs={{0,48},{48,0},{96,144},{144,96},{192,240},{240,192},{288,336},{336... | collective-permute-start | bytes 208904 | tf_op jit(solution)/shard_map/ppermute | solution.py:276
  16.5 22.4 %copy-start = (bf16[816,128]{1,0:T(8,128)(2,1)}, bf16[816,128]{1,0:T(8,128)(2,1)S(1)}, u32[]{:S(2)}) copy-start(bf16[816,128]{1,0:T(8,128)(2,1)S(1)} %concatenate.10.slab_own) | copy-start | bytes 626692
  16.5 22.4 %collective-permute-start.3 = (bf16[816,128]{1,0:T(8,128)(2,1)S(1)}, bf16[816,128]{1,0:T(8,128)(2,1)S(1)}, u32[]{:S(2)}, u32[]{:S(2)}) collective-permute-start(bf16[816,128]{1,0:T(8,128)(2,1)S(1)} %concatenate.10.slab_own), channel_id=1, source_target_pairs={{0,47},{1,2},{2,1},{3,4},{4,3},{5,6},{6,5},{7,8},{8,7},{9,10},{10,... | collective-permute-start | bytes 626696 | tf_op jit(solution)/shard_map/ppermute | solution.py:317
  23.3 15.7 %collective-permute-start.2 = (bf16[816,128]{1,0:T(8,128)(2,1)S(1)}, bf16[816,128]{1,0:T(8,128)(2,1)S(1)}, u32[]{:S(2)}, u32[]{:S(2)}) collective-permute-start(bf16[816,128]{1,0:T(8,128)(2,1)S(1)} %concatenate.10.slab_own), channel_id=1, source_target_pairs={{0,1},{1,0},{2,3},{3,2},{4,5},{5,4},{6,7},{7,6},{8,9},{9,8},{10,11... | collective-permute-start | bytes 626696 | tf_op jit(solution)/shard_map/ppermute | solution.py:318
  38.9 0.7 copy-start.1
  39.0 0.8 %copy-start.2 = (bf16[816,128]{1,0:T(8,128)(2,1)}, bf16[816,128]{1,0:T(8,128)(2,1)S(1)}, u32[]{:S(2)}) copy-start(bf16[816,128]{1,0:T(8,128)(2,1)S(1)} %collective-permute-done.2.slab_in) | copy-start | bytes 626692
  44.4 11.0 %collective-permute-start.4 = (f32[3,768]{1,0:T(4,128)}, f32[3,768]{1,0:T(4,128)S(1)}, u32[]{:S(2)}, u32[]{:S(2)}) collective-permute-start(f32[3,768]{1,0:T(4,128)} %get-tuple-element.30), channel_id=1, source_target_pairs={{0,47},{1,2},{2,1},{3,4},{4,3},{5,6},{6,5},{7,8},{8,7},{9,10},{10,... | collective-permute-start | bytes 27656 | tf_op jit(solution)/shard_map/ppermute | solution.py:328
  46.3 10.1 %collective-permute-start.5 = (f32[3,768]{1,0:T(4,128)}, f32[3,768]{1,0:T(4,128)S(1)}, u32[]{:S(2)}, u32[]{:S(2)}) collective-permute-start(f32[3,768]{1,0:T(4,128)} %get-tuple-element.31), channel_id=1, source_target_pairs={{0,1},{1,0},{2,3},{3,2},{4,5},{5,4},{6,7},{7,6},{8,9},{9,8},{10,11... | collective-permute-start | bytes 27656 | tf_op jit(solution)/shard_map/ppermute | solution.py:329
  57.2 8.3 %collective-permute-start.6 = (f32[3,256]{1,0:T(4,128)S(1)}, f32[3,256]{1,0:T(4,128)S(1)}, u32[]{:S(2)}, u32[]{:S(2)}) collective-permute-start(f32[3,256]{1,0:T(4,128)S(1)} %get-tuple-element.34), channel_id=1, source_target_pairs={{0,720},{48,96},{96,48},{144,192},{192,144},{240,288},{288,240},{3... | collective-permute-start | bytes 9224 | tf_op jit(solution)/shard_map/ppermute | solution.py:331
  63.5 4.4 %collective-permute-start.7 = (f32[3,256]{1,0:T(4,128)S(1)}, f32[3,256]{1,0:T(4,128)S(1)}, u32[]{:S(2)}, u32[]{:S(2)}) collective-permute-start(f32[3,256]{1,0:T(4,128)S(1)} %get-tuple-element.35), channel_id=1, source_target_pairs={{0,48},{48,0},{96,144},{144,96},{192,240},{240,192},{288,336},{336... | collective-permute-start | bytes 9224 | tf_op jit(solution)/shard_map/ppermute | solution.py:332

commit v2 on v1

--- a/solution.py
+++ b/solution.py
@@ -57,6 +57,8 @@
     wr_t,
     wr16,
     read_b,
+    w2_copy,
+    we_copy,
 ):
     atoms = feats.shape[2]
     edges = center.shape[2]
@@ -111,6 +113,8 @@
         axis=0,
     )
 
+    w2_copy[...] = w_second[...]
+    we_copy[...] = w_env[...]
     wn_t[...] = turned(w_neighbor[...]).astype(jnp.bfloat16)
     w2_t[...] = turned(w_second[...]).astype(jnp.bfloat16)
     we_t[...] = turned(w_env[...]).astype(jnp.bfloat16)
@@ -145,9 +149,8 @@
     w_second,
     w_env,
     energy,
-    f_own,
-    f_in,
-    f_out,
+    outer,
+    inner,
 ):
     bf16, f32 = jnp.bfloat16, jnp.float32
     channels, edges = near.shape
@@ -227,14 +230,64 @@
     to_c = mm(lines, hot_c[...])
     to_c = to_c[0:4] + to_c[4:8]
     energy[0] = to_c[3:4]
-    for part, out in enumerate((f_own, f_in, f_out)):
+    parts = []
+    for part in range(3):
         to_nb = mm(lines, hot_nb[:, part * wide : (part + 1) * wide])
         to_nb = -(to_nb[0:3] + to_nb[4:7])
-        if part == 0:
-            out[:, 0:atoms] = to_nb[:, 0:atoms] + to_c[0:3]
-            out[:, atoms:wide] = to_nb[:, atoms:wide]
-        else:
-            out[...] = to_nb
+        parts.append([to_nb[:, k * atoms : (k + 1) * atoms] for k in range(3)])
+    me = 2 * (1 - lax.axis_index("gx") % 2) + 1 - lax.axis_index("gy") % 2
+    outer[me] = jnp.zeros((8, atoms), f32)
+    for toward, first, second in (
+        (1, parts[2][0], parts[2][1]),
+        (2, parts[0][2], parts[1][2]),
+        (3, parts[2][2], jnp.zeros((3, atoms), f32)),
+    ):
+        gap = jnp.zeros((1, atoms), f32)
+        outer[me ^ toward] = jnp.concatenate([first, gap, second, gap], axis=0)
+    for k, mine in enumerate((parts[0][0] + to_c[0:3], parts[1][0], parts[0][1], parts[1][1])):
+        inner[k] = jnp.concatenate([mine, jnp.zeros((1, atoms), f32)], axis=0)
+
+
+def pack(feats, positions, packed, pos, sems):
+    atoms = feats.shape[2]
+    half = atoms // 2
+    move_pos = pltpu.make_async_copy(positions.at[0, 0], pos, sems.at[0])
+    move_feats = pltpu.make_async_copy(feats.at[0, 0], packed.at[0:atoms], sems.at[1])
+    move_pos.start()
+    move_feats.start()
+    move_pos.wait()
+    rows = pos[...].astype(jnp.float32)
+    gap = jnp.zeros((5, half), jnp.float32)
+    packed[atoms : atoms + POS_ROWS] = jnp.concatenate(
+        [rows[:, :half], gap, rows[:, half:], gap], axis=0
+    ).astype(jnp.bfloat16)
+    move_feats.wait()
+
+
+def assemble(own, x_in, x_out, slab):
+    atoms = own.shape[0] - POS_ROWS
+    for k, part in enumerate((own, x_in, x_out)):
+        slab[k * atoms : (k + 1) * atoms] = part[0:atoms]
+        start = 3 * atoms + k * POS_ROWS
+        slab[start : start + POS_ROWS] = part[atoms : atoms + POS_ROWS]
+
+
+def regroup(arrived, inner, sent):
+    far = 2 * (1 - lax.axis_index("gx") % 2) + 1 - lax.axis_index("gy") % 2
+    near = 2 * (lax.axis_index("gx") % 2) + lax.axis_index("gy") % 2
+    from_y = arrived[far ^ 1]
+    from_x = arrived[far ^ 2]
+    from_xy = arrived[far ^ 3]
+    sent[near] = inner[0] + from_y[0:4] + from_x[0:4] + from_xy[0:4]
+    sent[near ^ 1] = inner[1] + from_x[4:8]
+    sent[near ^ 2] = inner[2] + from_y[4:8]
+    sent[near ^ 3] = inner[3]
+
+
+def total(arrived, forces):
+    summed = arrived[0] + arrived[1] + arrived[2] + arrived[3]
+    for k in range(3):
+        forces[0, k] = summed[k : k + 1]
 
 
 def vmem(n):
@@ -248,6 +301,19 @@
 def pair_out(axis):
     count = lax.axis_size(axis)
     return [(i, (i + 1) % count if i % 2 else (i - 1) % count) for i in range(count)]
+
+
+def squares(shift):
+    rows, columns = lax.axis_size("gx"), lax.axis_size("gy")
+    return [
+        [
+            (i + shift + a) % rows * columns + (j + shift + b) % columns
+            for a in range(2)
+            for b in range(2)
+        ]
+        for i in range(0, rows, 2)
+        for j in range(0, columns, 2)
+    ]
 
 
 def body(
@@ -267,16 +333,19 @@
     f32, bf16 = jnp.float32, jnp.bfloat16
     atoms, channels = feats.shape[2:]
     edges = edge_center.shape[2]
-    half = atoms // 2
-    pos = positions[0, 0]
-    gap = jnp.zeros((5, half), bf16)
-    pos_rows = jnp.concatenate([pos[:, :half], gap, pos[:, half:], gap], axis=0)
-    own = jnp.concatenate([feats[0, 0], pos_rows], axis=0)
+    shape = jax.ShapeDtypeStruct
+    own = pl.pallas_call(
+        pack,
+        out_shape=shape((atoms + POS_ROWS, channels), bf16),
+        in_specs=[pl.BlockSpec(memory_space=pl.ANY)] * 2,
+        out_specs=pl.BlockSpec(memory_space=pltpu.VMEM),
+        scratch_shapes=[pltpu.VMEM((3, atoms), bf16), pltpu.SemaphoreType.DMA((2,))],
+        name="pack",
+    )(feats, positions)
     x_out = lax.ppermute(own, "gx", pair_out("gx"))
     x_in = lax.ppermute(own, "gx", pair_in("gx"))
 
-    shape = jax.ShapeDtypeStruct
-    prepared = pl.pallas_call(
+    *prepared, w2_copy, we_copy = pl.pallas_call(
         prepare,
         out_shape=[
             shape((edges, 9 * atoms), bf16),
@@ -290,9 +359,11 @@
             shape((channels, 4 * NBASIS), bf16),
             shape((2 * NBASIS, channels), bf16),
             shape((3, channels, edges), f32),
+            shape((channels, channels), bf16),
+            shape((channels, 3 * channels), bf16),
         ],
         in_specs=vmem(2) + [pl.BlockSpec(memory_space=pltpu.SMEM)] + vmem(9),
-        out_specs=vmem(11),
+        out_specs=vmem(13),
         name="prepare",
         cost_estimate=pl.CostEstimate(flops=100000000, bytes_accessed=3000000, transcendentals=0),
     )(
@@ -310,28 +381,45 @@
         readout,
     )
 
-    slab = jnp.concatenate(
-        [part[:atoms] for part in (own, x_in, x_out)] + [part[atoms:] for part in (own, x_in, x_out)],
-        axis=0,
-    )
+    slab = pl.pallas_call(
+        assemble,
+        out_shape=shape((3 * (atoms + POS_ROWS), channels), bf16),
+        in_specs=vmem(3),
+        out_specs=pl.BlockSpec(memory_space=pltpu.VMEM),
+        name="assemble",
+    )(own, x_in, x_out)
     y_out = lax.ppermute(slab, "gy", pair_out("gy"))
     y_in = lax.ppermute(slab, "gy", pair_in("gy"))
 
-    energy, f_own, f_in, f_out = pl.pallas_call(
+    energy, outer, inner = pl.pallas_call(
         layer,
-        out_shape=[shape((1, 1, edges), f32)] + [shape((3, 3 * atoms), f32)] * 3,
+        out_shape=[
+            shape((1, 1, edges), f32),
+            shape((4, 8, atoms), f32),
+            shape((4, 4, atoms), f32),
+        ],
         in_specs=vmem(16),
-        out_specs=vmem(4),
+        out_specs=vmem(3),
         name="layer",
-    )(slab, y_in, y_out, *prepared, w_second, w_env)
-
-    r_out = lax.ppermute(f_out, "gy", pair_out("gy"))
-    r_in = lax.ppermute(f_in, "gy", pair_in("gy"))
-    column = f_own + r_out + r_in
-    s_out = lax.ppermute(column[:, 2 * atoms :], "gx", pair_out("gx"))
-    s_in = lax.ppermute(column[:, atoms : 2 * atoms], "gx", pair_in("gx"))
-    forces = column[:, :atoms] + s_out + s_in
-    return (energy, forces[None, None])
+    )(slab, y_in, y_out, *prepared, w2_copy, we_copy)
+
+    outer = lax.all_to_all(outer, ("gx", "gy"), 0, 0, axis_index_groups=squares(1))
+    sent = pl.pallas_call(
+        regroup,
+        out_shape=shape((4, 4, atoms), f32),
+        in_specs=vmem(2),
+        out_specs=pl.BlockSpec(memory_space=pltpu.VMEM),
+        name="regroup",
+    )(outer, inner)
+    sent = lax.all_to_all(sent, ("gx", "gy"), 0, 0, axis_index_groups=squares(0))
+    forces = pl.pallas_call(
+        total,
+        out_shape=shape((1, 3, 1, atoms), f32),
+        in_specs=vmem(1),
+        out_specs=pl.BlockSpec(memory_space=pltpu.VMEM),
+        name="total",
+    )(sent)
+    return (energy, jnp.swapaxes(forces, 1, 2))
 
 
 def solution(mesh):

time: 69 us -> 73.2 us (1.061)
  blocking collectives: 0 us -> 24.1 us
  starting transfers between devices: 48.8 us -> 29.6 us
  Pallas kernels: 7.62 us -> 13.4 us
  waiting for transfers between devices: 6.53 us -> 3.34 us
  local copies, waits for them, and re-layouts: 3.94 us -> 1.35 us
    all_to_all x0 -> x2, blocking collectives: none -> 24.1 us  [the longest x1 13.1 us: body(): lax.all_to_all(sent, ('gx', 'gy'), 0, 0, axis_index_groups=squares(0))]
    ppermute x4 -> x0, starting transfers between devices: 19.2 us -> none  [the longest x1 9.09 us: body(): r_in = lax.ppermute(f_in, 'gy', pair_in('gy'))]
    pallas_call x1 -> x5, Pallas kernels: 4.7 us -> 10.4 us  [the longest x1 4.64 us: body(): pl.pallas_call(layer, out_shape=[shape((1, 1, edges), f32), shape((4, 8,...]
    ppermute x4 -> x0, waiting for transfers between devices: 3.44 us -> none  [the longest x1 2.41 us: body(): s_in = lax.ppermute(column[:, atoms:2 * atoms], 'gx', pair_in('gx'))]
    concatenate x2 -> x0, local copies, waits for them, and re-layouts: 1.88 us -> none  [the longest x1 0.97 us: body(): jnp.concatenate([part[:atoms] for part in (own, x_in, x_out)] + [part[ato...]
  transfers between devices with their start and end apart: 8 -> 4, of which waited for: 3 -> 1; matrix products, arithmetic and copies ran while one was open for 0% -> 0% of each run, Pallas kernels for 4% -> 4%
where the time goes in v2:
time: 73.2 us; the launch traced here: 72.5 us
  starting transfers between devices  29.6 us (40%)
  blocking collectives  24.1 us (33%)
  Pallas kernels  13.4 us (18%)
  waiting for transfers between devices  3.34 us (5%)
  local copies, waits for them, and re-layouts  1.35 us (2%)
    all_to_all x1, blocking collectives, body(): lax.all_to_all(sent, ('gx', 'gy'), 0, 0, axis_index_groups=squares(0))  13.1 us
    ppermute x1, starting transfers between devices, body(): y_in = lax.ppermute(slab, 'gy', pair_in('gy'))  12.7 us
    all_to_all x1, blocking collectives, body(): lax.all_to_all(outer, ('gx', 'gy'), 0, 0, axis_index_groups=squares(1))  11 us
    ppermute x1, starting transfers between devices, body(): x_out = lax.ppermute(own, 'gx', pair_out('gx'))  8.25 us
    ppermute x1, starting transfers between devices, body(): y_out = lax.ppermute(slab, 'gy', pair_out('gy'))  6.73 us
    pallas_call x1, Pallas kernels, body(): pl.pallas_call(layer, out_shape=[shape((1, 1, edges), f32), shape((4, 8,...  4.64 us
    ppermute x1, waiting for transfers between devices, body(): x_in = lax.ppermute(own, 'gx', pair_in('gx'))  3.32 us
    pallas_call x1, Pallas kernels, body(): pl.pallas_call(prepare, out_shape=[shape((edges, 9 * atoms), bf16), shape...  2.97 us
  transfers between devices with their start and end apart: 4, of which 1 were waited for; matrix products, arithmetic and copies ran while one was open for 0% of the time, Pallas kernels for 4%

profile of v2, /device:TPU:1, one launch (start us, length us, event | category | flops | bytes accessed | tf_op | source)
XLA Modules:
  0.0 72.5 jit_solution(6571540807392342916)
XLA Ops:
  0.6 1.5 %pack.1.own = bf16[272,128]{1,0:T(8,128)(2,1)} custom-call(bf16[1,1,256,128]{3,2,1,0:T(8,128)(2,1)} %feats.3, bf16[1,1,3,256]{3,2,1,0:T(4,128)(2,1)} %positions.3), custom_call_target="tpu_custom_call" | custom-call | tf_op jit(solution)/shard_map/pack/pallas_call | solution.py:337
  2.1 8.3 %collective-permute-start.1 = (bf16[272,128]{1,0:T(8,128)(2,1)}, bf16[272,128]{1,0:T(8,128)(2,1)S(1)}, u32[]{:S(2)}, u32[]{:S(2)}) collective-permute-start(bf16[272,128]{1,0:T(8,128)(2,1)} %pack.1.own), channel_id=1, source_target_pairs={{0,720},{48,96},{96,48},{144,192},{192,144},{240,288},{288,240},{3... | collective-permute-start | bytes 208904 | tf_op jit(solution)/shard_map/ppermute | solution.py:345
  10.4 1.9 %collective-permute-start = (bf16[272,128]{1,0:T(8,128)(2,1)}, bf16[272,128]{1,0:T(8,128)(2,1)S(1)}, u32[]{:S(2)}, u32[]{:S(2)}) collective-permute-start(bf16[272,128]{1,0:T(8,128)(2,1)} %pack.1.own), channel_id=1, source_target_pairs={{0,48},{48,0},{96,144},{144,96},{192,240},{240,192},{288,336},{336... | collective-permute-start | bytes 208904 | tf_op jit(solution)/shard_map/ppermute | solution.py:346
  12.3 0.0 collective-permute-done.1.x_out
  12.3 0.0 copy-start.2
  12.3 3.3 %collective-permute-done.x_in = bf16[272,128]{1,0:T(8,128)(2,1)S(1)} collective-permute-done((bf16[272,128]{1,0:T(8,128)(2,1)}, bf16[272,128]{1,0:T(8,128)(2,1)S(1)}, u32[]{:S(2)}, u32[]{:S(2)}) %collective-permute-start) | collective-permute-done | bytes 69664 | tf_op jit(solution)/shard_map/ppermute | solution.py:346
  15.7 0.0 copy-done.2
  15.7 0.0 copy-start.3
  15.7 0.6 copy-done.3
  16.3 1.6 %assemble.1.slab_own = bf16[816,128]{1,0:T(8,128)(2,1)} custom-call(bf16[272,128]{1,0:T(8,128)(2,1)} %pack.1.own, bf16[272,128]{1,0:T(8,128)(2,1)} %copy-done.3, bf16[272,128]{1,0:T(8,128)(2,1)} %copy-done.2), custom_call_target="tpu_custom_call" | custom-call | tf_op jit(solution)/shard_map/assemble/pallas_call | solution.py:384
  17.9 6.7 %collective-permute-start.3 = (bf16[816,128]{1,0:T(8,128)(2,1)}, bf16[816,128]{1,0:T(8,128)(2,1)S(1)}, u32[]{:S(2)}, u32[]{:S(2)}) collective-permute-start(bf16[816,128]{1,0:T(8,128)(2,1)} %assemble.1.slab_own), channel_id=1, source_target_pairs={{0,47},{1,2},{2,1},{3,4},{4,3},{5,6},{6,5},{7,8},{8,7},{9,10},{10,... | collective-permute-start | bytes 626696 | tf_op jit(solution)/shard_map/ppermute | solution.py:391
  24.7 12.7 %collective-permute-start.2 = (bf16[816,128]{1,0:T(8,128)(2,1)}, bf16[816,128]{1,0:T(8,128)(2,1)S(1)}, u32[]{:S(2)}, u32[]{:S(2)}) collective-permute-start(bf16[816,128]{1,0:T(8,128)(2,1)} %assemble.1.slab_own), channel_id=1, source_target_pairs={{0,1},{1,0},{2,3},{3,2},{4,5},{5,4},{6,7},{7,6},{8,9},{9,8},{10,11... | collective-permute-start | bytes 626696 | tf_op jit(solution)/shard_map/ppermute | solution.py:392
  37.4 3.0 %prepare.1 = (bf16[256,2304]{1,0:T(8,128)(2,1)}, bf16[256,256]{1,0:T(8,128)(2,1)}, bf16[256,256]{1,0:T(8,128)(2,1)}, f32[128,256]{1,0:T(8,128)}, f32[16,256]{1,0...) custom-call(bf16[1,1,256,128]{3,2,1,0:T(8,128)(2,1)} %feats.3, ...), custom_call_target="tpu_custom_call" | custom-call | flops 100000000 | bytes 3000000 | tf_op jit(solution)/shard_map/prepare/pallas_call | solution.py:348
  40.4 0.0 collective-permute-done.3.slab_out
  40.4 0.0 copy-start
  40.4 0.0 collective-permute-done.2.slab_in
  40.4 0.0 copy-start.1
  40.4 0.7 copy-done
  41.1 0.1 copy-done.1
  41.1 4.6 %layer.1 = (f32[1,1,256]{2,1,0:T(1,128)}, f32[4,8,256]{2,1,0:T(8,128)}, f32[4,4,256]{2,1,0:T(4,128)}) custom-call(bf16[816,128]{1,0:T(8,128)(2,1)} %assemble.1.slab_own, bf16[816,128]{1,0:T(8,128)(2,1)} %copy-done.1, bf16[816,128]{1,0:T(8,128)(2,1)} %copy-done, bf16[256,2304]{1,0:T(8,128)(2,1)} %get-tuple-element.18.hot_nb, ...), custom_call_target="tpu_custom_call" | custom-call | tf_op jit(solution)/shard_map/layer/pallas_call | solution.py:394
  45.8 11.0 %all_to_all.10.arrived = f32[4,8,256]{2,1,0:T(8,128)} all-to-all(f32[4,8,256]{2,1,0:T(8,128)} %get-tuple-element.32), channel_id=1, replica_groups={{49,50,97,98},{51,52,99,100},{53,54,101,102},{55,56,103,104},{57,58,105..., dimensions={0} | all-to-all | bytes 65536 | tf_op jit(solution)/shard_map/all_to_all | solution.py:406
  56.7 1.4 %regroup.1 = f32[4,4,256]{2,1,0:T(4,128)} custom-call(f32[4,8,256]{2,1,0:T(8,128)} %all_to_all.10.arrived, f32[4,4,256]{2,1,0:T(4,128)} %get-tuple-element.33.inner), custom_call_target="tpu_custom_call" | custom-call | tf_op jit(solution)/shard_map/regroup/pallas_call | solution.py:407
  58.1 13.1 %all_to_all.11.arrived = f32[4,4,256]{2,1,0:T(4,128)} all-to-all(f32[4,4,256]{2,1,0:T(4,128)} %regroup.1), channel_id=1, replica_groups={{0,1,48,49},{2,3,50,51},{4,5,52,53},{6,7,54,55},{8,9,56,57},{10,11,58,5..., dimensions={0} | all-to-all | bytes 32768 | tf_op jit(solution)/shard_map/all_to_all | solution.py:414
  71.2 1.3 %total.1 = f32[1,3,1,256]{3,2,1,0:T(1,128)} custom-call(f32[4,4,256]{2,1,0:T(4,128)} %all_to_all.11.arrived), custom_call_target="tpu_custom_call" | custom-call | tf_op jit(solution)/shard_map/total/pallas_call | solution.py:415
Async XLA Ops:
  2.1 10.2 %collective-permute-start.1 = (bf16[272,128]{1,0:T(8,128)(2,1)}, bf16[272,128]{1,0:T(8,128)(2,1)S(1)}, u32[]{:S(2)}, u32[]{:S(2)}) collective-permute-start(bf16[272,128]{1,0:T(8,128)(2,1)} %pack.1.own), channel_id=1, source_target_pairs={{0,720},{48,96},{96,48},{144,192},{192,144},{240,288},{288,240},{3... | collective-permute-start | bytes 208904 | tf_op jit(solution)/shard_map/ppermute | solution.py:345
  10.4 5.3 %collective-permute-start = (bf16[272,128]{1,0:T(8,128)(2,1)}, bf16[272,128]{1,0:T(8,128)(2,1)S(1)}, u32[]{:S(2)}, u32[]{:S(2)}) collective-permute-start(bf16[272,128]{1,0:T(8,128)(2,1)} %pack.1.own), channel_id=1, source_target_pairs={{0,48},{48,0},{96,144},{144,96},{192,240},{240,192},{288,336},{336... | collective-permute-start | bytes 208904 | tf_op jit(solution)/shard_map/ppermute | solution.py:346
  12.3 3.3 %copy-start.2 = (bf16[272,128]{1,0:T(8,128)(2,1)}, bf16[272,128]{1,0:T(8,128)(2,1)S(1)}, u32[]{:S(2)}) copy-start(bf16[272,128]{1,0:T(8,128)(2,1)S(1)} %collective-permute-done.1.x_out) | copy-start | bytes 208900
  15.7 0.6 copy-start.3
  17.9 22.4 %collective-permute-start.3 = (bf16[816,128]{1,0:T(8,128)(2,1)}, bf16[816,128]{1,0:T(8,128)(2,1)S(1)}, u32[]{:S(2)}, u32[]{:S(2)}) collective-permute-start(bf16[816,128]{1,0:T(8,128)(2,1)} %assemble.1.slab_own), channel_id=1, source_target_pairs={{0,47},{1,2},{2,1},{3,4},{4,3},{5,6},{6,5},{7,8},{8,7},{9,10},{10,... | collective-permute-start | bytes 626696 | tf_op jit(solution)/shard_map/ppermute | solution.py:391
  24.7 15.7 %collective-permute-start.2 = (bf16[816,128]{1,0:T(8,128)(2,1)}, bf16[816,128]{1,0:T(8,128)(2,1)S(1)}, u32[]{:S(2)}, u32[]{:S(2)}) collective-permute-start(bf16[816,128]{1,0:T(8,128)(2,1)} %assemble.1.slab_own), channel_id=1, source_target_pairs={{0,1},{1,0},{2,3},{3,2},{4,5},{5,4},{6,7},{7,6},{8,9},{9,8},{10,11... | collective-permute-start | bytes 626696 | tf_op jit(solution)/shard_map/ppermute | solution.py:392
  40.4 0.7 copy-start
  40.4 0.7 %copy-start.1 = (bf16[816,128]{1,0:T(8,128)(2,1)}, bf16[816,128]{1,0:T(8,128)(2,1)S(1)}, u32[]{:S(2)}) copy-start(bf16[816,128]{1,0:T(8,128)(2,1)S(1)} %collective-permute-done.2.slab_in) | copy-start | bytes 626692

commit v3 on v1

--- a/solution.py
+++ b/solution.py
@@ -57,6 +57,8 @@
     wr_t,
     wr16,
     read_b,
+    w2_copy,
+    we_copy,
 ):
     atoms = feats.shape[2]
     edges = center.shape[2]
@@ -111,6 +113,8 @@
         axis=0,
     )
 
+    w2_copy[...] = w_second[...]
+    we_copy[...] = w_env[...]
     wn_t[...] = turned(w_neighbor[...]).astype(jnp.bfloat16)
     w2_t[...] = turned(w_second[...]).astype(jnp.bfloat16)
     we_t[...] = turned(w_env[...]).astype(jnp.bfloat16)
@@ -237,6 +241,34 @@
             out[...] = to_nb
 
 
+def pack(feats, positions, packed, pos, sems):
+    atoms = feats.shape[2]
+    half = atoms // 2
+    move_pos = pltpu.make_async_copy(positions.at[0, 0], pos, sems.at[0])
+    move_feats = pltpu.make_async_copy(feats.at[0, 0], packed.at[0:atoms], sems.at[1])
+    move_pos.start()
+    move_feats.start()
+    move_pos.wait()
+    rows = pos[...].astype(jnp.float32)
+    gap = jnp.zeros((5, half), jnp.float32)
+    packed[atoms : atoms + POS_ROWS] = jnp.concatenate(
+        [rows[:, :half], gap, rows[:, half:], gap], axis=0
+    ).astype(jnp.bfloat16)
+    move_feats.wait()
+
+
+def assemble(own, x_in, x_out, slab):
+    atoms = own.shape[0] - POS_ROWS
+    for k, part in enumerate((own, x_in, x_out)):
+        slab[k * atoms : (k + 1) * atoms] = part[0:atoms]
+        start = 3 * atoms + k * POS_ROWS
+        slab[start : start + POS_ROWS] = part[atoms : atoms + POS_ROWS]
+
+
+def grant(mib):
+    return pltpu.CompilerParams(vmem_limit_bytes=mib << 20)
+
+
 def vmem(n):
     return [pl.BlockSpec(memory_space=pltpu.VMEM)] * n
 
@@ -267,16 +299,20 @@
     f32, bf16 = jnp.float32, jnp.bfloat16
     atoms, channels = feats.shape[2:]
     edges = edge_center.shape[2]
-    half = atoms // 2
-    pos = positions[0, 0]
-    gap = jnp.zeros((5, half), bf16)
-    pos_rows = jnp.concatenate([pos[:, :half], gap, pos[:, half:], gap], axis=0)
-    own = jnp.concatenate([feats[0, 0], pos_rows], axis=0)
+    shape = jax.ShapeDtypeStruct
+    own = pl.pallas_call(
+        pack,
+        out_shape=shape((atoms + POS_ROWS, channels), bf16),
+        in_specs=[pl.BlockSpec(memory_space=pl.ANY)] * 2,
+        out_specs=pl.BlockSpec(memory_space=pltpu.VMEM),
+        scratch_shapes=[pltpu.VMEM((3, atoms), bf16), pltpu.SemaphoreType.DMA((2,))],
+        name="pack",
+        compiler_params=grant(2),
+    )(feats, positions)
     x_out = lax.ppermute(own, "gx", pair_out("gx"))
     x_in = lax.ppermute(own, "gx", pair_in("gx"))
 
-    shape = jax.ShapeDtypeStruct
-    prepared = pl.pallas_call(
+    *prepared, w2_copy, we_copy = pl.pallas_call(
         prepare,
         out_shape=[
             shape((edges, 9 * atoms), bf16),
@@ -290,10 +326,13 @@
             shape((channels, 4 * NBASIS), bf16),
             shape((2 * NBASIS, channels), bf16),
             shape((3, channels, edges), f32),
+            shape((channels, channels), bf16),
+            shape((channels, 3 * channels), bf16),
         ],
         in_specs=vmem(2) + [pl.BlockSpec(memory_space=pltpu.SMEM)] + vmem(9),
-        out_specs=vmem(11),
+        out_specs=vmem(13),
         name="prepare",
+        compiler_params=grant(8),
         cost_estimate=pl.CostEstimate(flops=100000000, bytes_accessed=3000000, transcendentals=0),
     )(
         feats,
@@ -310,10 +349,14 @@
         readout,
     )
 
-    slab = jnp.concatenate(
-        [part[:atoms] for part in (own, x_in, x_out)] + [part[atoms:] for part in (own, x_in, x_out)],
-        axis=0,
-    )
+    slab = pl.pallas_call(
+        assemble,
+        out_shape=shape((3 * (atoms + POS_ROWS), channels), bf16),
+        in_specs=vmem(3),
+        out_specs=pl.BlockSpec(memory_space=pltpu.VMEM),
+        name="assemble",
+        compiler_params=grant(2),
+    )(own, x_in, x_out)
     y_out = lax.ppermute(slab, "gy", pair_out("gy"))
     y_in = lax.ppermute(slab, "gy", pair_in("gy"))
 
@@ -323,7 +366,8 @@
         in_specs=vmem(16),
         out_specs=vmem(4),
         name="layer",
-    )(slab, y_in, y_out, *prepared, w_second, w_env)
+        compiler_params=grant(8),
+    )(slab, y_in, y_out, *prepared, w2_copy, we_copy)
 
     r_out = lax.ppermute(f_out, "gy", pair_out("gy"))
     r_in = lax.ppermute(f_in, "gy", pair_in("gy"))

time: 69 us -> 70.6 us (1.023)
  local copies, waits for them, and re-layouts: 3.94 us -> 10.9 us
  Pallas kernels: 7.62 us -> 4.26 us
  starting transfers between devices: 48.8 us -> 45.9 us
  waiting for transfers between devices: 6.53 us -> 8.01 us
  other arithmetic: 0.72 us -> 0.01 us
    unnamed x7 -> x29, local copies, waits for them, and re-layouts: 1.33 us -> 10.9 us
    ppermute x1, starting transfers between devices: 9.09 us -> 4.52 us  [body(): r_in = lax.ppermute(f_in, 'gy', pair_in('gy'))]
    ppermute x1, waiting for transfers between devices: 0.01 us -> 2.47 us  [body(): r_out = lax.ppermute(f_out, 'gy', pair_out('gy'))]
    pallas_call x1, Pallas kernels: 4.7 us -> 2.68 us  [body(): pl.pallas_call(layer, out_shape=[shape((1, 1, edges), f32)] + [shape((3,...]
    concatenate x2 -> x0, local copies, waits for them, and re-layouts: 1.88 us -> none  [the longest x1 0.97 us: body(): jnp.concatenate([part[:atoms] for part in (own, x_in, x_out)] + [part[ato...]
    ppermute x1, starting transfers between devices: 6.31 us -> 7.86 us  [body(): s_out = lax.ppermute(column[:, 2 * atoms:], 'gx', pair_out('gx'))]
    pallas_call x1, Pallas kernels: 2.92 us -> 1.48 us  [body(): pl.pallas_call(prepare, out_shape=[shape((edges, 9 * atoms), bf16), shape...]
    ppermute x1, waiting for transfers between devices: 1.01 us -> 0.01 us  [body(): r_in = lax.ppermute(f_in, 'gy', pair_in('gy'))]
  transfers between devices with their start and end apart: 8 -> 8, of which waited for: 3 -> 3; matrix products, arithmetic and copies ran while one was open for 0% -> 0% of each run, Pallas kernels for 4% -> 2%
where the time goes in v3:
time: 70.6 us; the launch traced here: 69.8 us
  starting transfers between devices  45.9 us (65%)
  local copies, waits for them, and re-layouts  10.9 us (15%)
  waiting for transfers between devices  8.01 us (11%)
  Pallas kernels  4.26 us (6%)
  between operations  0.78 us (1%)
    ppermute x1, starting transfers between devices, body(): y_in = lax.ppermute(slab, 'gy', pair_in('gy'))  12.7 us
    unnamed x29, local copies, waits for them, and re-layouts  10.9 us
    ppermute x1, starting transfers between devices, body(): x_out = lax.ppermute(own, 'gx', pair_out('gx'))  8.25 us
    ppermute x1, starting transfers between devices, body(): s_out = lax.ppermute(column[:, 2 * atoms:], 'gx', pair_out('gx'))  7.86 us
    ppermute x1, starting transfers between devices, body(): y_out = lax.ppermute(slab, 'gy', pair_out('gy'))  6.75 us
    ppermute x1, starting transfers between devices, body(): r_in = lax.ppermute(f_in, 'gy', pair_in('gy'))  4.52 us
    ppermute x1, waiting for transfers between devices, body(): x_in = lax.ppermute(own, 'gx', pair_in('gx'))  3.11 us
    pallas_call x1, Pallas kernels, body(): pl.pallas_call(layer, out_shape=[shape((1, 1, edges), f32)] + [shape((3,...  2.68 us
  transfers between devices with their start and end apart: 8, of which 3 were waited for; matrix products, arithmetic and copies ran while one was open for 0% of the time, Pallas kernels for 2%

profile of v3, /device:TPU:1, one launch (start us, length us, event | category | flops | bytes accessed | tf_op | source)
XLA Modules:
  0.0 69.8 jit_solution(17416384354869998055)
XLA Ops:
  0.6 0.8 %copy-done = bf16[1,1,256,128]{3,2,1,0:T(8,128)(2,1)S(1)} copy-done((bf16[1,1,256,128]{3,2,1,0:T(8,128)(2,1)S(1)}, bf16[1,1,256,128]{3,2,1,0:T(8,128)(2,1)}, u32[]{:S(2)}) %copy-start) | copy-done | bytes 65560
  1.5 0.7 copy-done.2
  2.2 8.3 %collective-permute-start.1 = (bf16[272,128]{1,0:T(8,128)(2,1)S(1)}, bf16[272,128]{1,0:T(8,128)(2,1)S(1)}, u32[]{:S(2)}, u32[]{:S(2)}) collective-permute-start(bf16[272,128]{1,0:T(8,128)(2,1)S(1)} %pack.1.own), channel_id=1, source_target_pairs={{0,720},{48,96},{96,48},{144,192},{192,144},{240,288},{288,240},{3... | collective-permute-start | bytes 208904 | tf_op jit(solution)/shard_map/ppermute | solution.py:312
  10.5 1.9 %collective-permute-start = (bf16[272,128]{1,0:T(8,128)(2,1)S(1)}, bf16[272,128]{1,0:T(8,128)(2,1)S(1)}, u32[]{:S(2)}, u32[]{:S(2)}) collective-permute-start(bf16[272,128]{1,0:T(8,128)(2,1)S(1)} %pack.1.own), channel_id=1, source_target_pairs={{0,48},{48,0},{96,144},{144,96},{192,240},{240,192},{288,336},{336... | collective-permute-start | bytes 208904 | tf_op jit(solution)/shard_map/ppermute | solution.py:313
  12.4 3.1 %collective-permute-done.x_in = bf16[272,128]{1,0:T(8,128)(2,1)S(1)} collective-permute-done((bf16[272,128]{1,0:T(8,128)(2,1)S(1)}, bf16[272,128]{1,0:T(8,128)(2,1)S(1)}, u32[]{:S(2)}, u32[]{:S(2)}) %collective-permute-start) | collective-permute-done | bytes 69664 | tf_op jit(solution)/shard_map/ppermute | solution.py:313
  15.6 6.7 %collective-permute-start.3 = (bf16[816,128]{1,0:T(8,128)(2,1)S(1)}, bf16[816,128]{1,0:T(8,128)(2,1)S(1)}, u32[]{:S(2)}, u32[]{:S(2)}) collective-permute-start(bf16[816,128]{1,0:T(8,128)(2,1)S(1)} %assemble.1.slab_own), channel_id=1, source_target_pairs={{0,47},{1,2},{2,1},{3,4},{4,3},{5,6},{6,5},{7,8},{8,7},{9,10},{10,... | collective-permute-start | bytes 626696 | tf_op jit(solution)/shard_map/ppermute | solution.py:360
  22.3 12.7 %collective-permute-start.2 = (bf16[816,128]{1,0:T(8,128)(2,1)S(1)}, bf16[816,128]{1,0:T(8,128)(2,1)S(1)}, u32[]{:S(2)}, u32[]{:S(2)}) collective-permute-start(bf16[816,128]{1,0:T(8,128)(2,1)S(1)} %assemble.1.slab_own), channel_id=1, source_target_pairs={{0,1},{1,0},{2,3},{3,2},{4,5},{5,4},{6,7},{7,6},{8,9},{9,8},{10,11... | collective-permute-start | bytes 626696 | tf_op jit(solution)/shard_map/ppermute | solution.py:361
  35.1 0.8 %copy-done.1 = bf16[1,1,256,128]{3,2,1,0:T(8,128)(2,1)S(1)} copy-done((bf16[1,1,256,128]{3,2,1,0:T(8,128)(2,1)S(1)}, bf16[1,1,256,128]{3,2,1,0:T(8,128)(2,1)}, u32[]{:S(2)}) %copy-start.1) | copy-done | bytes 65560
  35.9 0.7 copy-done.3
  36.6 0.9 %copy-done.4 = bf16[128,384]{1,0:T(8,128)(2,1)S(1)} copy-done((bf16[128,384]{1,0:T(8,128)(2,1)S(1)}, bf16[128,384]{1,0:T(8,128)(2,1)}, u32[]{:S(2)}) %copy-start.4) | copy-done | bytes 98328
  37.5 0.8 %copy-done.5 = bf16[128,128]{1,0:T(8,128)(2,1)S(1)} copy-done((bf16[128,128]{1,0:T(8,128)(2,1)S(1)}, bf16[128,128]{1,0:T(8,128)(2,1)}, u32[]{:S(2)}) %copy-start.5) | copy-done | bytes 32792
  38.2 0.8 %copy-done.6 = bf16[128,128]{1,0:T(8,128)(2,1)S(1)} copy-done((bf16[128,128]{1,0:T(8,128)(2,1)S(1)}, bf16[128,128]{1,0:T(8,128)(2,1)}, u32[]{:S(2)}) %copy-start.6) | copy-done | bytes 32792
  39.0 0.8 %copy-done.7 = bf16[128,128]{1,0:T(8,128)(2,1)S(1)} copy-done((bf16[128,128]{1,0:T(8,128)(2,1)S(1)}, bf16[128,128]{1,0:T(8,128)(2,1)}, u32[]{:S(2)}) %copy-start.7) | copy-done | bytes 32792
  39.8 0.7 copy-done.8
  40.5 0.7 copy-done.9
  41.1 0.7 copy-done.10
  43.9 1.5 %prepare.1 = (bf16[256,2304]{1,0:T(8,128)(2,1)S(1)}, bf16[256,256]{1,0:T(8,128)(2,1)S(1)}, bf16[256,256]{1,0:T(8,128)(2,1)S(1)}, f32[128,256]{1,0:T(8,128)S(1)},...) custom-call(bf16[1,1,256,128]{3,2,1,0:T(8,128)(2,1)S(1)} %copy-done., ...), custom_call_target="tpu_custom_call" | custom-call | flops 100000000 | bytes 3000000 | tf_op jit(solution)/shard_map/prepare/pallas_call | solution.py:315
  45.4 2.7 %layer.1 = (f32[1,1,256]{2,1,0:T(1,128)}, f32[3,768]{1,0:T(4,128)S(1)}, f32[3,768]{1,0:T(4,128)S(1)}, f32[3,768]{1,0:T(4,128)S(1)}) custom-call(bf16[816,128]{1,0:T(8,128)(2,1)S(1)} %assemble.1.slab_own, bf16[816,128]{1,0:T(8,128)(2,1)S(1)} %collective-permute-done.2.slab_in, bf16[816,128]{1,0:T(8,128)(2,1)S(1)} %collective-permute-done.3.slab_out, ...), custom_call_target="tpu_custom_call" | custom-call | tf_op jit(solution)/shard_map/layer/pallas_call | solution.py:363
  48.0 1.9 %collective-permute-start.4 = (f32[3,768]{1,0:T(4,128)S(1)}, f32[3,768]{1,0:T(4,128)S(1)}, u32[]{:S(2)}, u32[]{:S(2)}) collective-permute-start(f32[3,768]{1,0:T(4,128)S(1)} %get-tuple-element.34), channel_id=1, source_target_pairs={{0,47},{1,2},{2,1},{3,4},{4,3},{5,6},{6,5},{7,8},{8,7},{9,10},{10,... | collective-permute-start | bytes 27656 | tf_op jit(solution)/shard_map/ppermute | solution.py:372
  50.0 4.5 %collective-permute-start.5 = (f32[3,768]{1,0:T(4,128)S(1)}, f32[3,768]{1,0:T(4,128)S(1)}, u32[]{:S(2)}, u32[]{:S(2)}) collective-permute-start(f32[3,768]{1,0:T(4,128)S(1)} %get-tuple-element.35), channel_id=1, source_target_pairs={{0,1},{1,0},{2,3},{3,2},{4,5},{5,4},{6,7},{7,6},{8,9},{9,8},{10,11... | collective-permute-start | bytes 27656 | tf_op jit(solution)/shard_map/ppermute | solution.py:373
  54.5 2.5 %collective-permute-done.4 = f32[3,768]{1,0:T(4,128)S(1)} collective-permute-done((f32[3,768]{1,0:T(4,128)S(1)}, f32[3,768]{1,0:T(4,128)S(1)}, u32[]{:S(2)}, u32[]{:S(2)}) %collective-permute-start.4) | collective-permute-done | bytes 9248 | tf_op jit(solution)/shard_map/ppermute | solution.py:372
  57.0 7.9 %collective-permute-start.6 = (f32[3,256]{1,0:T(4,128)S(1)}, f32[3,256]{1,0:T(4,128)S(1)}, u32[]{:S(2)}, u32[]{:S(2)}) collective-permute-start(f32[3,256]{1,0:T(4,128)S(1)} %get-tuple-element.38), channel_id=1, source_target_pairs={{0,720},{48,96},{96,48},{144,192},{192,144},{240,288},{288,240},{3... | collective-permute-start | bytes 9224 | tf_op jit(solution)/shard_map/ppermute | solution.py:375
  64.9 1.9 %collective-permute-start.7 = (f32[3,256]{1,0:T(4,128)S(1)}, f32[3,256]{1,0:T(4,128)S(1)}, u32[]{:S(2)}, u32[]{:S(2)}) collective-permute-start(f32[3,256]{1,0:T(4,128)S(1)} %get-tuple-element.39), channel_id=1, source_target_pairs={{0,48},{48,0},{96,144},{144,96},{192,240},{240,192},{288,336},{336... | collective-permute-start | bytes 9224 | tf_op jit(solution)/shard_map/ppermute | solution.py:376
  66.8 2.4 %collective-permute-done.7 = f32[3,256]{1,0:T(4,128)S(1)} collective-permute-done((f32[3,256]{1,0:T(4,128)S(1)}, f32[3,256]{1,0:T(4,128)S(1)}, u32[]{:S(2)}, u32[]{:S(2)}) %collective-permute-start.7) | collective-permute-done | bytes 3104 | tf_op jit(solution)/shard_map/ppermute | solution.py:376
  (28 shorter events, 2.8 us)
Async XLA Ops:
  0.6 0.8 %copy-start = (bf16[1,1,256,128]{3,2,1,0:T(8,128)(2,1)S(1)}, bf16[1,1,256,128]{3,2,1,0:T(8,128)(2,1)}, u32[]{:S(2)}) copy-start(bf16[1,1,256,128]{3,2,1,0:T(8,128)(2,1)} %feats.3) | copy-start | bytes 196612
  1.5 0.7 copy-start.2
  2.2 10.2 %collective-permute-start.1 = (bf16[272,128]{1,0:T(8,128)(2,1)S(1)}, bf16[272,128]{1,0:T(8,128)(2,1)S(1)}, u32[]{:S(2)}, u32[]{:S(2)}) collective-permute-start(bf16[272,128]{1,0:T(8,128)(2,1)S(1)} %pack.1.own), channel_id=1, source_target_pairs={{0,720},{48,96},{96,48},{144,192},{192,144},{240,288},{288,240},{3... | collective-permute-start | bytes 208904 | tf_op jit(solution)/shard_map/ppermute | solution.py:312
  10.5 5.1 %collective-permute-start = (bf16[272,128]{1,0:T(8,128)(2,1)S(1)}, bf16[272,128]{1,0:T(8,128)(2,1)S(1)}, u32[]{:S(2)}, u32[]{:S(2)}) collective-permute-start(bf16[272,128]{1,0:T(8,128)(2,1)S(1)} %pack.1.own), channel_id=1, source_target_pairs={{0,48},{48,0},{96,144},{144,96},{192,240},{240,192},{288,336},{336... | collective-permute-start | bytes 208904 | tf_op jit(solution)/shard_map/ppermute | solution.py:313
  15.6 29.8 %collective-permute-start.3 = (bf16[816,128]{1,0:T(8,128)(2,1)S(1)}, bf16[816,128]{1,0:T(8,128)(2,1)S(1)}, u32[]{:S(2)}, u32[]{:S(2)}) collective-permute-start(bf16[816,128]{1,0:T(8,128)(2,1)S(1)} %assemble.1.slab_own), channel_id=1, source_target_pairs={{0,47},{1,2},{2,1},{3,4},{4,3},{5,6},{6,5},{7,8},{8,7},{9,10},{10,... | collective-permute-start | bytes 626696 | tf_op jit(solution)/shard_map/ppermute | solution.py:360
  22.3 23.0 %collective-permute-start.2 = (bf16[816,128]{1,0:T(8,128)(2,1)S(1)}, bf16[816,128]{1,0:T(8,128)(2,1)S(1)}, u32[]{:S(2)}, u32[]{:S(2)}) collective-permute-start(bf16[816,128]{1,0:T(8,128)(2,1)S(1)} %assemble.1.slab_own), channel_id=1, source_target_pairs={{0,1},{1,0},{2,3},{3,2},{4,5},{5,4},{6,7},{7,6},{8,9},{9,8},{10,11... | collective-permute-start | bytes 626696 | tf_op jit(solution)/shard_map/ppermute | solution.py:361
  35.1 0.8 %copy-start.1 = (bf16[1,1,256,128]{3,2,1,0:T(8,128)(2,1)S(1)}, bf16[1,1,256,128]{3,2,1,0:T(8,128)(2,1)}, u32[]{:S(2)}) copy-start(bf16[1,1,256,128]{3,2,1,0:T(8,128)(2,1)} %feats.3) | copy-start | bytes 196612
  35.9 0.7 copy-start.3
  36.6 0.9 %copy-start.4 = (bf16[128,384]{1,0:T(8,128)(2,1)S(1)}, bf16[128,384]{1,0:T(8,128)(2,1)}, u32[]{:S(2)}) copy-start(bf16[128,384]{1,0:T(8,128)(2,1)} %w_env.1) | copy-start | bytes 294916
  37.5 0.8 %copy-start.5 = (bf16[128,128]{1,0:T(8,128)(2,1)S(1)}, bf16[128,128]{1,0:T(8,128)(2,1)}, u32[]{:S(2)}) copy-start(bf16[128,128]{1,0:T(8,128)(2,1)} %w_center.1) | copy-start | bytes 98308
  38.2 0.8 %copy-start.6 = (bf16[128,128]{1,0:T(8,128)(2,1)S(1)}, bf16[128,128]{1,0:T(8,128)(2,1)}, u32[]{:S(2)}) copy-start(bf16[128,128]{1,0:T(8,128)(2,1)} %w_neighbor.1) | copy-start | bytes 98308
  39.0 0.8 %copy-start.7 = (bf16[128,128]{1,0:T(8,128)(2,1)S(1)}, bf16[128,128]{1,0:T(8,128)(2,1)}, u32[]{:S(2)}) copy-start(bf16[128,128]{1,0:T(8,128)(2,1)} %w_second.1) | copy-start | bytes 98308
  39.8 0.7 copy-start.8
  40.5 0.7 copy-start.9
  41.1 0.7 copy-start.10
  41.8 0.7 copy-start.11
  42.5 0.7 copy-start.12
  43.2 0.7 copy-start.13
  48.0 8.9 %collective-permute-start.4 = (f32[3,768]{1,0:T(4,128)S(1)}, f32[3,768]{1,0:T(4,128)S(1)}, u32[]{:S(2)}, u32[]{:S(2)}) collective-permute-start(f32[3,768]{1,0:T(4,128)S(1)} %get-tuple-element.34), channel_id=1, source_target_pairs={{0,47},{1,2},{2,1},{3,4},{4,3},{5,6},{6,5},{7,8},{8,7},{9,10},{10,... | collective-permute-start | bytes 27656 | tf_op jit(solution)/shard_map/ppermute | solution.py:372
  50.0 7.0 %collective-permute-start.5 = (f32[3,768]{1,0:T(4,128)S(1)}, f32[3,768]{1,0:T(4,128)S(1)}, u32[]{:S(2)}, u32[]{:S(2)}) collective-permute-start(f32[3,768]{1,0:T(4,128)S(1)} %get-tuple-element.35), channel_id=1, source_target_pairs={{0,1},{1,0},{2,3},{3,2},{4,5},{5,4},{6,7},{7,6},{8,9},{9,8},{10,11... | collective-permute-start | bytes 27656 | tf_op jit(solution)/shard_map/ppermute | solution.py:373
  57.0 9.8 %collective-permute-start.6 = (f32[3,256]{1,0:T(4,128)S(1)}, f32[3,256]{1,0:T(4,128)S(1)}, u32[]{:S(2)}, u32[]{:S(2)}) collective-permute-start(f32[3,256]{1,0:T(4,128)S(1)} %get-tuple-element.38), channel_id=1, source_target_pairs={{0,720},{48,96},{96,48},{144,192},{192,144},{240,288},{288,240},{3... | collective-permute-start | bytes 9224 | tf_op jit(solution)/shard_map/ppermute | solution.py:375
  64.9 4.4 %collective-permute-start.7 = (f32[3,256]{1,0:T(4,128)S(1)}, f32[3,256]{1,0:T(4,128)S(1)}, u32[]{:S(2)}, u32[]{:S(2)}) collective-permute-start(f32[3,256]{1,0:T(4,128)S(1)} %get-tuple-element.39), channel_id=1, source_target_pairs={{0,48},{48,0},{96,144},{144,96},{192,240},{240,192},{288,336},{336... | collective-permute-start | bytes 9224 | tf_op jit(solution)/shard_map/ppermute | solution.py:376

commit v4 on v3

--- a/solution.py
+++ b/solution.py
@@ -34,18 +34,18 @@
 
 
 def prepare(
-    feats,
-    positions,
-    atom_count,
-    center,
-    neighbor,
-    valid,
-    w_center,
-    w_neighbor,
-    w_radial,
-    w_second,
-    w_env,
-    readout,
+    feats_hbm,
+    positions_hbm,
+    count_hbm,
+    center_hbm,
+    neighbor_hbm,
+    valid_hbm,
+    w_center_hbm,
+    w_neighbor_hbm,
+    w_radial_hbm,
+    w_second_hbm,
+    w_env_hbm,
+    readout_hbm,
     hot_nb,
     hot_c,
     same,
@@ -59,10 +59,44 @@
     read_b,
     w2_copy,
     we_copy,
+    feats,
+    positions,
+    atom_count,
+    center,
+    neighbor,
+    valid,
+    w_center,
+    w_neighbor,
+    w_radial,
+    readout,
+    sems,
 ):
+    moves = [
+        pltpu.make_async_copy(source, target, sems.at[k])
+        for k, (source, target) in enumerate(
+            (
+                (neighbor_hbm, neighbor),
+                (center_hbm, center),
+                (valid_hbm, valid),
+                (count_hbm, atom_count),
+                (feats_hbm, feats),
+                (positions_hbm, positions),
+                (w_center_hbm, w_center),
+                (w_neighbor_hbm, w_neighbor),
+                (w_second_hbm, w2_copy),
+                (w_env_hbm, we_copy),
+                (w_radial_hbm, w_radial),
+                (readout_hbm, readout),
+            )
+        )
+    ]
+    for move in moves:
+        move.start()
     atoms = feats.shape[2]
     edges = center.shape[2]
     gx, gy = lax.axis_index("gx"), lax.axis_index("gy")
+    for move in moves[:4]:
+        move.wait()
     c_row = center[0]
     n_row = neighbor[0]
     slot = n_row // atoms
@@ -92,13 +126,20 @@
     hot_c[...] = c_hot
     same[...] = jnp.where(c_col == c_row, 1.0, 0.0).astype(jnp.bfloat16)
 
+    for move in moves[4:]:
+        move.wait()
     near_all = mm(feats[0, 0], w_center[...]).astype(jnp.bfloat16)
     near[...] = mm(c_hot, near_all).T
     pos16 = jnp.concatenate(
         [positions[0, 0].astype(jnp.float32), jnp.zeros((13, atoms), jnp.float32)], axis=0
     ).astype(jnp.bfloat16)
     pos_c = mm(pos16, c_hot, NT)
-    used = (atom_count[gx, gy] * (edges // EBLK) + atoms - 1) // atoms
+    here = (lax.broadcasted_iota(jnp.int32, atom_count.shape, 0) == gx) & (
+        lax.broadcasted_iota(jnp.int32, atom_count.shape, 1) == gy
+    )
+    count = jnp.where(here, atom_count[...], 0).astype(jnp.float32)
+    count = jnp.sum(jnp.sum(count, axis=1, keepdims=True), axis=0, keepdims=True)
+    used = (count.astype(jnp.int32) * (edges // EBLK) + atoms - 1) // atoms
     block = lax.broadcasted_iota(jnp.int32, (1, edges), 1) // EBLK
     mask = jnp.where(block < used, valid[0], 0).astype(jnp.float32)
     aux[...] = jnp.concatenate(
@@ -113,11 +154,9 @@
         axis=0,
     )
 
-    w2_copy[...] = w_second[...]
-    we_copy[...] = w_env[...]
     wn_t[...] = turned(w_neighbor[...]).astype(jnp.bfloat16)
-    w2_t[...] = turned(w_second[...]).astype(jnp.bfloat16)
-    we_t[...] = turned(w_env[...]).astype(jnp.bfloat16)
+    w2_t[...] = turned(w2_copy[...]).astype(jnp.bfloat16)
+    we_t[...] = turned(we_copy[...]).astype(jnp.bfloat16)
     high, low = halves(w_radial[...])
     wr16[...] = jnp.concatenate([high, low], axis=0).astype(jnp.bfloat16)
     wr_t[...] = (
@@ -273,6 +312,14 @@
     return [pl.BlockSpec(memory_space=pltpu.VMEM)] * n
 
 
+def in_hbm(*arrays):
+    return [pltpu.with_memory_space_constraint(a, pltpu.HBM) for a in arrays]
+
+
+def hbm(n):
+    return [pl.BlockSpec(memory_space=pltpu.HBM)] * n
+
+
 def pair_in(axis):
     return [(i, i ^ 1) for i in range(lax.axis_size(axis))]
 
@@ -303,12 +350,12 @@
     own = pl.pallas_call(
         pack,
         out_shape=shape((atoms + POS_ROWS, channels), bf16),
-        in_specs=[pl.BlockSpec(memory_space=pl.ANY)] * 2,
+        in_specs=hbm(2),
         out_specs=pl.BlockSpec(memory_space=pltpu.VMEM),
         scratch_shapes=[pltpu.VMEM((3, atoms), bf16), pltpu.SemaphoreType.DMA((2,))],
         name="pack",
         compiler_params=grant(2),
-    )(feats, positions)
+    )(*in_hbm(feats, positions))
     x_out = lax.ppermute(own, "gx", pair_out("gx"))
     x_in = lax.ppermute(own, "gx", pair_in("gx"))
 
@@ -329,24 +376,42 @@
             shape((channels, channels), bf16),
             shape((channels, 3 * channels), bf16),
         ],
-        in_specs=vmem(2) + [pl.BlockSpec(memory_space=pltpu.SMEM)] + vmem(9),
+        in_specs=hbm(12),
         out_specs=vmem(13),
+        scratch_shapes=[
+            pltpu.VMEM(part.shape, part.dtype)
+            for part in (
+                feats,
+                positions,
+                atom_count,
+                edge_center,
+                edge_neighbor,
+                edge_valid,
+                w_center,
+                w_neighbor,
+                w_radial,
+                readout,
+            )
+        ]
+        + [pltpu.SemaphoreType.DMA((12,))],
         name="prepare",
         compiler_params=grant(8),
         cost_estimate=pl.CostEstimate(flops=100000000, bytes_accessed=3000000, transcendentals=0),
     )(
-        feats,
-        positions,
-        atom_count,
-        edge_center,
-        edge_neighbor,
-        edge_valid,
-        w_center,
-        w_neighbor,
-        w_radial,
-        w_second,
-        w_env,
-        readout,
+        *in_hbm(
+            feats,
+            positions,
+            atom_count,
+            edge_center,
+            edge_neighbor,
+            edge_valid,
+            w_center,
+            w_neighbor,
+            w_radial,
+            w_second,
+            w_env,
+            readout,
+        )
     )
 
     slab = pl.pallas_call(

time: 70.6 us -> 65.6 us (0.929)
  the two profiles are of different devices: /device:TPU:1 before, /device:TPU:8 now
where the time goes in v4:
time: 65.6 us; the launch traced here: 65.2 us
  starting transfers between devices  53.3 us (81%)
  Pallas kernels  5.43 us (8%)
  waiting for transfers between devices  5.13 us (8%)
  between operations  0.74 us (1%)
    ppermute x1, starting transfers between devices, body(): y_out = lax.ppermute(slab, 'gy', pair_out('gy'))  12.2 us
    ppermute x1, starting transfers between devices, body(): r_out = lax.ppermute(f_out, 'gy', pair_out('gy'))  11.2 us
    ppermute x1, starting transfers between devices, body(): x_in = lax.ppermute(own, 'gx', pair_in('gx'))  9.81 us
    ppermute x1, starting transfers between devices, body(): s_in = lax.ppermute(column[:, atoms:2 * atoms], 'gx', pair_in('gx'))  9.54 us
    ppermute x1, starting transfers between devices, body(): x_out = lax.ppermute(own, 'gx', pair_out('gx'))  3.48 us
    ppermute x1, starting transfers between devices, body(): s_out = lax.ppermute(column[:, 2 * atoms:], 'gx', pair_out('gx'))  3.22 us
    pallas_call x1, Pallas kernels, body(): pl.pallas_call(layer, out_shape=[shape((1, 1, edges), f32)] + [shape((3,...  2.68 us
    ppermute x1, waiting for transfers between devices, body(): x_in = lax.ppermute(own, 'gx', pair_in('gx'))  2.26 us
  transfers between devices with their start and end apart: 8, of which 4 were waited for; matrix products, arithmetic and copies ran while one was open for 0% of the time, Pallas kernels for 3%

profile of v4, /device:TPU:8, one launch (start us, length us, event | category | flops | bytes accessed | tf_op | source)
XLA Modules:
  0.0 65.2 jit_solution(12825534756922435348)
XLA Ops:
  0.6 0.9 %pack.1.own = bf16[272,128]{1,0:T(8,128)(2,1)S(1)} custom-call(bf16[1,1,256,128]{3,2,1,0:T(8,128)(2,1)} %feats_hbm.1, bf16[1,1,3,256]{3,2,1,0:T(4,128)(2,1)} %positions_hbm.1), custom_call_target="tpu_custom_call" | custom-call | tf_op jit(solution)/shard_map/pack/pallas_call | solution.py:350
  1.5 3.5 %collective-permute-start.1 = (bf16[272,128]{1,0:T(8,128)(2,1)S(1)}, bf16[272,128]{1,0:T(8,128)(2,1)S(1)}, u32[]{:S(2)}, u32[]{:S(2)}) collective-permute-start(bf16[272,128]{1,0:T(8,128)(2,1)S(1)} %pack.1.own), channel_id=1, source_target_pairs={{0,720},{48,96},{96,48},{144,192},{192,144},{240,288},{288,240},{3... | collective-permute-start | bytes 208904 | tf_op jit(solution)/shard_map/ppermute | solution.py:359
  5.0 9.8 %collective-permute-start = (bf16[272,128]{1,0:T(8,128)(2,1)S(1)}, bf16[272,128]{1,0:T(8,128)(2,1)S(1)}, u32[]{:S(2)}, u32[]{:S(2)}) collective-permute-start(bf16[272,128]{1,0:T(8,128)(2,1)S(1)} %pack.1.own), channel_id=1, source_target_pairs={{0,48},{48,0},{96,144},{144,96},{192,240},{240,192},{288,336},{336... | collective-permute-start | bytes 208904 | tf_op jit(solution)/shard_map/ppermute | solution.py:360
  14.8 0.0 collective-permute-done.1.x_out
  14.8 2.3 %collective-permute-done.x_in = bf16[272,128]{1,0:T(8,128)(2,1)S(1)} collective-permute-done((bf16[272,128]{1,0:T(8,128)(2,1)S(1)}, bf16[272,128]{1,0:T(8,128)(2,1)S(1)}, u32[]{:S(2)}, u32[]{:S(2)}) %collective-permute-start) | collective-permute-done | bytes 69664 | tf_op jit(solution)/shard_map/ppermute | solution.py:360
  17.1 12.2 %collective-permute-start.3 = (bf16[816,128]{1,0:T(8,128)(2,1)S(1)}, bf16[816,128]{1,0:T(8,128)(2,1)S(1)}, u32[]{:S(2)}, u32[]{:S(2)}) collective-permute-start(bf16[816,128]{1,0:T(8,128)(2,1)S(1)} %assemble.1.slab_own), channel_id=1, source_target_pairs={{0,47},{1,2},{2,1},{3,4},{4,3},{5,6},{6,5},{7,8},{8,7},{9,10},{10,... | collective-permute-start | bytes 626696 | tf_op jit(solution)/shard_map/ppermute | solution.py:425
  29.3 1.9 %collective-permute-start.2 = (bf16[816,128]{1,0:T(8,128)(2,1)S(1)}, bf16[816,128]{1,0:T(8,128)(2,1)S(1)}, u32[]{:S(2)}, u32[]{:S(2)}) collective-permute-start(bf16[816,128]{1,0:T(8,128)(2,1)S(1)} %assemble.1.slab_own), channel_id=1, source_target_pairs={{0,1},{1,0},{2,3},{3,2},{4,5},{5,4},{6,7},{7,6},{8,9},{9,8},{10,11... | collective-permute-start | bytes 626696 | tf_op jit(solution)/shard_map/ppermute | solution.py:426
  31.3 1.9 %prepare.1 = (bf16[256,2304]{1,0:T(8,128)(2,1)S(1)}, bf16[256,256]{1,0:T(8,128)(2,1)S(1)}, bf16[256,256]{1,0:T(8,128)(2,1)S(1)}, f32[128,256]{1,0:T(8,128)S(1)},...) custom-call(bf16[1,1,256,128]{3,2,1,0:T(8,128)(2,1)} %feats_hbm.1, ...), custom_call_target="tpu_custom_call" | custom-call | flops 100000000 | bytes 3000000 | tf_op jit(solution)/shard_map/prepare/pallas_call | solution.py:362
  33.1 0.2 collective-permute-done.3.slab_out
  33.3 0.0 collective-permute-done.2.slab_in
  33.3 2.7 %layer.1 = (f32[1,1,256]{2,1,0:T(1,128)}, f32[3,768]{1,0:T(4,128)S(1)}, f32[3,768]{1,0:T(4,128)S(1)}, f32[3,768]{1,0:T(4,128)S(1)}) custom-call(bf16[816,128]{1,0:T(8,128)(2,1)S(1)} %assemble.1.slab_own, bf16[816,128]{1,0:T(8,128)(2,1)S(1)} %collective-permute-done.2.slab_in, bf16[816,128]{1,0:T(8,128)(2,1)S(1)} %collective-permute-done.3.slab_out, ...), custom_call_target="tpu_custom_call" | custom-call | tf_op jit(solution)/shard_map/layer/pallas_call | solution.py:428
  36.0 11.2 %collective-permute-start.4 = (f32[3,768]{1,0:T(4,128)S(1)}, f32[3,768]{1,0:T(4,128)S(1)}, u32[]{:S(2)}, u32[]{:S(2)}) collective-permute-start(f32[3,768]{1,0:T(4,128)S(1)} %get-tuple-element.34), channel_id=1, source_target_pairs={{0,47},{1,2},{2,1},{3,4},{4,3},{5,6},{6,5},{7,8},{8,7},{9,10},{10,... | collective-permute-start | bytes 27656 | tf_op jit(solution)/shard_map/ppermute | solution.py:437
  47.2 1.9 %collective-permute-start.5 = (f32[3,768]{1,0:T(4,128)S(1)}, f32[3,768]{1,0:T(4,128)S(1)}, u32[]{:S(2)}, u32[]{:S(2)}) collective-permute-start(f32[3,768]{1,0:T(4,128)S(1)} %get-tuple-element.35), channel_id=1, source_target_pairs={{0,1},{1,0},{2,3},{3,2},{4,5},{5,4},{6,7},{7,6},{8,9},{9,8},{10,11... | collective-permute-start | bytes 27656 | tf_op jit(solution)/shard_map/ppermute | solution.py:438
  49.1 0.0 collective-permute-done.4
  49.1 1.1 %collective-permute-done.5 = f32[3,768]{1,0:T(4,128)S(1)} collective-permute-done((f32[3,768]{1,0:T(4,128)S(1)}, f32[3,768]{1,0:T(4,128)S(1)}, u32[]{:S(2)}, u32[]{:S(2)}) %collective-permute-start.5) | collective-permute-done | bytes 9248 | tf_op jit(solution)/shard_map/ppermute | solution.py:438
  50.2 3.2 %collective-permute-start.6 = (f32[3,256]{1,0:T(4,128)S(1)}, f32[3,256]{1,0:T(4,128)S(1)}, u32[]{:S(2)}, u32[]{:S(2)}) collective-permute-start(f32[3,256]{1,0:T(4,128)S(1)} %get-tuple-element.38), channel_id=1, source_target_pairs={{0,720},{48,96},{96,48},{144,192},{192,144},{240,288},{288,240},{3... | collective-permute-start | bytes 9224 | tf_op jit(solution)/shard_map/ppermute | solution.py:440
  53.5 9.5 %collective-permute-start.7 = (f32[3,256]{1,0:T(4,128)S(1)}, f32[3,256]{1,0:T(4,128)S(1)}, u32[]{:S(2)}, u32[]{:S(2)}) collective-permute-start(f32[3,256]{1,0:T(4,128)S(1)} %get-tuple-element.39), channel_id=1, source_target_pairs={{0,48},{48,0},{96,144},{144,96},{192,240},{240,192},{288,336},{336... | collective-permute-start | bytes 9224 | tf_op jit(solution)/shard_map/ppermute | solution.py:441
  63.0 0.0 collective-permute-done.6
  63.0 1.6 %collective-permute-done.7 = f32[3,256]{1,0:T(4,128)S(1)} collective-permute-done((f32[3,256]{1,0:T(4,128)S(1)}, f32[3,256]{1,0:T(4,128)S(1)}, u32[]{:S(2)}, u32[]{:S(2)}) %collective-permute-start.7) | collective-permute-done | bytes 3104 | tf_op jit(solution)/shard_map/ppermute | solution.py:441
  64.6 0.6 copy.14
  (4 shorter events, 0.0 us)
Async XLA Ops:
  1.5 13.3 %collective-permute-start.1 = (bf16[272,128]{1,0:T(8,128)(2,1)S(1)}, bf16[272,128]{1,0:T(8,128)(2,1)S(1)}, u32[]{:S(2)}, u32[]{:S(2)}) collective-permute-start(bf16[272,128]{1,0:T(8,128)(2,1)S(1)} %pack.1.own), channel_id=1, source_target_pairs={{0,720},{48,96},{96,48},{144,192},{192,144},{240,288},{288,240},{3... | collective-permute-start | bytes 208904 | tf_op jit(solution)/shard_map/ppermute | solution.py:359
  5.0 12.1 %collective-permute-start = (bf16[272,128]{1,0:T(8,128)(2,1)S(1)}, bf16[272,128]{1,0:T(8,128)(2,1)S(1)}, u32[]{:S(2)}, u32[]{:S(2)}) collective-permute-start(bf16[272,128]{1,0:T(8,128)(2,1)S(1)} %pack.1.own), channel_id=1, source_target_pairs={{0,48},{48,0},{96,144},{144,96},{192,240},{240,192},{288,336},{336... | collective-permute-start | bytes 208904 | tf_op jit(solution)/shard_map/ppermute | solution.py:360
  17.1 16.2 %collective-permute-start.3 = (bf16[816,128]{1,0:T(8,128)(2,1)S(1)}, bf16[816,128]{1,0:T(8,128)(2,1)S(1)}, u32[]{:S(2)}, u32[]{:S(2)}) collective-permute-start(bf16[816,128]{1,0:T(8,128)(2,1)S(1)} %assemble.1.slab_own), channel_id=1, source_target_pairs={{0,47},{1,2},{2,1},{3,4},{4,3},{5,6},{6,5},{7,8},{8,7},{9,10},{10,... | collective-permute-start | bytes 626696 | tf_op jit(solution)/shard_map/ppermute | solution.py:425
  29.3 4.0 %collective-permute-start.2 = (bf16[816,128]{1,0:T(8,128)(2,1)S(1)}, bf16[816,128]{1,0:T(8,128)(2,1)S(1)}, u32[]{:S(2)}, u32[]{:S(2)}) collective-permute-start(bf16[816,128]{1,0:T(8,128)(2,1)S(1)} %assemble.1.slab_own), channel_id=1, source_target_pairs={{0,1},{1,0},{2,3},{3,2},{4,5},{5,4},{6,7},{7,6},{8,9},{9,8},{10,11... | collective-permute-start | bytes 626696 | tf_op jit(solution)/shard_map/ppermute | solution.py:426
  36.0 13.1 %collective-permute-start.4 = (f32[3,768]{1,0:T(4,128)S(1)}, f32[3,768]{1,0:T(4,128)S(1)}, u32[]{:S(2)}, u32[]{:S(2)}) collective-permute-start(f32[3,768]{1,0:T(4,128)S(1)} %get-tuple-element.34), channel_id=1, source_target_pairs={{0,47},{1,2},{2,1},{3,4},{4,3},{5,6},{6,5},{7,8},{8,7},{9,10},{10,... | collective-permute-start | bytes 27656 | tf_op jit(solution)/shard_map/ppermute | solution.py:437
  47.2 3.1 %collective-permute-start.5 = (f32[3,768]{1,0:T(4,128)S(1)}, f32[3,768]{1,0:T(4,128)S(1)}, u32[]{:S(2)}, u32[]{:S(2)}) collective-permute-start(f32[3,768]{1,0:T(4,128)S(1)} %get-tuple-element.35), channel_id=1, source_target_pairs={{0,1},{1,0},{2,3},{3,2},{4,5},{5,4},{6,7},{7,6},{8,9},{9,8},{10,11... | collective-permute-start | bytes 27656 | tf_op jit(solution)/shard_map/ppermute | solution.py:438
  50.2 12.8 %collective-permute-start.6 = (f32[3,256]{1,0:T(4,128)S(1)}, f32[3,256]{1,0:T(4,128)S(1)}, u32[]{:S(2)}, u32[]{:S(2)}) collective-permute-start(f32[3,256]{1,0:T(4,128)S(1)} %get-tuple-element.38), channel_id=1, source_target_pairs={{0,720},{48,96},{96,48},{144,192},{192,144},{240,288},{288,240},{3... | collective-permute-start | bytes 9224 | tf_op jit(solution)/shard_map/ppermute | solution.py:440
  53.5 11.1 %collective-permute-start.7 = (f32[3,256]{1,0:T(4,128)S(1)}, f32[3,256]{1,0:T(4,128)S(1)}, u32[]{:S(2)}, u32[]{:S(2)}) collective-permute-start(f32[3,256]{1,0:T(4,128)S(1)} %get-tuple-element.39), channel_id=1, source_target_pairs={{0,48},{48,0},{96,144},{144,96},{192,240},{240,192},{288,336},{336... | collective-permute-start | bytes 9224 | tf_op jit(solution)/shard_map/ppermute | solution.py:441

commit v5 on v4

--- a/solution.py
+++ b/solution.py
@@ -189,8 +189,8 @@
     w_env,
     energy,
     f_own,
-    f_in,
-    f_out,
+    f_up,
+    f_down,
 ):
     bf16, f32 = jnp.bfloat16, jnp.float32
     channels, edges = near.shape
@@ -270,14 +270,15 @@
     to_c = mm(lines, hot_c[...])
     to_c = to_c[0:4] + to_c[4:8]
     energy[0] = to_c[3:4]
-    for part, out in enumerate((f_own, f_in, f_out)):
+    parts = []
+    for part in range(3):
         to_nb = mm(lines, hot_nb[:, part * wide : (part + 1) * wide])
-        to_nb = -(to_nb[0:3] + to_nb[4:7])
-        if part == 0:
-            out[:, 0:atoms] = to_nb[:, 0:atoms] + to_c[0:3]
-            out[:, atoms:wide] = to_nb[:, atoms:wide]
-        else:
-            out[...] = to_nb
+        parts.append(-(to_nb[0:3] + to_nb[4:7]))
+    f_own[:, 0:atoms] = parts[0][:, 0:atoms] + to_c[0:3]
+    f_own[:, atoms:wide] = parts[0][:, atoms:wide]
+    upper_in = lax.axis_index("gy") % 2 == 0
+    f_up[...] = jnp.where(upper_in, parts[1], parts[2])
+    f_down[...] = jnp.where(upper_in, parts[2], parts[1])
 
 
 def pack(feats, positions, packed, pos, sems):
@@ -327,6 +328,11 @@
 def pair_out(axis):
     count = lax.axis_size(axis)
     return [(i, (i + 1) % count if i % 2 else (i - 1) % count) for i in range(count)]
+
+
+def step_by(axis, distance):
+    count = lax.axis_size(axis)
+    return [(i, (i + distance) % count) for i in range(count)]
 
 
 def body(
@@ -425,7 +431,7 @@
     y_out = lax.ppermute(slab, "gy", pair_out("gy"))
     y_in = lax.ppermute(slab, "gy", pair_in("gy"))
 
-    energy, f_own, f_in, f_out = pl.pallas_call(
+    energy, f_own, f_up, f_down = pl.pallas_call(
         layer,
         out_shape=[shape((1, 1, edges), f32)] + [shape((3, 3 * atoms), f32)] * 3,
         in_specs=vmem(16),
@@ -434,9 +440,9 @@
         compiler_params=grant(8),
     )(slab, y_in, y_out, *prepared, w2_copy, we_copy)
 
-    r_out = lax.ppermute(f_out, "gy", pair_out("gy"))
-    r_in = lax.ppermute(f_in, "gy", pair_in("gy"))
-    column = f_own + r_out + r_in
+    r_up = lax.ppermute(f_up, "gy", step_by("gy", 1))
+    r_down = lax.ppermute(f_down, "gy", step_by("gy", -1))
+    column = f_own + r_up + r_down
     s_out = lax.ppermute(column[:, 2 * atoms :], "gx", pair_out("gx"))
     s_in = lax.ppermute(column[:, atoms : 2 * atoms], "gx", pair_in("gx"))
     forces = column[:, :atoms] + s_out + s_in

time: 65.6 us -> 67.4 us (1.027)
  starting transfers between devices: 53.3 us -> 54.9 us
    ppermute x1, starting transfers between devices: 9.54 us -> 11.1 us  [body(): s_in = lax.ppermute(column[:, atoms:2 * atoms], 'gx', pair_in('gx'))]
where the time goes in v5:
time: 67.4 us; the launch traced here: 67 us
  starting transfers between devices  54.9 us (81%)
  Pallas kernels  5.43 us (8%)
  waiting for transfers between devices  5.37 us (8%)
  between operations  0.74 us (1%)
    ppermute x1, starting transfers between devices, body(): y_out = lax.ppermute(slab, 'gy', pair_out('gy'))  12.2 us
    ppermute x1, starting transfers between devices, body(): s_in = lax.ppermute(column[:, atoms:2 * atoms], 'gx', pair_in('gx'))  11.1 us
    ppermute x1, starting transfers between devices, body(): r_down = lax.ppermute(f_down, 'gy', step_by('gy', -1))  10.8 us
    ppermute x1, starting transfers between devices, body(): x_in = lax.ppermute(own, 'gx', pair_in('gx'))  9.81 us
    ppermute x1, starting transfers between devices, body(): x_out = lax.ppermute(own, 'gx', pair_out('gx'))  3.48 us
    ppermute x1, starting transfers between devices, body(): s_out = lax.ppermute(column[:, 2 * atoms:], 'gx', pair_out('gx'))  3.22 us
    pallas_call x1, Pallas kernels, body(): pl.pallas_call(layer, out_shape=[shape((1, 1, edges), f32)] + [shape((3,...  2.68 us
    ppermute x1, waiting for transfers between devices, body(): x_in = lax.ppermute(own, 'gx', pair_in('gx'))  2.26 us
  transfers between devices with their start and end apart: 8, of which 4 were waited for; matrix products, arithmetic and copies ran while one was open for 0% of the time, Pallas kernels for 3%

profile of v5, /device:TPU:8, one launch (start us, length us, event | category | flops | bytes accessed | tf_op | source)
XLA Modules:
  0.0 67.0 jit_solution(9433331459027014605)
XLA Ops:
  0.6 0.9 %pack.1.own = bf16[272,128]{1,0:T(8,128)(2,1)S(1)} custom-call(bf16[1,1,256,128]{3,2,1,0:T(8,128)(2,1)} %feats_hbm.1, bf16[1,1,3,256]{3,2,1,0:T(4,128)(2,1)} %positions_hbm.1), custom_call_target="tpu_custom_call" | custom-call | tf_op jit(solution)/shard_map/pack/pallas_call | solution.py:356
  1.5 3.5 %collective-permute-start.1 = (bf16[272,128]{1,0:T(8,128)(2,1)S(1)}, bf16[272,128]{1,0:T(8,128)(2,1)S(1)}, u32[]{:S(2)}, u32[]{:S(2)}) collective-permute-start(bf16[272,128]{1,0:T(8,128)(2,1)S(1)} %pack.1.own), channel_id=1, source_target_pairs={{0,720},{48,96},{96,48},{144,192},{192,144},{240,288},{288,240},{3... | collective-permute-start | bytes 208904 | tf_op jit(solution)/shard_map/ppermute | solution.py:365
  5.0 9.8 %collective-permute-start = (bf16[272,128]{1,0:T(8,128)(2,1)S(1)}, bf16[272,128]{1,0:T(8,128)(2,1)S(1)}, u32[]{:S(2)}, u32[]{:S(2)}) collective-permute-start(bf16[272,128]{1,0:T(8,128)(2,1)S(1)} %pack.1.own), channel_id=1, source_target_pairs={{0,48},{48,0},{96,144},{144,96},{192,240},{240,192},{288,336},{336... | collective-permute-start | bytes 208904 | tf_op jit(solution)/shard_map/ppermute | solution.py:366
  14.8 0.0 collective-permute-done.1.x_out
  14.8 2.3 %collective-permute-done.x_in = bf16[272,128]{1,0:T(8,128)(2,1)S(1)} collective-permute-done((bf16[272,128]{1,0:T(8,128)(2,1)S(1)}, bf16[272,128]{1,0:T(8,128)(2,1)S(1)}, u32[]{:S(2)}, u32[]{:S(2)}) %collective-permute-start) | collective-permute-done | bytes 69664 | tf_op jit(solution)/shard_map/ppermute | solution.py:366
  17.1 12.2 %collective-permute-start.3 = (bf16[816,128]{1,0:T(8,128)(2,1)S(1)}, bf16[816,128]{1,0:T(8,128)(2,1)S(1)}, u32[]{:S(2)}, u32[]{:S(2)}) collective-permute-start(bf16[816,128]{1,0:T(8,128)(2,1)S(1)} %assemble.1.slab_own), channel_id=1, source_target_pairs={{0,47},{1,2},{2,1},{3,4},{4,3},{5,6},{6,5},{7,8},{8,7},{9,10},{10,... | collective-permute-start | bytes 626696 | tf_op jit(solution)/shard_map/ppermute | solution.py:431
  29.3 1.9 %collective-permute-start.2 = (bf16[816,128]{1,0:T(8,128)(2,1)S(1)}, bf16[816,128]{1,0:T(8,128)(2,1)S(1)}, u32[]{:S(2)}, u32[]{:S(2)}) collective-permute-start(bf16[816,128]{1,0:T(8,128)(2,1)S(1)} %assemble.1.slab_own), channel_id=1, source_target_pairs={{0,1},{1,0},{2,3},{3,2},{4,5},{5,4},{6,7},{7,6},{8,9},{9,8},{10,11... | collective-permute-start | bytes 626696 | tf_op jit(solution)/shard_map/ppermute | solution.py:432
  31.3 1.9 %prepare.1 = (bf16[256,2304]{1,0:T(8,128)(2,1)S(1)}, bf16[256,256]{1,0:T(8,128)(2,1)S(1)}, bf16[256,256]{1,0:T(8,128)(2,1)S(1)}, f32[128,256]{1,0:T(8,128)S(1)},...) custom-call(bf16[1,1,256,128]{3,2,1,0:T(8,128)(2,1)} %feats_hbm.1, ...), custom_call_target="tpu_custom_call" | custom-call | flops 100000000 | bytes 3000000 | tf_op jit(solution)/shard_map/prepare/pallas_call | solution.py:368
  33.1 0.2 collective-permute-done.3.slab_out
  33.3 0.0 collective-permute-done.2.slab_in
  33.3 2.7 %layer.1 = (f32[1,1,256]{2,1,0:T(1,128)}, f32[3,768]{1,0:T(4,128)S(1)}, f32[3,768]{1,0:T(4,128)S(1)}, f32[3,768]{1,0:T(4,128)S(1)}) custom-call(bf16[816,128]{1,0:T(8,128)(2,1)S(1)} %assemble.1.slab_own, bf16[816,128]{1,0:T(8,128)(2,1)S(1)} %collective-permute-done.2.slab_in, bf16[816,128]{1,0:T(8,128)(2,1)S(1)} %collective-permute-done.3.slab_out, ...), custom_call_target="tpu_custom_call" | custom-call | tf_op jit(solution)/shard_map/layer/pallas_call | solution.py:434
  36.0 2.3 %collective-permute-start.4 = (f32[3,768]{1,0:T(4,128)S(1)}, f32[3,768]{1,0:T(4,128)S(1)}, u32[]{:S(2)}, u32[]{:S(2)}) collective-permute-start(f32[3,768]{1,0:T(4,128)S(1)} %get-tuple-element.34), channel_id=1, source_target_pairs={{0,1},{1,2},{2,3},{3,4},{4,5},{5,6},{6,7},{7,8},{8,9},{9,10},{10,1... | collective-permute-start | bytes 27656 | tf_op jit(solution)/shard_map/ppermute | solution.py:443
  38.2 10.8 %collective-permute-start.5 = (f32[3,768]{1,0:T(4,128)S(1)}, f32[3,768]{1,0:T(4,128)S(1)}, u32[]{:S(2)}, u32[]{:S(2)}) collective-permute-start(f32[3,768]{1,0:T(4,128)S(1)} %get-tuple-element.35), channel_id=1, source_target_pairs={{0,47},{1,0},{2,1},{3,2},{4,3},{5,4},{6,5},{7,6},{8,7},{9,8},{10,9... | collective-permute-start | bytes 27656 | tf_op jit(solution)/shard_map/ppermute | solution.py:444
  49.1 0.0 collective-permute-done.4
  49.1 1.4 %collective-permute-done.5 = f32[3,768]{1,0:T(4,128)S(1)} collective-permute-done((f32[3,768]{1,0:T(4,128)S(1)}, f32[3,768]{1,0:T(4,128)S(1)}, u32[]{:S(2)}, u32[]{:S(2)}) %collective-permute-start.5) | collective-permute-done | bytes 9248 | tf_op jit(solution)/shard_map/ppermute | solution.py:444
  50.5 3.2 %collective-permute-start.6 = (f32[3,256]{1,0:T(4,128)S(1)}, f32[3,256]{1,0:T(4,128)S(1)}, u32[]{:S(2)}, u32[]{:S(2)}) collective-permute-start(f32[3,256]{1,0:T(4,128)S(1)} %get-tuple-element.38), channel_id=1, source_target_pairs={{0,720},{48,96},{96,48},{144,192},{192,144},{240,288},{288,240},{3... | collective-permute-start | bytes 9224 | tf_op jit(solution)/shard_map/ppermute | solution.py:446
  53.7 11.1 %collective-permute-start.7 = (f32[3,256]{1,0:T(4,128)S(1)}, f32[3,256]{1,0:T(4,128)S(1)}, u32[]{:S(2)}, u32[]{:S(2)}) collective-permute-start(f32[3,256]{1,0:T(4,128)S(1)} %get-tuple-element.39), channel_id=1, source_target_pairs={{0,48},{48,0},{96,144},{144,96},{192,240},{240,192},{288,336},{336... | collective-permute-start | bytes 9224 | tf_op jit(solution)/shard_map/ppermute | solution.py:447
  64.8 0.0 collective-permute-done.6
  64.8 1.6 %collective-permute-done.7 = f32[3,256]{1,0:T(4,128)S(1)} collective-permute-done((f32[3,256]{1,0:T(4,128)S(1)}, f32[3,256]{1,0:T(4,128)S(1)}, u32[]{:S(2)}, u32[]{:S(2)}) %collective-permute-start.7) | collective-permute-done | bytes 3104 | tf_op jit(solution)/shard_map/ppermute | solution.py:447
  66.4 0.6 copy.14
  (4 shorter events, 0.0 us)
Async XLA Ops:
  1.5 13.3 %collective-permute-start.1 = (bf16[272,128]{1,0:T(8,128)(2,1)S(1)}, bf16[272,128]{1,0:T(8,128)(2,1)S(1)}, u32[]{:S(2)}, u32[]{:S(2)}) collective-permute-start(bf16[272,128]{1,0:T(8,128)(2,1)S(1)} %pack.1.own), channel_id=1, source_target_pairs={{0,720},{48,96},{96,48},{144,192},{192,144},{240,288},{288,240},{3... | collective-permute-start | bytes 208904 | tf_op jit(solution)/shard_map/ppermute | solution.py:365
  5.0 12.1 %collective-permute-start = (bf16[272,128]{1,0:T(8,128)(2,1)S(1)}, bf16[272,128]{1,0:T(8,128)(2,1)S(1)}, u32[]{:S(2)}, u32[]{:S(2)}) collective-permute-start(bf16[272,128]{1,0:T(8,128)(2,1)S(1)} %pack.1.own), channel_id=1, source_target_pairs={{0,48},{48,0},{96,144},{144,96},{192,240},{240,192},{288,336},{336... | collective-permute-start | bytes 208904 | tf_op jit(solution)/shard_map/ppermute | solution.py:366
  17.1 16.2 %collective-permute-start.3 = (bf16[816,128]{1,0:T(8,128)(2,1)S(1)}, bf16[816,128]{1,0:T(8,128)(2,1)S(1)}, u32[]{:S(2)}, u32[]{:S(2)}) collective-permute-start(bf16[816,128]{1,0:T(8,128)(2,1)S(1)} %assemble.1.slab_own), channel_id=1, source_target_pairs={{0,47},{1,2},{2,1},{3,4},{4,3},{5,6},{6,5},{7,8},{8,7},{9,10},{10,... | collective-permute-start | bytes 626696 | tf_op jit(solution)/shard_map/ppermute | solution.py:431
  29.3 4.0 %collective-permute-start.2 = (bf16[816,128]{1,0:T(8,128)(2,1)S(1)}, bf16[816,128]{1,0:T(8,128)(2,1)S(1)}, u32[]{:S(2)}, u32[]{:S(2)}) collective-permute-start(bf16[816,128]{1,0:T(8,128)(2,1)S(1)} %assemble.1.slab_own), channel_id=1, source_target_pairs={{0,1},{1,0},{2,3},{3,2},{4,5},{5,4},{6,7},{7,6},{8,9},{9,8},{10,11... | collective-permute-start | bytes 626696 | tf_op jit(solution)/shard_map/ppermute | solution.py:432
  36.0 13.1 %collective-permute-start.4 = (f32[3,768]{1,0:T(4,128)S(1)}, f32[3,768]{1,0:T(4,128)S(1)}, u32[]{:S(2)}, u32[]{:S(2)}) collective-permute-start(f32[3,768]{1,0:T(4,128)S(1)} %get-tuple-element.34), channel_id=1, source_target_pairs={{0,1},{1,2},{2,3},{3,4},{4,5},{5,6},{6,7},{7,8},{8,9},{9,10},{10,1... | collective-permute-start | bytes 27656 | tf_op jit(solution)/shard_map/ppermute | solution.py:443
  38.2 12.2 %collective-permute-start.5 = (f32[3,768]{1,0:T(4,128)S(1)}, f32[3,768]{1,0:T(4,128)S(1)}, u32[]{:S(2)}, u32[]{:S(2)}) collective-permute-start(f32[3,768]{1,0:T(4,128)S(1)} %get-tuple-element.35), channel_id=1, source_target_pairs={{0,47},{1,0},{2,1},{3,2},{4,3},{5,4},{6,5},{7,6},{8,7},{9,8},{10,9... | collective-permute-start | bytes 27656 | tf_op jit(solution)/shard_map/ppermute | solution.py:444
  50.5 14.3 %collective-permute-start.6 = (f32[3,256]{1,0:T(4,128)S(1)}, f32[3,256]{1,0:T(4,128)S(1)}, u32[]{:S(2)}, u32[]{:S(2)}) collective-permute-start(f32[3,256]{1,0:T(4,128)S(1)} %get-tuple-element.38), channel_id=1, source_target_pairs={{0,720},{48,96},{96,48},{144,192},{192,144},{240,288},{288,240},{3... | collective-permute-start | bytes 9224 | tf_op jit(solution)/shard_map/ppermute | solution.py:446
  53.7 12.7 %collective-permute-start.7 = (f32[3,256]{1,0:T(4,128)S(1)}, f32[3,256]{1,0:T(4,128)S(1)}, u32[]{:S(2)}, u32[]{:S(2)}) collective-permute-start(f32[3,256]{1,0:T(4,128)S(1)} %get-tuple-element.39), channel_id=1, source_target_pairs={{0,48},{48,0},{96,144},{144,96},{192,240},{240,192},{288,336},{336... | collective-permute-start | bytes 9224 | tf_op jit(solution)/shard_map/ppermute | solution.py:447

commit v6 on v4

--- a/solution.py
+++ b/solution.py
@@ -34,6 +34,7 @@
 
 
 def prepare(
+    slab,
     feats_hbm,
     positions_hbm,
     count_hbm,
@@ -59,6 +60,8 @@
     read_b,
     w2_copy,
     we_copy,
+    rows_own,
+    pos_own,
     feats,
     positions,
     atom_count,
@@ -122,6 +125,13 @@
         hot_nb[:, part * atoms : (part + 1) * atoms] = jnp.where(
             lane == n_col - part * atoms, 1.0, 0.0
         ).astype(jnp.bfloat16)
+    wide = 3 * atoms
+    hot = hot_nb[:, 0:wide]
+    rows_own[...] = mm(hot, slab[0:wide])
+    packed = slab[wide : wide + 3 * POS_ROWS].astype(jnp.float32)
+    pos = jnp.concatenate([packed[8 * k : 8 * k + 8] for k in range(6)], axis=1)
+    pos = jnp.concatenate([pos, jnp.zeros_like(pos)], axis=0).astype(jnp.bfloat16)
+    pos_own[...] = mm(pos, hot, NT)[0:8]
     c_hot = jnp.where(lane == c_col, 1.0, 0.0).astype(jnp.bfloat16)
     hot_c[...] = c_hot
     same[...] = jnp.where(c_col == c_row, 1.0, 0.0).astype(jnp.bfloat16)
@@ -171,7 +181,6 @@
 
 
 def layer(
-    slab_own,
     slab_in,
     slab_out,
     hot_nb,
@@ -187,6 +196,8 @@
     read_b,
     w_second,
     w_env,
+    rows_own,
+    pos_own,
     energy,
     f_own,
     f_in,
@@ -196,9 +207,9 @@
     channels, edges = near.shape
     atoms = hot_c.shape[1]
     wide = 3 * atoms
-    rows_nb = jnp.zeros((edges, channels), f32)
-    pos_nb = jnp.zeros((8, edges), f32)
-    for part, slab in enumerate((slab_own, slab_in, slab_out)):
+    rows_nb = rows_own[...]
+    pos_nb = pos_own[...]
+    for part, slab in enumerate((slab_in, slab_out), 1):
         hot = hot_nb[:, part * wide : (part + 1) * wide]
         rows_nb = rows_nb + mm(hot, slab[0:wide])
         packed = slab[wide : wide + 3 * POS_ROWS].astype(f32)
@@ -270,14 +281,14 @@
     to_c = mm(lines, hot_c[...])
     to_c = to_c[0:4] + to_c[4:8]
     energy[0] = to_c[3:4]
+    upper_in = lax.axis_index("gx") % 2 == 0
     for part, out in enumerate((f_own, f_in, f_out)):
         to_nb = mm(lines, hot_nb[:, part * wide : (part + 1) * wide])
         to_nb = -(to_nb[0:3] + to_nb[4:7])
-        if part == 0:
-            out[:, 0:atoms] = to_nb[:, 0:atoms] + to_c[0:3]
-            out[:, atoms:wide] = to_nb[:, atoms:wide]
-        else:
-            out[...] = to_nb
+        mine, inner, outer = (to_nb[:, k * atoms : (k + 1) * atoms] for k in range(3))
+        out[:, 0:atoms] = mine + to_c[0:3] if part == 0 else mine
+        out[:, atoms : 2 * atoms] = jnp.where(upper_in, inner, outer)
+        out[:, 2 * atoms : wide] = jnp.where(upper_in, outer, inner)
 
 
 def pack(feats, positions, packed, pos, sems):
@@ -327,6 +338,11 @@
 def pair_out(axis):
     count = lax.axis_size(axis)
     return [(i, (i + 1) % count if i % 2 else (i - 1) % count) for i in range(count)]
+
+
+def step_by(axis, distance):
+    count = lax.axis_size(axis)
+    return [(i, (i + distance) % count) for i in range(count)]
 
 
 def body(
@@ -359,7 +375,18 @@
     x_out = lax.ppermute(own, "gx", pair_out("gx"))
     x_in = lax.ppermute(own, "gx", pair_in("gx"))
 
-    *prepared, w2_copy, we_copy = pl.pallas_call(
+    slab = pl.pallas_call(
+        assemble,
+        out_shape=shape((3 * (atoms + POS_ROWS), channels), bf16),
+        in_specs=vmem(3),
+        out_specs=pl.BlockSpec(memory_space=pltpu.VMEM),
+        name="assemble",
+        compiler_params=grant(2),
+    )(own, x_in, x_out)
+    y_out = lax.ppermute(slab, "gy", pair_out("gy"))
+    y_in = lax.ppermute(slab, "gy", pair_in("gy"))
+
+    *prepared, w2_copy, we_copy, rows_own, pos_own = pl.pallas_call(
         prepare,
         out_shape=[
             shape((edges, 9 * atoms), bf16),
@@ -375,9 +402,11 @@
             shape((3, channels, edges), f32),
             shape((channels, channels), bf16),
             shape((channels, 3 * channels), bf16),
+            shape((edges, channels), f32),
+            shape((8, edges), f32),
         ],
-        in_specs=hbm(12),
-        out_specs=vmem(13),
+        in_specs=vmem(1) + hbm(12),
+        out_specs=vmem(15),
         scratch_shapes=[
             pltpu.VMEM(part.shape, part.dtype)
             for part in (
@@ -398,6 +427,7 @@
         compiler_params=grant(8),
         cost_estimate=pl.CostEstimate(flops=100000000, bytes_accessed=3000000, transcendentals=0),
     )(
+        slab,
         *in_hbm(
             feats,
             positions,
@@ -414,32 +444,21 @@
         )
     )
 
-    slab = pl.pallas_call(
-        assemble,
-        out_shape=shape((3 * (atoms + POS_ROWS), channels), bf16),
-        in_specs=vmem(3),
-        out_specs=pl.BlockSpec(memory_space=pltpu.VMEM),
-        name="assemble",
-        compiler_params=grant(2),
-    )(own, x_in, x_out)
-    y_out = lax.ppermute(slab, "gy", pair_out("gy"))
-    y_in = lax.ppermute(slab, "gy", pair_in("gy"))
-
     energy, f_own, f_in, f_out = pl.pallas_call(
         layer,
         out_shape=[shape((1, 1, edges), f32)] + [shape((3, 3 * atoms), f32)] * 3,
-        in_specs=vmem(16),
+        in_specs=vmem(17),
         out_specs=vmem(4),
         name="layer",
         compiler_params=grant(8),
-    )(slab, y_in, y_out, *prepared, w2_copy, we_copy)
+    )(y_in, y_out, *prepared, w2_copy, we_copy, rows_own, pos_own)
 
     r_out = lax.ppermute(f_out, "gy", pair_out("gy"))
     r_in = lax.ppermute(f_in, "gy", pair_in("gy"))
     column = f_own + r_out + r_in
-    s_out = lax.ppermute(column[:, 2 * atoms :], "gx", pair_out("gx"))
-    s_in = lax.ppermute(column[:, atoms : 2 * atoms], "gx", pair_in("gx"))
-    forces = column[:, :atoms] + s_out + s_in
+    s_up = lax.ppermute(column[:, atoms : 2 * atoms], "gx", step_by("gx", 1))
+    s_down = lax.ppermute(column[:, 2 * atoms :], "gx", step_by("gx", -1))
+    forces = column[:, :atoms] + s_up + s_down
     return (energy, forces[None, None])
 
 

time: 65.6 us -> 65.1 us (level)
  the two profiles are of different devices: /device:TPU:8 before, /device:TPU:30 now
where the time goes in v6:
time: 65.1 us; the launch traced here: 64.7 us
  starting transfers between devices  29.2 us (45%)
  waiting for transfers between devices  28.9 us (44%)
  Pallas kernels  5.3 us (8%)
  between operations  0.74 us (1%)
    ppermute x1, waiting for transfers between devices, body(): x_in = lax.ppermute(own, 'gx', pair_in('gx'))  11.1 us
    ppermute x1, starting transfers between devices, body(): x_out = lax.ppermute(own, 'gx', pair_out('gx'))  11.1 us
    ppermute x1, waiting for transfers between devices, body(): y_out = lax.ppermute(slab, 'gy', pair_out('gy'))  7.41 us
    ppermute x1, waiting for transfers between devices, body(): s_down = lax.ppermute(column[:, 2 * atoms:], 'gx', step_by('gx', -1))  5.47 us
    ppermute x1, waiting for transfers between devices, body(): r_out = lax.ppermute(f_out, 'gy', pair_out('gy'))  4.57 us
    ppermute x1, starting transfers between devices, body(): r_out = lax.ppermute(f_out, 'gy', pair_out('gy'))  4.51 us
    ppermute x1, starting transfers between devices, body(): s_down = lax.ppermute(column[:, 2 * atoms:], 'gx', step_by('gx', -1))  3.92 us
    pallas_call x1, Pallas kernels, body(): pl.pallas_call(layer, out_shape=[shape((1, 1, edges), f32)] + [shape((3,...  2.48 us
  transfers between devices with their start and end apart: 8, of which 5 were waited for; matrix products, arithmetic and copies ran while one was open for 0% of the time, Pallas kernels for 3%

profile of v6, /device:TPU:30, one launch (start us, length us, event | category | flops | bytes accessed | tf_op | source)
XLA Modules:
  0.0 64.7 jit_solution(15894436579710772550)
XLA Ops:
  0.6 0.9 %pack.1.own = bf16[272,128]{1,0:T(8,128)(2,1)S(1)} custom-call(bf16[1,1,256,128]{3,2,1,0:T(8,128)(2,1)} %feats_hbm.1, bf16[1,1,3,256]{3,2,1,0:T(4,128)(2,1)} %positions_hbm.1), custom_call_target="tpu_custom_call" | custom-call | tf_op jit(solution)/shard_map/pack/pallas_call | solution.py:366
  1.5 11.1 %collective-permute-start.1 = (bf16[272,128]{1,0:T(8,128)(2,1)S(1)}, bf16[272,128]{1,0:T(8,128)(2,1)S(1)}, u32[]{:S(2)}, u32[]{:S(2)}) collective-permute-start(bf16[272,128]{1,0:T(8,128)(2,1)S(1)} %pack.1.own), channel_id=1, source_target_pairs={{0,720},{48,96},{96,48},{144,192},{192,144},{240,288},{288,240},{3... | collective-permute-start | bytes 208904 | tf_op jit(solution)/shard_map/ppermute | solution.py:375
  12.6 1.9 %collective-permute-start = (bf16[272,128]{1,0:T(8,128)(2,1)S(1)}, bf16[272,128]{1,0:T(8,128)(2,1)S(1)}, u32[]{:S(2)}, u32[]{:S(2)}) collective-permute-start(bf16[272,128]{1,0:T(8,128)(2,1)S(1)} %pack.1.own), channel_id=1, source_target_pairs={{0,48},{48,0},{96,144},{144,96},{192,240},{240,192},{288,336},{336... | collective-permute-start | bytes 208904 | tf_op jit(solution)/shard_map/ppermute | solution.py:376
  14.5 0.3 collective-permute-done.1.x_out
  14.8 11.1 %collective-permute-done.x_in = bf16[272,128]{1,0:T(8,128)(2,1)S(1)} collective-permute-done((bf16[272,128]{1,0:T(8,128)(2,1)S(1)}, bf16[272,128]{1,0:T(8,128)(2,1)S(1)}, u32[]{:S(2)}, u32[]{:S(2)}) %collective-permute-start) | collective-permute-done | bytes 69664 | tf_op jit(solution)/shard_map/ppermute | solution.py:376
  25.9 2.0 %collective-permute-start.3 = (bf16[816,128]{1,0:T(8,128)(2,1)S(1)}, bf16[816,128]{1,0:T(8,128)(2,1)S(1)}, u32[]{:S(2)}, u32[]{:S(2)}) collective-permute-start(bf16[816,128]{1,0:T(8,128)(2,1)S(1)} %assemble.1.slab), channel_id=1, source_target_pairs={{0,47},{1,2},{2,1},{3,4},{4,3},{5,6},{6,5},{7,8},{8,7},{9,10},{10,... | collective-permute-start | bytes 626696 | tf_op jit(solution)/shard_map/ppermute | solution.py:386
  27.9 1.9 %collective-permute-start.2 = (bf16[816,128]{1,0:T(8,128)(2,1)S(1)}, bf16[816,128]{1,0:T(8,128)(2,1)S(1)}, u32[]{:S(2)}, u32[]{:S(2)}) collective-permute-start(bf16[816,128]{1,0:T(8,128)(2,1)S(1)} %assemble.1.slab), channel_id=1, source_target_pairs={{0,1},{1,0},{2,3},{3,2},{4,5},{5,4},{6,7},{7,6},{8,9},{9,8},{10,11... | collective-permute-start | bytes 626696 | tf_op jit(solution)/shard_map/ppermute | solution.py:387
  29.9 1.9 %prepare.1 = (bf16[256,2304]{1,0:T(8,128)(2,1)S(1)}, bf16[256,256]{1,0:T(8,128)(2,1)S(1)}, bf16[256,256]{1,0:T(8,128)(2,1)S(1)}, f32[128,256]{1,0:T(8,128)S(1)},...) custom-call(bf16[816,128]{1,0:T(8,128)(2,1)S(1)} %assemble.1.slab, ...), custom_call_target="tpu_custom_call" | custom-call | flops 100000000 | bytes 3000000 | tf_op jit(solution)/shard_map/prepare/pallas_call | solution.py:389
  31.8 7.4 %collective-permute-done.3.slab_out = bf16[816,128]{1,0:T(8,128)(2,1)S(1)} collective-permute-done((bf16[816,128]{1,0:T(8,128)(2,1)S(1)}, bf16[816,128]{1,0:T(8,128)(2,1)S(1)}, u32[]{:S(2)}, u32[]{:S(2)}) %collective-permute-start.3) | collective-permute-done | bytes 208928 | tf_op jit(solution)/shard_map/ppermute | solution.py:386
  39.2 0.0 collective-permute-done.2.slab_in
  39.2 2.5 %layer.1 = (f32[1,1,256]{2,1,0:T(1,128)}, f32[3,768]{1,0:T(4,128)S(1)}, f32[3,768]{1,0:T(4,128)S(1)}, f32[3,768]{1,0:T(4,128)S(1)}) custom-call(bf16[816,128]{1,0:T(8,128)(2,1)S(1)} %collective-permute-done.2.slab_in, bf16[816,128]{1,0:T(8,128)(2,1)S(1)} %collective-permute-done.3.slab_out, bf16[256,2304]{1,0:T(8,128)(2,1)S(1)} %get-tuple-element.21.hot_nb, ...), custom_call_target="tpu_custom_call" | custom-call | tf_op jit(solution)/shard_map/layer/pallas_call | solution.py:447
  41.7 4.5 %collective-permute-start.4 = (f32[3,768]{1,0:T(4,128)S(1)}, f32[3,768]{1,0:T(4,128)S(1)}, u32[]{:S(2)}, u32[]{:S(2)}) collective-permute-start(f32[3,768]{1,0:T(4,128)S(1)} %get-tuple-element.38), channel_id=1, source_target_pairs={{0,47},{1,2},{2,1},{3,4},{4,3},{5,6},{6,5},{7,8},{8,7},{9,10},{10,... | collective-permute-start | bytes 27656 | tf_op jit(solution)/shard_map/ppermute | solution.py:456
  46.2 1.9 %collective-permute-start.5 = (f32[3,768]{1,0:T(4,128)S(1)}, f32[3,768]{1,0:T(4,128)S(1)}, u32[]{:S(2)}, u32[]{:S(2)}) collective-permute-start(f32[3,768]{1,0:T(4,128)S(1)} %get-tuple-element.39), channel_id=1, source_target_pairs={{0,1},{1,0},{2,3},{3,2},{4,5},{5,4},{6,7},{7,6},{8,9},{9,8},{10,11... | collective-permute-start | bytes 27656 | tf_op jit(solution)/shard_map/ppermute | solution.py:457
  48.2 4.6 %collective-permute-done.4 = f32[3,768]{1,0:T(4,128)S(1)} collective-permute-done((f32[3,768]{1,0:T(4,128)S(1)}, f32[3,768]{1,0:T(4,128)S(1)}, u32[]{:S(2)}, u32[]{:S(2)}) %collective-permute-start.4) | collective-permute-done | bytes 9248 | tf_op jit(solution)/shard_map/ppermute | solution.py:456
  52.7 0.0 collective-permute-done.5
  52.7 1.9 %collective-permute-start.6 = (f32[3,256]{1,0:T(4,128)S(1)}, f32[3,256]{1,0:T(4,128)S(1)}, u32[]{:S(2)}, u32[]{:S(2)}) collective-permute-start(f32[3,256]{1,0:T(4,128)S(1)} %get-tuple-element.42), channel_id=1, source_target_pairs={{0,48},{48,96},{96,144},{144,192},{192,240},{240,288},{288,336},{3... | collective-permute-start | bytes 9224 | tf_op jit(solution)/shard_map/ppermute | solution.py:459
  54.7 3.9 %collective-permute-start.7 = (f32[3,256]{1,0:T(4,128)S(1)}, f32[3,256]{1,0:T(4,128)S(1)}, u32[]{:S(2)}, u32[]{:S(2)}) collective-permute-start(f32[3,256]{1,0:T(4,128)S(1)} %get-tuple-element.43), channel_id=1, source_target_pairs={{0,720},{48,0},{96,48},{144,96},{192,144},{240,192},{288,240},{336... | collective-permute-start | bytes 9224 | tf_op jit(solution)/shard_map/ppermute | solution.py:460
  58.6 0.0 collective-permute-done.6
  58.6 5.5 %collective-permute-done.7 = f32[3,256]{1,0:T(4,128)S(1)} collective-permute-done((f32[3,256]{1,0:T(4,128)S(1)}, f32[3,256]{1,0:T(4,128)S(1)}, u32[]{:S(2)}, u32[]{:S(2)}) %collective-permute-start.7) | collective-permute-done | bytes 3104 | tf_op jit(solution)/shard_map/ppermute | solution.py:460
  64.1 0.6 copy.14
  (4 shorter events, 0.0 us)
Async XLA Ops:
  1.5 13.3 %collective-permute-start.1 = (bf16[272,128]{1,0:T(8,128)(2,1)S(1)}, bf16[272,128]{1,0:T(8,128)(2,1)S(1)}, u32[]{:S(2)}, u32[]{:S(2)}) collective-permute-start(bf16[272,128]{1,0:T(8,128)(2,1)S(1)} %pack.1.own), channel_id=1, source_target_pairs={{0,720},{48,96},{96,48},{144,192},{192,144},{240,288},{288,240},{3... | collective-permute-start | bytes 208904 | tf_op jit(solution)/shard_map/ppermute | solution.py:375
  12.6 13.4 %collective-permute-start = (bf16[272,128]{1,0:T(8,128)(2,1)S(1)}, bf16[272,128]{1,0:T(8,128)(2,1)S(1)}, u32[]{:S(2)}, u32[]{:S(2)}) collective-permute-start(bf16[272,128]{1,0:T(8,128)(2,1)S(1)} %pack.1.own), channel_id=1, source_target_pairs={{0,48},{48,0},{96,144},{144,96},{192,240},{240,192},{288,336},{336... | collective-permute-start | bytes 208904 | tf_op jit(solution)/shard_map/ppermute | solution.py:376
  25.9 13.3 %collective-permute-start.3 = (bf16[816,128]{1,0:T(8,128)(2,1)S(1)}, bf16[816,128]{1,0:T(8,128)(2,1)S(1)}, u32[]{:S(2)}, u32[]{:S(2)}) collective-permute-start(bf16[816,128]{1,0:T(8,128)(2,1)S(1)} %assemble.1.slab), channel_id=1, source_target_pairs={{0,47},{1,2},{2,1},{3,4},{4,3},{5,6},{6,5},{7,8},{8,7},{9,10},{10,... | collective-permute-start | bytes 626696 | tf_op jit(solution)/shard_map/ppermute | solution.py:386
  27.9 11.3 %collective-permute-start.2 = (bf16[816,128]{1,0:T(8,128)(2,1)S(1)}, bf16[816,128]{1,0:T(8,128)(2,1)S(1)}, u32[]{:S(2)}, u32[]{:S(2)}) collective-permute-start(bf16[816,128]{1,0:T(8,128)(2,1)S(1)} %assemble.1.slab), channel_id=1, source_target_pairs={{0,1},{1,0},{2,3},{3,2},{4,5},{5,4},{6,7},{7,6},{8,9},{9,8},{10,11... | collective-permute-start | bytes 626696 | tf_op jit(solution)/shard_map/ppermute | solution.py:387
  41.7 11.0 %collective-permute-start.4 = (f32[3,768]{1,0:T(4,128)S(1)}, f32[3,768]{1,0:T(4,128)S(1)}, u32[]{:S(2)}, u32[]{:S(2)}) collective-permute-start(f32[3,768]{1,0:T(4,128)S(1)} %get-tuple-element.38), channel_id=1, source_target_pairs={{0,47},{1,2},{2,1},{3,4},{4,3},{5,6},{6,5},{7,8},{8,7},{9,10},{10,... | collective-permute-start | bytes 27656 | tf_op jit(solution)/shard_map/ppermute | solution.py:456
  46.2 6.5 %collective-permute-start.5 = (f32[3,768]{1,0:T(4,128)S(1)}, f32[3,768]{1,0:T(4,128)S(1)}, u32[]{:S(2)}, u32[]{:S(2)}) collective-permute-start(f32[3,768]{1,0:T(4,128)S(1)} %get-tuple-element.39), channel_id=1, source_target_pairs={{0,1},{1,0},{2,3},{3,2},{4,5},{5,4},{6,7},{7,6},{8,9},{9,8},{10,11... | collective-permute-start | bytes 27656 | tf_op jit(solution)/shard_map/ppermute | solution.py:457
  52.7 5.9 %collective-permute-start.6 = (f32[3,256]{1,0:T(4,128)S(1)}, f32[3,256]{1,0:T(4,128)S(1)}, u32[]{:S(2)}, u32[]{:S(2)}) collective-permute-start(f32[3,256]{1,0:T(4,128)S(1)} %get-tuple-element.42), channel_id=1, source_target_pairs={{0,48},{48,96},{96,144},{144,192},{192,240},{240,288},{288,336},{3... | collective-permute-start | bytes 9224 | tf_op jit(solution)/shard_map/ppermute | solution.py:459
  54.7 9.4 %collective-permute-start.7 = (f32[3,256]{1,0:T(4,128)S(1)}, f32[3,256]{1,0:T(4,128)S(1)}, u32[]{:S(2)}, u32[]{:S(2)}) collective-permute-start(f32[3,256]{1,0:T(4,128)S(1)} %get-tuple-element.43), channel_id=1, source_target_pairs={{0,720},{48,0},{96,48},{144,96},{192,144},{240,192},{288,240},{336... | collective-permute-start | bytes 9224 | tf_op jit(solution)/shard_map/ppermute | solution.py:460

commit v7 on v6

--- a/solution.py
+++ b/solution.py
@@ -198,7 +198,6 @@
     w_env,
     rows_own,
     pos_own,
-    energy,
     f_own,
     f_in,
     f_out,
@@ -280,15 +279,16 @@
     lines = jnp.concatenate([four_high, four_low, jnp.zeros((8, edges), f32)], axis=0).astype(bf16)
     to_c = mm(lines, hot_c[...])
     to_c = to_c[0:4] + to_c[4:8]
-    energy[0] = to_c[3:4]
+    f_own[3:4, 0:atoms] = to_c[3:4]
+    f_own[3:4, atoms:wide] = jnp.zeros((1, wide - atoms), f32)
     upper_in = lax.axis_index("gx") % 2 == 0
     for part, out in enumerate((f_own, f_in, f_out)):
         to_nb = mm(lines, hot_nb[:, part * wide : (part + 1) * wide])
         to_nb = -(to_nb[0:3] + to_nb[4:7])
         mine, inner, outer = (to_nb[:, k * atoms : (k + 1) * atoms] for k in range(3))
-        out[:, 0:atoms] = mine + to_c[0:3] if part == 0 else mine
-        out[:, atoms : 2 * atoms] = jnp.where(upper_in, inner, outer)
-        out[:, 2 * atoms : wide] = jnp.where(upper_in, outer, inner)
+        out[0:3, 0:atoms] = mine + to_c[0:3] if part == 0 else mine
+        out[0:3, atoms : 2 * atoms] = jnp.where(upper_in, inner, outer)
+        out[0:3, 2 * atoms : wide] = jnp.where(upper_in, outer, inner)
 
 
 def pack(feats, positions, packed, pos, sems):
@@ -307,7 +307,7 @@
     move_feats.wait()
 
 
-def assemble(own, x_in, x_out, slab):
+def assemble(own, x_out, x_in, slab):
     atoms = own.shape[0] - POS_ROWS
     for k, part in enumerate((own, x_in, x_out)):
         slab[k * atoms : (k + 1) * atoms] = part[0:atoms]
@@ -382,7 +382,7 @@
         out_specs=pl.BlockSpec(memory_space=pltpu.VMEM),
         name="assemble",
         compiler_params=grant(2),
-    )(own, x_in, x_out)
+    )(own, x_out, x_in)
     y_out = lax.ppermute(slab, "gy", pair_out("gy"))
     y_in = lax.ppermute(slab, "gy", pair_in("gy"))
 
@@ -444,18 +444,19 @@
         )
     )
 
-    energy, f_own, f_in, f_out = pl.pallas_call(
+    f_own, f_in, f_out = pl.pallas_call(
         layer,
-        out_shape=[shape((1, 1, edges), f32)] + [shape((3, 3 * atoms), f32)] * 3,
+        out_shape=[shape((4, 3 * atoms), f32)] + [shape((3, 3 * atoms), f32)] * 2,
         in_specs=vmem(17),
-        out_specs=vmem(4),
+        out_specs=vmem(3),
         name="layer",
         compiler_params=grant(8),
     )(y_in, y_out, *prepared, w2_copy, we_copy, rows_own, pos_own)
 
     r_out = lax.ppermute(f_out, "gy", pair_out("gy"))
     r_in = lax.ppermute(f_in, "gy", pair_in("gy"))
-    column = f_own + r_out + r_in
+    column = f_own[0:3] + r_out + r_in
+    energy = f_own[3:4, :atoms][None]
     s_up = lax.ppermute(column[:, atoms : 2 * atoms], "gx", step_by("gx", 1))
     s_down = lax.ppermute(column[:, 2 * atoms :], "gx", step_by("gx", -1))
     forces = column[:, :atoms] + s_up + s_down

time: 65.1 us -> 63 us (0.968)
  the two profiles are of different devices: /device:TPU:30 before, /device:TPU:1 now
where the time goes in v7:
time: 63 us; the launch traced here: 62.2 us
  starting transfers between devices  51.7 us (82%)
  Pallas kernels  4.89 us (8%)
  waiting for transfers between devices  3.67 us (6%)
  local copies, waits for them, and re-layouts  1.15 us (2%)
  between operations  0.75 us (1%)
    ppermute x1, starting transfers between devices, body(): y_in = lax.ppermute(slab, 'gy', pair_in('gy'))  12.4 us
    ppermute x1, starting transfers between devices, body(): r_in = lax.ppermute(f_in, 'gy', pair_in('gy'))  9.35 us
    ppermute x1, starting transfers between devices, body(): y_out = lax.ppermute(slab, 'gy', pair_out('gy'))  8.57 us
    ppermute x1, starting transfers between devices, body(): s_down = lax.ppermute(column[:, 2 * atoms:], 'gx', step_by('gx', -1))  7.27 us
    ppermute x1, starting transfers between devices, body(): x_out = lax.ppermute(own, 'gx', pair_out('gx'))  6.3 us
    ppermute x1, starting transfers between devices, body(): x_in = lax.ppermute(own, 'gx', pair_in('gx'))  4.03 us
    ppermute x1, waiting for transfers between devices, body(): x_out = lax.ppermute(own, 'gx', pair_out('gx'))  2.69 us
    pallas_call x1, Pallas kernels, body(): pl.pallas_call(layer, out_shape=[shape((4, 3 * atoms), f32)] + [shape((3,...  2.08 us
  transfers between devices with their start and end apart: 8, of which 3 were waited for; matrix products, arithmetic and copies ran while one was open for 1% of the time, Pallas kernels for 3%

profile of v7, /device:TPU:1, one launch (start us, length us, event | category | flops | bytes accessed | tf_op | source)
XLA Modules:
  0.0 62.2 jit_solution(15016930366560578157)
XLA Ops:
  0.6 0.9 %pack.1.own = bf16[272,128]{1,0:T(8,128)(2,1)S(1)} custom-call(bf16[1,1,256,128]{3,2,1,0:T(8,128)(2,1)} %feats_hbm.1, bf16[1,1,3,256]{3,2,1,0:T(4,128)(2,1)} %positions_hbm.1), custom_call_target="tpu_custom_call" | custom-call | tf_op jit(solution)/shard_map/pack/pallas_call | solution.py:366
  1.5 4.0 %collective-permute-start.1 = (bf16[272,128]{1,0:T(8,128)(2,1)S(1)}, bf16[272,128]{1,0:T(8,128)(2,1)S(1)}, u32[]{:S(2)}, u32[]{:S(2)}) collective-permute-start(bf16[272,128]{1,0:T(8,128)(2,1)S(1)} %pack.1.own), channel_id=1, source_target_pairs={{0,48},{48,0},{96,144},{144,96},{192,240},{240,192},{288,336},{336... | collective-permute-start | bytes 208904 | tf_op jit(solution)/shard_map/ppermute | solution.py:376
  5.6 6.3 %collective-permute-start = (bf16[272,128]{1,0:T(8,128)(2,1)S(1)}, bf16[272,128]{1,0:T(8,128)(2,1)S(1)}, u32[]{:S(2)}, u32[]{:S(2)}) collective-permute-start(bf16[272,128]{1,0:T(8,128)(2,1)S(1)} %pack.1.own), channel_id=1, source_target_pairs={{0,720},{48,96},{96,48},{144,192},{192,144},{240,288},{288,240},{3... | collective-permute-start | bytes 208904 | tf_op jit(solution)/shard_map/ppermute | solution.py:375
  11.9 0.0 collective-permute-done.1.x_in
  11.9 2.7 %collective-permute-done.x_out = bf16[272,128]{1,0:T(8,128)(2,1)S(1)} collective-permute-done((bf16[272,128]{1,0:T(8,128)(2,1)S(1)}, bf16[272,128]{1,0:T(8,128)(2,1)S(1)}, u32[]{:S(2)}, u32[]{:S(2)}) %collective-permute-start) | collective-permute-done | bytes 69664 | tf_op jit(solution)/shard_map/ppermute | solution.py:375
  14.6 8.6 %collective-permute-start.3 = (bf16[816,128]{1,0:T(8,128)(2,1)S(1)}, bf16[816,128]{1,0:T(8,128)(2,1)S(1)}, u32[]{:S(2)}, u32[]{:S(2)}) collective-permute-start(bf16[816,128]{1,0:T(8,128)(2,1)S(1)} %assemble.1.slab), channel_id=1, source_target_pairs={{0,47},{1,2},{2,1},{3,4},{4,3},{5,6},{6,5},{7,8},{8,7},{9,10},{10,... | collective-permute-start | bytes 626696 | tf_op jit(solution)/shard_map/ppermute | solution.py:386
  23.2 12.4 %collective-permute-start.2 = (bf16[816,128]{1,0:T(8,128)(2,1)S(1)}, bf16[816,128]{1,0:T(8,128)(2,1)S(1)}, u32[]{:S(2)}, u32[]{:S(2)}) collective-permute-start(bf16[816,128]{1,0:T(8,128)(2,1)S(1)} %assemble.1.slab), channel_id=1, source_target_pairs={{0,1},{1,0},{2,3},{3,2},{4,5},{5,4},{6,7},{7,6},{8,9},{9,8},{10,11... | collective-permute-start | bytes 626696 | tf_op jit(solution)/shard_map/ppermute | solution.py:387
  35.5 1.9 %prepare.1 = (bf16[256,2304]{1,0:T(8,128)(2,1)S(1)}, bf16[256,256]{1,0:T(8,128)(2,1)S(1)}, bf16[256,256]{1,0:T(8,128)(2,1)S(1)}, f32[128,256]{1,0:T(8,128)S(1)},...) custom-call(bf16[816,128]{1,0:T(8,128)(2,1)S(1)} %assemble.1.slab, ...), custom_call_target="tpu_custom_call" | custom-call | flops 100000000 | bytes 3000000 | tf_op jit(solution)/shard_map/prepare/pallas_call | solution.py:389
  37.5 0.0 collective-permute-done.3.slab_out
  37.5 0.0 collective-permute-done.2.slab_in
  37.5 2.1 %layer.1 = (f32[4,768]{1,0:T(4,128)S(1)}, f32[3,768]{1,0:T(4,128)S(1)}, f32[3,768]{1,0:T(4,128)S(1)}) custom-call(bf16[816,128]{1,0:T(8,128)(2,1)S(1)} %collective-permute-done.2.slab_in, bf16[816,128]{1,0:T(8,128)(2,1)S(1)} %collective-permute-done.3.slab_out, bf16[256,2304]{1,0:T(8,128)(2,1)S(1)} %get-tuple-element.20.hot_nb, ...), custom_call_target="tpu_custom_call" | custom-call | tf_op jit(solution)/shard_map/layer/pallas_call | solution.py:447
  39.6 1.9 %collective-permute-start.4 = (f32[3,768]{1,0:T(4,128)S(1)}, f32[3,768]{1,0:T(4,128)S(1)}, u32[]{:S(2)}, u32[]{:S(2)}) collective-permute-start(f32[3,768]{1,0:T(4,128)S(1)} %get-tuple-element.36), channel_id=1, source_target_pairs={{0,47},{1,2},{2,1},{3,4},{4,3},{5,6},{6,5},{7,8},{8,7},{9,10},{10,... | collective-permute-start | bytes 27656 | tf_op jit(solution)/shard_map/ppermute | solution.py:456
  41.5 9.4 %collective-permute-start.5 = (f32[3,768]{1,0:T(4,128)S(1)}, f32[3,768]{1,0:T(4,128)S(1)}, u32[]{:S(2)}, u32[]{:S(2)}) collective-permute-start(f32[3,768]{1,0:T(4,128)S(1)} %get-tuple-element.37), channel_id=1, source_target_pairs={{0,1},{1,0},{2,3},{3,2},{4,5},{5,4},{6,7},{7,6},{8,9},{9,8},{10,11... | collective-permute-start | bytes 27656 | tf_op jit(solution)/shard_map/ppermute | solution.py:457
  50.9 0.0 collective-permute-done.4
  50.9 0.8 %collective-permute-done.5 = f32[3,768]{1,0:T(4,128)S(1)} collective-permute-done((f32[3,768]{1,0:T(4,128)S(1)}, f32[3,768]{1,0:T(4,128)S(1)}, u32[]{:S(2)}, u32[]{:S(2)}) %collective-permute-start.5) | collective-permute-done | bytes 9248 | tf_op jit(solution)/shard_map/ppermute | solution.py:457
  51.7 1.9 %collective-permute-start.6 = (f32[3,256]{1,0:T(4,128)S(1)}, f32[3,256]{1,0:T(4,128)S(1)}, u32[]{:S(2)}, u32[]{:S(2)}) collective-permute-start(f32[3,256]{1,0:T(4,128)S(1)} %get-tuple-element.40), channel_id=1, source_target_pairs={{0,48},{48,96},{96,144},{144,192},{192,240},{240,288},{288,336},{3... | collective-permute-start | bytes 9224 | tf_op jit(solution)/shard_map/ppermute | solution.py:460
  53.6 7.3 %collective-permute-start.7 = (f32[3,256]{1,0:T(4,128)S(1)}, f32[3,256]{1,0:T(4,128)S(1)}, u32[]{:S(2)}, u32[]{:S(2)}) collective-permute-start(f32[3,256]{1,0:T(4,128)S(1)} %get-tuple-element.41), channel_id=1, source_target_pairs={{0,720},{48,0},{96,48},{144,96},{192,144},{240,192},{288,240},{336... | collective-permute-start | bytes 9224 | tf_op jit(solution)/shard_map/ppermute | solution.py:461
  60.9 0.6 slice_bitcast_fusion
  61.5 0.0 collective-permute-done.6
  61.5 0.2 collective-permute-done.7
  61.6 0.6 copy.14
  (4 shorter events, 0.0 us)
Async XLA Ops:
  1.5 10.4 %collective-permute-start.1 = (bf16[272,128]{1,0:T(8,128)(2,1)S(1)}, bf16[272,128]{1,0:T(8,128)(2,1)S(1)}, u32[]{:S(2)}, u32[]{:S(2)}) collective-permute-start(bf16[272,128]{1,0:T(8,128)(2,1)S(1)} %pack.1.own), channel_id=1, source_target_pairs={{0,48},{48,0},{96,144},{144,96},{192,240},{240,192},{288,336},{336... | collective-permute-start | bytes 208904 | tf_op jit(solution)/shard_map/ppermute | solution.py:376
  5.6 9.0 %collective-permute-start = (bf16[272,128]{1,0:T(8,128)(2,1)S(1)}, bf16[272,128]{1,0:T(8,128)(2,1)S(1)}, u32[]{:S(2)}, u32[]{:S(2)}) collective-permute-start(bf16[272,128]{1,0:T(8,128)(2,1)S(1)} %pack.1.own), channel_id=1, source_target_pairs={{0,720},{48,96},{96,48},{144,192},{192,144},{240,288},{288,240},{3... | collective-permute-start | bytes 208904 | tf_op jit(solution)/shard_map/ppermute | solution.py:375
  14.6 22.9 %collective-permute-start.3 = (bf16[816,128]{1,0:T(8,128)(2,1)S(1)}, bf16[816,128]{1,0:T(8,128)(2,1)S(1)}, u32[]{:S(2)}, u32[]{:S(2)}) collective-permute-start(bf16[816,128]{1,0:T(8,128)(2,1)S(1)} %assemble.1.slab), channel_id=1, source_target_pairs={{0,47},{1,2},{2,1},{3,4},{4,3},{5,6},{6,5},{7,8},{8,7},{9,10},{10,... | collective-permute-start | bytes 626696 | tf_op jit(solution)/shard_map/ppermute | solution.py:386
  23.2 14.3 %collective-permute-start.2 = (bf16[816,128]{1,0:T(8,128)(2,1)S(1)}, bf16[816,128]{1,0:T(8,128)(2,1)S(1)}, u32[]{:S(2)}, u32[]{:S(2)}) collective-permute-start(bf16[816,128]{1,0:T(8,128)(2,1)S(1)} %assemble.1.slab), channel_id=1, source_target_pairs={{0,1},{1,0},{2,3},{3,2},{4,5},{5,4},{6,7},{7,6},{8,9},{9,8},{10,11... | collective-permute-start | bytes 626696 | tf_op jit(solution)/shard_map/ppermute | solution.py:387
  39.6 11.3 %collective-permute-start.4 = (f32[3,768]{1,0:T(4,128)S(1)}, f32[3,768]{1,0:T(4,128)S(1)}, u32[]{:S(2)}, u32[]{:S(2)}) collective-permute-start(f32[3,768]{1,0:T(4,128)S(1)} %get-tuple-element.36), channel_id=1, source_target_pairs={{0,47},{1,2},{2,1},{3,4},{4,3},{5,6},{6,5},{7,8},{8,7},{9,10},{10,... | collective-permute-start | bytes 27656 | tf_op jit(solution)/shard_map/ppermute | solution.py:456
  41.5 10.2 %collective-permute-start.5 = (f32[3,768]{1,0:T(4,128)S(1)}, f32[3,768]{1,0:T(4,128)S(1)}, u32[]{:S(2)}, u32[]{:S(2)}) collective-permute-start(f32[3,768]{1,0:T(4,128)S(1)} %get-tuple-element.37), channel_id=1, source_target_pairs={{0,1},{1,0},{2,3},{3,2},{4,5},{5,4},{6,7},{7,6},{8,9},{9,8},{10,11... | collective-permute-start | bytes 27656 | tf_op jit(solution)/shard_map/ppermute | solution.py:457
  51.7 9.8 %collective-permute-start.6 = (f32[3,256]{1,0:T(4,128)S(1)}, f32[3,256]{1,0:T(4,128)S(1)}, u32[]{:S(2)}, u32[]{:S(2)}) collective-permute-start(f32[3,256]{1,0:T(4,128)S(1)} %get-tuple-element.40), channel_id=1, source_target_pairs={{0,48},{48,96},{96,144},{144,192},{192,240},{240,288},{288,336},{3... | collective-permute-start | bytes 9224 | tf_op jit(solution)/shard_map/ppermute | solution.py:460
  53.6 8.0 %collective-permute-start.7 = (f32[3,256]{1,0:T(4,128)S(1)}, f32[3,256]{1,0:T(4,128)S(1)}, u32[]{:S(2)}, u32[]{:S(2)}) collective-permute-start(f32[3,256]{1,0:T(4,128)S(1)} %get-tuple-element.41), channel_id=1, source_target_pairs={{0,720},{48,0},{96,48},{144,96},{192,144},{240,192},{288,240},{336... | collective-permute-start | bytes 9224 | tf_op jit(solution)/shard_map/ppermute | solution.py:461

commit v8 on v7

--- a/solution.py
+++ b/solution.py
@@ -281,14 +281,13 @@
     to_c = to_c[0:4] + to_c[4:8]
     f_own[3:4, 0:atoms] = to_c[3:4]
     f_own[3:4, atoms:wide] = jnp.zeros((1, wide - atoms), f32)
-    upper_in = lax.axis_index("gx") % 2 == 0
     for part, out in enumerate((f_own, f_in, f_out)):
         to_nb = mm(lines, hot_nb[:, part * wide : (part + 1) * wide])
         to_nb = -(to_nb[0:3] + to_nb[4:7])
         mine, inner, outer = (to_nb[:, k * atoms : (k + 1) * atoms] for k in range(3))
         out[0:3, 0:atoms] = mine + to_c[0:3] if part == 0 else mine
-        out[0:3, atoms : 2 * atoms] = jnp.where(upper_in, inner, outer)
-        out[0:3, 2 * atoms : wide] = jnp.where(upper_in, outer, inner)
+        out[0:3, atoms : 2 * atoms] = inner
+        out[0:3, 2 * atoms : wide] = outer
 
 
 def pack(feats, positions, packed, pos, sems):
@@ -338,11 +337,6 @@
 def pair_out(axis):
     count = lax.axis_size(axis)
     return [(i, (i + 1) % count if i % 2 else (i - 1) % count) for i in range(count)]
-
-
-def step_by(axis, distance):
-    count = lax.axis_size(axis)
-    return [(i, (i + distance) % count) for i in range(count)]
 
 
 def body(
@@ -457,9 +451,9 @@
     r_in = lax.ppermute(f_in, "gy", pair_in("gy"))
     column = f_own[0:3] + r_out + r_in
     energy = f_own[3:4, :atoms][None]
-    s_up = lax.ppermute(column[:, atoms : 2 * atoms], "gx", step_by("gx", 1))
-    s_down = lax.ppermute(column[:, 2 * atoms :], "gx", step_by("gx", -1))
-    forces = column[:, :atoms] + s_up + s_down
+    s_in = lax.ppermute(column[:, atoms : 2 * atoms], "gx", pair_in("gx"))
+    s_out = lax.ppermute(column[:, 2 * atoms :], "gx", pair_out("gx"))
+    forces = column[:, :atoms] + s_out + s_in
     return (energy, forces[None, None])
 
 

time: 63 us -> 63.1 us (level)
  waiting for transfers between devices: 3.67 us -> 5.36 us
  starting transfers between devices: 51.7 us -> 50.6 us
    ppermute x2, waiting for transfers between devices: 0.17 us -> 1.86 us  [the longest x1 1.85 us: body(): s_in = lax.ppermute(column[:, atoms:2 * atoms], 'gx', pair_in('gx'))]
    ppermute x2, starting transfers between devices: 9.19 us -> 8 us  [the longest x1 6.08 us: body(): s_out = lax.ppermute(column[:, 2 * atoms:], 'gx', pair_out('gx'))]
where the time goes in v8:
time: 63.1 us; the launch traced here: 62.7 us
  starting transfers between devices  50.6 us (80%)
  waiting for transfers between devices  5.36 us (8%)
  Pallas kernels  4.89 us (8%)
  local copies, waits for them, and re-layouts  1.16 us (2%)
  between operations  0.75 us (1%)
    ppermute x1, starting transfers between devices, body(): y_in = lax.ppermute(slab, 'gy', pair_in('gy'))  12.4 us
    ppermute x1, starting transfers between devices, body(): r_in = lax.ppermute(f_in, 'gy', pair_in('gy'))  9.35 us
    ppermute x1, starting transfers between devices, body(): y_out = lax.ppermute(slab, 'gy', pair_out('gy'))  8.57 us
    ppermute x1, starting transfers between devices, body(): x_out = lax.ppermute(own, 'gx', pair_out('gx'))  6.3 us
    ppermute x1, starting transfers between devices, body(): s_out = lax.ppermute(column[:, 2 * atoms:], 'gx', pair_out('gx'))  6.08 us
    ppermute x1, starting transfers between devices, body(): x_in = lax.ppermute(own, 'gx', pair_in('gx'))  4.03 us
    ppermute x1, waiting for transfers between devices, body(): x_out = lax.ppermute(own, 'gx', pair_out('gx'))  2.69 us
    pallas_call x1, Pallas kernels, body(): pl.pallas_call(layer, out_shape=[shape((4, 3 * atoms), f32)] + [shape((3,...  2.08 us
  transfers between devices with their start and end apart: 8, of which 3 were waited for; matrix products, arithmetic and copies ran while one was open for 1% of the time, Pallas kernels for 3%

profile of v8, /device:TPU:1, one launch (start us, length us, event | category | flops | bytes accessed | tf_op | source)
XLA Modules:
  0.0 62.7 jit_solution(607176497418931202)
XLA Ops:
  0.6 0.9 %pack.1.own = bf16[272,128]{1,0:T(8,128)(2,1)S(1)} custom-call(bf16[1,1,256,128]{3,2,1,0:T(8,128)(2,1)} %feats_hbm.1, bf16[1,1,3,256]{3,2,1,0:T(4,128)(2,1)} %positions_hbm.1), custom_call_target="tpu_custom_call" | custom-call | tf_op jit(solution)/shard_map/pack/pallas_call | solution.py:360
  1.5 4.0 %collective-permute-start.1 = (bf16[272,128]{1,0:T(8,128)(2,1)S(1)}, bf16[272,128]{1,0:T(8,128)(2,1)S(1)}, u32[]{:S(2)}, u32[]{:S(2)}) collective-permute-start(bf16[272,128]{1,0:T(8,128)(2,1)S(1)} %pack.1.own), channel_id=1, source_target_pairs={{0,48},{48,0},{96,144},{144,96},{192,240},{240,192},{288,336},{336... | collective-permute-start | bytes 208904 | tf_op jit(solution)/shard_map/ppermute | solution.py:370
  5.6 6.3 %collective-permute-start = (bf16[272,128]{1,0:T(8,128)(2,1)S(1)}, bf16[272,128]{1,0:T(8,128)(2,1)S(1)}, u32[]{:S(2)}, u32[]{:S(2)}) collective-permute-start(bf16[272,128]{1,0:T(8,128)(2,1)S(1)} %pack.1.own), channel_id=1, source_target_pairs={{0,720},{48,96},{96,48},{144,192},{192,144},{240,288},{288,240},{3... | collective-permute-start | bytes 208904 | tf_op jit(solution)/shard_map/ppermute | solution.py:369
  11.9 0.0 collective-permute-done.1.x_in
  11.9 2.7 %collective-permute-done.x_out = bf16[272,128]{1,0:T(8,128)(2,1)S(1)} collective-permute-done((bf16[272,128]{1,0:T(8,128)(2,1)S(1)}, bf16[272,128]{1,0:T(8,128)(2,1)S(1)}, u32[]{:S(2)}, u32[]{:S(2)}) %collective-permute-start) | collective-permute-done | bytes 69664 | tf_op jit(solution)/shard_map/ppermute | solution.py:369
  14.6 8.6 %collective-permute-start.3 = (bf16[816,128]{1,0:T(8,128)(2,1)S(1)}, bf16[816,128]{1,0:T(8,128)(2,1)S(1)}, u32[]{:S(2)}, u32[]{:S(2)}) collective-permute-start(bf16[816,128]{1,0:T(8,128)(2,1)S(1)} %assemble.1.slab), channel_id=1, source_target_pairs={{0,47},{1,2},{2,1},{3,4},{4,3},{5,6},{6,5},{7,8},{8,7},{9,10},{10,... | collective-permute-start | bytes 626696 | tf_op jit(solution)/shard_map/ppermute | solution.py:380
  23.2 12.4 %collective-permute-start.2 = (bf16[816,128]{1,0:T(8,128)(2,1)S(1)}, bf16[816,128]{1,0:T(8,128)(2,1)S(1)}, u32[]{:S(2)}, u32[]{:S(2)}) collective-permute-start(bf16[816,128]{1,0:T(8,128)(2,1)S(1)} %assemble.1.slab), channel_id=1, source_target_pairs={{0,1},{1,0},{2,3},{3,2},{4,5},{5,4},{6,7},{7,6},{8,9},{9,8},{10,11... | collective-permute-start | bytes 626696 | tf_op jit(solution)/shard_map/ppermute | solution.py:381
  35.5 1.9 %prepare.1 = (bf16[256,2304]{1,0:T(8,128)(2,1)S(1)}, bf16[256,256]{1,0:T(8,128)(2,1)S(1)}, bf16[256,256]{1,0:T(8,128)(2,1)S(1)}, f32[128,256]{1,0:T(8,128)S(1)},...) custom-call(bf16[816,128]{1,0:T(8,128)(2,1)S(1)} %assemble.1.slab, ...), custom_call_target="tpu_custom_call" | custom-call | flops 100000000 | bytes 3000000 | tf_op jit(solution)/shard_map/prepare/pallas_call | solution.py:383
  37.5 0.0 collective-permute-done.3.slab_out
  37.5 0.0 collective-permute-done.2.slab_in
  37.5 2.1 %layer.1 = (f32[4,768]{1,0:T(4,128)S(1)}, f32[3,768]{1,0:T(4,128)S(1)}, f32[3,768]{1,0:T(4,128)S(1)}) custom-call(bf16[816,128]{1,0:T(8,128)(2,1)S(1)} %collective-permute-done.2.slab_in, bf16[816,128]{1,0:T(8,128)(2,1)S(1)} %collective-permute-done.3.slab_out, bf16[256,2304]{1,0:T(8,128)(2,1)S(1)} %get-tuple-element.20.hot_nb, ...), custom_call_target="tpu_custom_call" | custom-call | tf_op jit(solution)/shard_map/layer/pallas_call | solution.py:441
  39.6 1.9 %collective-permute-start.4 = (f32[3,768]{1,0:T(4,128)S(1)}, f32[3,768]{1,0:T(4,128)S(1)}, u32[]{:S(2)}, u32[]{:S(2)}) collective-permute-start(f32[3,768]{1,0:T(4,128)S(1)} %get-tuple-element.36), channel_id=1, source_target_pairs={{0,47},{1,2},{2,1},{3,4},{4,3},{5,6},{6,5},{7,8},{8,7},{9,10},{10,... | collective-permute-start | bytes 27656 | tf_op jit(solution)/shard_map/ppermute | solution.py:450
  41.5 9.4 %collective-permute-start.5 = (f32[3,768]{1,0:T(4,128)S(1)}, f32[3,768]{1,0:T(4,128)S(1)}, u32[]{:S(2)}, u32[]{:S(2)}) collective-permute-start(f32[3,768]{1,0:T(4,128)S(1)} %get-tuple-element.37), channel_id=1, source_target_pairs={{0,1},{1,0},{2,3},{3,2},{4,5},{5,4},{6,7},{7,6},{8,9},{9,8},{10,11... | collective-permute-start | bytes 27656 | tf_op jit(solution)/shard_map/ppermute | solution.py:451
  50.9 0.0 collective-permute-done.4
  50.9 0.8 %collective-permute-done.5 = f32[3,768]{1,0:T(4,128)S(1)} collective-permute-done((f32[3,768]{1,0:T(4,128)S(1)}, f32[3,768]{1,0:T(4,128)S(1)}, u32[]{:S(2)}, u32[]{:S(2)}) %collective-permute-start.5) | collective-permute-done | bytes 9248 | tf_op jit(solution)/shard_map/ppermute | solution.py:451
  51.7 6.1 %collective-permute-start.6 = (f32[3,256]{1,0:T(4,128)S(1)}, f32[3,256]{1,0:T(4,128)S(1)}, u32[]{:S(2)}, u32[]{:S(2)}) collective-permute-start(f32[3,256]{1,0:T(4,128)S(1)} %get-tuple-element.40), channel_id=1, source_target_pairs={{0,720},{48,96},{96,48},{144,192},{192,144},{240,288},{288,240},{3... | collective-permute-start | bytes 9224 | tf_op jit(solution)/shard_map/ppermute | solution.py:455
  57.8 1.9 %collective-permute-start.7 = (f32[3,256]{1,0:T(4,128)S(1)}, f32[3,256]{1,0:T(4,128)S(1)}, u32[]{:S(2)}, u32[]{:S(2)}) collective-permute-start(f32[3,256]{1,0:T(4,128)S(1)} %get-tuple-element.41), channel_id=1, source_target_pairs={{0,48},{48,0},{96,144},{144,96},{192,240},{240,192},{288,336},{336... | collective-permute-start | bytes 9224 | tf_op jit(solution)/shard_map/ppermute | solution.py:454
  59.7 0.6 slice_bitcast_fusion
  60.3 0.0 collective-permute-done.6
  60.3 1.9 %collective-permute-done.7 = f32[3,256]{1,0:T(4,128)S(1)} collective-permute-done((f32[3,256]{1,0:T(4,128)S(1)}, f32[3,256]{1,0:T(4,128)S(1)}, u32[]{:S(2)}, u32[]{:S(2)}) %collective-permute-start.7) | collective-permute-done | bytes 3104 | tf_op jit(solution)/shard_map/ppermute | solution.py:454
  62.1 0.6 copy.14
  (4 shorter events, 0.0 us)
Async XLA Ops:
  1.5 10.4 %collective-permute-start.1 = (bf16[272,128]{1,0:T(8,128)(2,1)S(1)}, bf16[272,128]{1,0:T(8,128)(2,1)S(1)}, u32[]{:S(2)}, u32[]{:S(2)}) collective-permute-start(bf16[272,128]{1,0:T(8,128)(2,1)S(1)} %pack.1.own), channel_id=1, source_target_pairs={{0,48},{48,0},{96,144},{144,96},{192,240},{240,192},{288,336},{336... | collective-permute-start | bytes 208904 | tf_op jit(solution)/shard_map/ppermute | solution.py:370
  5.6 9.0 %collective-permute-start = (bf16[272,128]{1,0:T(8,128)(2,1)S(1)}, bf16[272,128]{1,0:T(8,128)(2,1)S(1)}, u32[]{:S(2)}, u32[]{:S(2)}) collective-permute-start(bf16[272,128]{1,0:T(8,128)(2,1)S(1)} %pack.1.own), channel_id=1, source_target_pairs={{0,720},{48,96},{96,48},{144,192},{192,144},{240,288},{288,240},{3... | collective-permute-start | bytes 208904 | tf_op jit(solution)/shard_map/ppermute | solution.py:369
  14.6 22.9 %collective-permute-start.3 = (bf16[816,128]{1,0:T(8,128)(2,1)S(1)}, bf16[816,128]{1,0:T(8,128)(2,1)S(1)}, u32[]{:S(2)}, u32[]{:S(2)}) collective-permute-start(bf16[816,128]{1,0:T(8,128)(2,1)S(1)} %assemble.1.slab), channel_id=1, source_target_pairs={{0,47},{1,2},{2,1},{3,4},{4,3},{5,6},{6,5},{7,8},{8,7},{9,10},{10,... | collective-permute-start | bytes 626696 | tf_op jit(solution)/shard_map/ppermute | solution.py:380
  23.2 14.3 %collective-permute-start.2 = (bf16[816,128]{1,0:T(8,128)(2,1)S(1)}, bf16[816,128]{1,0:T(8,128)(2,1)S(1)}, u32[]{:S(2)}, u32[]{:S(2)}) collective-permute-start(bf16[816,128]{1,0:T(8,128)(2,1)S(1)} %assemble.1.slab), channel_id=1, source_target_pairs={{0,1},{1,0},{2,3},{3,2},{4,5},{5,4},{6,7},{7,6},{8,9},{9,8},{10,11... | collective-permute-start | bytes 626696 | tf_op jit(solution)/shard_map/ppermute | solution.py:381
  39.6 11.3 %collective-permute-start.4 = (f32[3,768]{1,0:T(4,128)S(1)}, f32[3,768]{1,0:T(4,128)S(1)}, u32[]{:S(2)}, u32[]{:S(2)}) collective-permute-start(f32[3,768]{1,0:T(4,128)S(1)} %get-tuple-element.36), channel_id=1, source_target_pairs={{0,47},{1,2},{2,1},{3,4},{4,3},{5,6},{6,5},{7,8},{8,7},{9,10},{10,... | collective-permute-start | bytes 27656 | tf_op jit(solution)/shard_map/ppermute | solution.py:450
  41.5 10.2 %collective-permute-start.5 = (f32[3,768]{1,0:T(4,128)S(1)}, f32[3,768]{1,0:T(4,128)S(1)}, u32[]{:S(2)}, u32[]{:S(2)}) collective-permute-start(f32[3,768]{1,0:T(4,128)S(1)} %get-tuple-element.37), channel_id=1, source_target_pairs={{0,1},{1,0},{2,3},{3,2},{4,5},{5,4},{6,7},{7,6},{8,9},{9,8},{10,11... | collective-permute-start | bytes 27656 | tf_op jit(solution)/shard_map/ppermute | solution.py:451
  51.7 8.6 %collective-permute-start.6 = (f32[3,256]{1,0:T(4,128)S(1)}, f32[3,256]{1,0:T(4,128)S(1)}, u32[]{:S(2)}, u32[]{:S(2)}) collective-permute-start(f32[3,256]{1,0:T(4,128)S(1)} %get-tuple-element.40), channel_id=1, source_target_pairs={{0,720},{48,96},{96,48},{144,192},{192,144},{240,288},{288,240},{3... | collective-permute-start | bytes 9224 | tf_op jit(solution)/shard_map/ppermute | solution.py:455
  57.8 4.4 %collective-permute-start.7 = (f32[3,256]{1,0:T(4,128)S(1)}, f32[3,256]{1,0:T(4,128)S(1)}, u32[]{:S(2)}, u32[]{:S(2)}) collective-permute-start(f32[3,256]{1,0:T(4,128)S(1)} %get-tuple-element.41), channel_id=1, source_target_pairs={{0,48},{48,0},{96,144},{144,96},{192,240},{240,192},{288,336},{336... | collective-permute-start | bytes 9224 | tf_op jit(solution)/shard_map/ppermute | solution.py:454
